TPU v7x, 32 devices: a whole 2x2x4 slice. The times are simulated.
32 devices in a mesh: groups: 1, seq: 8 (over y, x, core), expert: 4 (over z).
Axes of the slice: x: 2, y: 2, z: 4, core: 2. Of those that a mesh axis runs over, the one named last changes fastest.
Arguments:
- queries: bfloat16 [4, 1024, 2048], P(('groups', 'expert'), 'seq'), may hold values from -6 to 6
- keys: bfloat16 [4, 1024, 256], P(('groups', 'expert'), 'seq'), may hold values from -6 to 6
- values: bfloat16 [4, 1024, 256], P(('groups', 'expert'), 'seq'), may hold values from -8 to 8
- document_index: int32 [4, 1024], P(('groups', 'expert')), may hold values from 0 to 3, never falling along the last dimension, each value on 1 to 512 neighbouring positions
- residual: bfloat16 [4, 1024, 2048], P(('groups', 'expert'), 'seq'), may hold values from -4 to 4
- output_projection: bfloat16 [2048, 2048], P(None, 'expert'), may hold values from -0.125 to 0.125
- norm_gain_weight: float32 [2048], replicated, may hold values from 0.5 to 1.5
- routed_experts: int32 [4, 1024, 8], P(('groups', 'expert'), 'seq'), may hold values from 0 to 31, all different within a row; in each aligned block of 128 rows (0 to 127, 128 to 255, ..., all dimensions but the last counted through in order) at most 36 rows name the same one
- router_logits: float32 [4, 1024, 8], P(('groups', 'expert'), 'seq'), may hold values from -12 to 320
- gate_weight: bfloat16 [32, 2048, 768], P(('seq', 'expert')), may hold values from -0.125 to 0.125
- up_weight: bfloat16 [32, 2048, 768], P(('seq', 'expert')), may hold values from -0.125 to 0.125
- down_weight: bfloat16 [32, 768, 2048], P(('seq', 'expert')), may hold values from -0.21875 to 0.21875
- adapter_down: bfloat16 [32, 768, 32], P(('seq', 'expert')), may hold values from -0.21875 to 0.21875
- adapter_up: bfloat16 [32, 32, 2048], P(('seq', 'expert')), may hold values from -1 to 1
- cotangent: bfloat16 [4, 1024, 2048], P(('groups', 'expert'), 'seq'), may hold values from -0.3984375 to 0.3984375
Outputs:
- expert_mixture_output: bfloat16 [4, 1024, 2048], P(('groups', 'expert'), 'seq')
- adapter_down_gradient: float32 [32, 768, 32], P(('groups', 'seq', 'expert'))
- adapter_up_gradient: float32 [32, 32, 2048], P(('groups', 'seq', 'expert'))
- router_logit_gradient: float32 [4, 1024, 8], P(('groups', 'expert'), 'seq')
Inputs may be any that keep to these rules, and one draw needn't show every extreme that they name: `routed_experts`: each row names 8 different experts; among the 128 rows of one device (aligned blocks of positions) no expert is named more than 36 times, a bound that some block reaches. `document_index`: never falls along a sequence; at most 4 documents in a sequence.
All inputs are finite; a program needn't handle non-finite values.
Results may differ from a plain program's by a relative error of at most 0.0085.
Values may be sent and summed in bfloat16 or wider, within the bound.
No kernel may reach another device: no remote copies, remote signals or barrier semaphores. Data moves between devices by JAX's collectives and lax.ppermute only.
A program may use at most 128 MiB of HBM per device.

v0:
```python
import math

import jax
import jax.numpy as jnp
from jax import lax
from jax.sharding import PartitionSpec as P

QUERY_HEADS = 16
KEY_VALUE_HEADS = 2
HEAD_SIZE = 128
PICKS_PER_TOKEN = 8


adapter_scale = 2.0
norm_eps = 1e-06


def attend_heads(query_heads, key_rows, value_rows, documents):
    length = key_rows.shape[0]
    heads_here = query_heads.shape[1] // HEAD_SIZE
    query_grid = query_heads.reshape(length, heads_here, HEAD_SIZE)
    block_count = max(1, min(8, length // 512))
    block_rows = length // block_count
    positions = jnp.arange(length)
    results = []
    for number in range(block_count):
        row_start = number * block_rows
        row_end = row_start + block_rows
        scores = jnp.einsum(
            "qhd,kd->hqk",
            query_grid[row_start:row_end],
            key_rows[:row_end],
            preferred_element_type=jnp.float32,
        ) * (1.0 / math.sqrt(HEAD_SIZE))
        allowed = (positions[None, :row_end] <= positions[row_start:row_end, None]) & (
            documents[None, :row_end] == documents[row_start:row_end, None]
        )
        scores = jnp.where(allowed[None], scores, -jnp.inf)
        highest = jnp.max(scores, axis=-1, keepdims=True)
        raised = jnp.exp(scores - highest)
        weights = (raised / jnp.sum(raised, axis=-1, keepdims=True)).astype(jnp.bfloat16)
        mixture = jnp.einsum(
            "hqk,kd->qhd", weights, value_rows[:row_end], preferred_element_type=jnp.float32
        )
        results.append(mixture.astype(jnp.bfloat16).reshape(block_rows, heads_here * HEAD_SIZE))
    return jnp.concatenate(results, axis=0)


def expert_forward(layer_inputs, scaled_rows, gate_w, up_w, down_matrix, factor_a, up_factor):
    gate_part = jnp.dot(layer_inputs, gate_w, preferred_element_type=jnp.float32)
    up_part = jnp.dot(layer_inputs, up_w, preferred_element_type=jnp.float32)
    active_rows = (jax.nn.silu(gate_part) * up_part).astype(jnp.bfloat16)
    lowrank_product = jnp.dot(active_rows, factor_a, preferred_element_type=jnp.float32).astype(
        jnp.bfloat16
    )
    layer_outputs = (
        jnp.dot(active_rows, down_matrix, preferred_element_type=jnp.float32)
        + adapter_scale * jnp.dot(lowrank_product, up_factor, preferred_element_type=jnp.float32)
    ).astype(jnp.bfloat16)
    up_factor_gradient = adapter_scale * jnp.einsum(
        "rk,rd->kd", lowrank_product, scaled_rows, preferred_element_type=jnp.float32
    )
    backward_lowrank = jnp.einsum(
        "rd,kd->rk", scaled_rows, up_factor, preferred_element_type=jnp.float32
    ).astype(jnp.bfloat16)
    down_factor_gradient = adapter_scale * jnp.einsum(
        "rf,rk->fk", active_rows, backward_lowrank, preferred_element_type=jnp.float32
    )
    return (layer_outputs, down_factor_gradient, up_factor_gradient)


def rank_picks(pick_ids, experts):
    picks_here = pick_ids.shape[0]
    block_len = math.gcd(picks_here, 512)
    block_total = picks_here // block_len
    onehot = (
        pick_ids.reshape(block_total, block_len)[:, :, None]
        == jnp.arange(experts, dtype=jnp.int32)[None, None, :]
    ).astype(jnp.bfloat16)
    inner = jnp.arange(block_len)
    strictly_lower = (inner[None, :] < inner[:, None]).astype(jnp.bfloat16)
    within = jnp.einsum("ij,bje->bie", strictly_lower, onehot, preferred_element_type=jnp.float32)
    block_sums = jnp.sum(onehot.astype(jnp.float32), axis=1)
    outer = jnp.arange(block_total)
    earlier_blocks = (outer[None, :] < outer[:, None]).astype(jnp.float32)
    prior = jnp.dot(earlier_blocks, block_sums, preferred_element_type=jnp.float32)
    before = within + prior[:, None, :]
    counted = jnp.sum(before * onehot.astype(jnp.float32), axis=-1)
    return counted.reshape(picks_here).astype(jnp.int32)


def shards(
    queries,
    keys,
    values,
    document_index,
    residual,
    output_projection,
    norm_gain_weight,
    routed_experts,
    router_logits,
    gate_weight,
    up_weight,
    down_weight,
    adapter_down,
    adapter_up,
    cotangent,
):
    seq_devices = lax.axis_size("seq")
    all_devices = seq_devices * lax.axis_size("expert")
    tokens_here = queries.shape[1]
    heads_here = QUERY_HEADS // seq_devices
    query_group_size = QUERY_HEADS // KEY_VALUE_HEADS
    local_queries = queries[0]
    query_heads = lax.all_to_all(local_queries, "seq", split_axis=1, concat_axis=0, tiled=True)
    key_all, value_all = (
        lax.all_gather(keys[0], "seq", axis=0, tiled=True),
        lax.all_gather(values[0], "seq", axis=0, tiled=True),
    )
    kv_head = lax.axis_index("seq") * heads_here // query_group_size
    key_rows = lax.dynamic_slice_in_dim(key_all, kv_head * HEAD_SIZE, HEAD_SIZE, 1)
    value_rows = lax.dynamic_slice_in_dim(value_all, kv_head * HEAD_SIZE, HEAD_SIZE, 1)
    attended = attend_heads(query_heads, key_rows, value_rows, document_index[0])
    merged = lax.all_to_all(attended, "seq", split_axis=0, concat_axis=1, tiled=True)
    projected = jnp.dot(
        merged,
        lax.all_gather(output_projection, "expert", axis=1, tiled=True),
        preferred_element_type=jnp.float32,
    )
    stream = residual[0].astype(jnp.float32) + projected
    spread = jnp.mean(stream * stream, axis=-1, keepdims=True)
    hidden = (stream * lax.rsqrt(spread + norm_eps) * norm_gain_weight).astype(jnp.bfloat16)
    model_width = hidden.shape[-1]
    experts = all_devices * gate_weight.shape[0]
    capacity = 9 * tokens_here * PICKS_PER_TOKEN // (8 * experts)
    picks_here = tokens_here * PICKS_PER_TOKEN
    gate_probs = jax.nn.softmax(router_logits[0], axis=-1)
    pick_ids = routed_experts[0].reshape(-1)
    pick_rank = rank_picks(pick_ids, experts)
    slot_index = pick_ids * capacity + pick_rank
    source = (
        jnp.full((experts * capacity,), picks_here, jnp.int32)
        .at[slot_index]
        .set(jnp.arange(picks_here, dtype=jnp.int32))
    )
    usable = source < picks_here
    clamped = jnp.minimum(source, picks_here - 1)
    token_rows = clamped // PICKS_PER_TOKEN
    gate_rows = jnp.where(usable, gate_probs.reshape(-1)[clamped], jnp.zeros((), jnp.float32))
    upstream = cotangent[0]
    layer_inputs = jnp.where(usable[:, None], hidden[token_rows], jnp.zeros((), jnp.bfloat16))
    scaled_rows = (gate_rows[:, None] * upstream[token_rows].astype(jnp.float32)).astype(
        jnp.bfloat16
    )
    layer_inputs = layer_inputs.reshape(experts, capacity, model_width)
    scaled_rows = scaled_rows.reshape(experts, capacity, model_width)
    got_inputs, got_scaled = (
        lax.all_to_all(layer_inputs, ("seq", "expert"), split_axis=0, concat_axis=0, tiled=True),
        lax.all_to_all(scaled_rows, ("seq", "expert"), split_axis=0, concat_axis=0, tiled=True),
    )
    layer_outputs, down_factor_gradient, up_factor_gradient = expert_forward(
        got_inputs.reshape(-1, model_width),
        got_scaled.reshape(-1, model_width),
        gate_weight[0],
        up_weight[0],
        down_weight[0],
        adapter_down[0],
        adapter_up[0],
    )
    back_rows = lax.all_to_all(
        layer_outputs.reshape(all_devices, capacity, model_width),
        ("seq", "expert"),
        split_axis=0,
        concat_axis=0,
        tiled=True,
    )
    per_pick = back_rows.reshape(experts * capacity, model_width)[slot_index].reshape(
        tokens_here, PICKS_PER_TOKEN, model_width
    )
    combined_output = jnp.sum(gate_probs[:, :, None] * per_pick.astype(jnp.float32), axis=1)
    picked_products = jnp.einsum(
        "td,tkd->tk", upstream, per_pick, preferred_element_type=jnp.float32
    )
    router_logit_gradient = gate_probs * (
        picked_products - jnp.sum(gate_probs * picked_products, axis=-1, keepdims=True)
    )
    return (
        combined_output.astype(jnp.bfloat16)[None],
        down_factor_gradient[None],
        up_factor_gradient[None],
        router_logit_gradient[None],
    )


def solution(mesh):
    return jax.shard_map(
        shards,
        mesh=mesh,
        in_specs=(
            P(("groups", "expert"), "seq", None),
            P(("groups", "expert"), "seq", None),
            P(("groups", "expert"), "seq", None),
            P(("groups", "expert"), None),
            P(("groups", "expert"), "seq", None),
            P(None, "expert"),
            P(),
            P(("groups", "expert"), "seq", None),
            P(("groups", "expert"), "seq", None),
            P(("seq", "expert"), None, None),
            P(("seq", "expert"), None, None),
            P(("seq", "expert"), None, None),
            P(("seq", "expert"), None, None),
            P(("seq", "expert"), None, None),
            P(("groups", "expert"), "seq", None),
        ),
        out_specs=(
            P(("groups", "expert"), "seq", None),
            P(("groups", "seq", "expert"), None, None),
            P(("groups", "seq", "expert"), None, None),
            P(("groups", "expert"), "seq", None),
        ),
        check_vma=False,
    )
```

profile of v0, /device:TPU:0, one launch (start us, length us, event | category | flops | bytes accessed | tf_op | source)
XLA Modules:
  0.0 591.8 jit_solution(13716606181137053072)
XLA Ops:
  8.0 1.3 copy.55
  9.2 1.0 copy.39
  10.2 5.2 all-to-all-start
  16.6 4.3 scatter_custom_fusion
  20.9 11.5 %all-gather = bf16[1,1024,256]{1,2,0:T(8,128)(2,1)} all-gather(bf16[1,128,256]{1,2,0:T(8,128)(2,1)S(1)} %copy.38), channel_id=2, replica_groups=mesh['groups'=1,'seq'=8,'expert'=4] {'seq'}, dimensions={1}, use_global_device_ids=true | all-gather | bytes 589824 | tf_op jit(solution)/shard_map/all_gather | solution.py:118
  32.5 10.7 %all-gather.1 = bf16[1,1024,256]{2,1,0:T(8,128)(2,1)} all-gather(bf16[1,128,256]{2,1,0:T(8,128)(2,1)S(1)} %copy-done.5), channel_id=3, replica_groups=mesh['groups'=1,'seq'=8,'expert'=4] {'seq'}, dimensions={1}, use_global_device_ids=true | all-gather | bytes 589824 | tf_op jit(solution)/shard_map/all_gather | solution.py:117
  43.2 1.0 compare_and_fusion
  44.2 1.3 fusion.16
  45.4 1.8 fusion.102
  48.0 2.0 fusion.113
  50.0 3.0 convolution_convert_fusion.2
  53.0 1.1 copy.44
  54.1 1.7 slice.46
  55.8 4.8 fusion.104
  60.6 3.5 fusion.20
  64.1 1.8 copy.45
  65.9 1.8 pad_maximum_fusion
  67.6 4.6 all-to-all-start.1
  72.9 4.6 gather_fusion.2
  77.6 4.5 all-to-all-done.1
  82.0 2.0 copy.46
  84.1 77.9 %all-gather.4.cloned.1.call-done = bf16[2048,2048]{1,0:T(8,128)(2,1)} async-done(((bf16[2048,512]{1,0:T(8,128)(2,1)}), bf16[2048,2048]{1,0:T(8,128)(2,1)}) %all-gather.4.cloned.1.call-update) | async-done | bytes 8388624 | tf_op jit(solution)/shard_map/all_gather | solution.py:127
  162.0 4.9 multiply_reduce_fusion.1
  167.9 11.8 %gather_fusion = bf16[1152,2048]{1,0:T(8,128)(2,1)} fusion(bf16[128,2048]{1,0:T(8,128)(2,1)} %multiply_convert_fusion.1, s32[2048]{0:T(1024)S(1)} %get-tuple-element.19), kind=kCustom, calls=%fused_computation | custom fusion | bytes 9441792 | tf_op jit(solution)/shard_map/gather | solution.py:151
  179.7 7.3 %gather.15 = bf16[32,36,2048]{2,1,0:T(8,128)(2,1)} reshape(bf16[1152,2048]{1,0:T(8,128)(2,1)} %gather_fusion) | data formatting | bytes 9437184 | tf_op jit(solution)/shard_map/gather | solution.py:151
  187.0 5.2 broadcast_select_fusion
  192.2 3.6 all-to-all-start.2
  195.9 11.8 %gather_fusion.3 = bf16[1152,2048]{1,0:T(8,128)(2,1)} fusion(bf16[128,2048]{1,0:T(8,128)(2,1)} %bitcast.156, s32[2048]{0:T(1024)S(1)} %get-tuple-element.19), kind=kCustom, calls=%fused_computation.3 | custom fusion | bytes 9441792 | tf_op jit(solution)/shard_map/gather | solution.py:152
  207.7 7.9 %reshape.281 = f32[32,36,2048]{2,1,0:T(8,128)} reshape(bf16[1152,2048]{1,0:T(8,128)(2,1)} %gather_fusion.3) | data formatting | bytes 14155776 | tf_op jit(solution)/shard_map/convert_element_type | solution.py:152
  215.6 7.0 %multiply_convert_fusion = bf16[32,36,2048]{2,1,0:T(8,128)(2,1)} fusion(f32[32,36,2048]{2,1,0:T(8,128)} %reshape.281, f32[32,36]{1,0:T(8,128)S(1)} %mul.136), kind=kLoop, calls=%fused_computation.7 | loop fusion | flops 4718592 | bytes 14160384 | tf_op jit(solution)/shard_map/convert_element_type | solution.py:152
  222.5 87.8 %all-to-all-done.2 = bf16[32,36,2048]{2,1,0:T(8,128)(2,1)} async-done(((bf16[32,36,2048]{2,1,0:T(8,128)(2,1)}), bf16[32,36,2048]{2,1,0:T(8,128)(2,1)}, u32[]{:S(2)}, u32[]{:S(2)}) %all-to-all-start.2) | async-done | bytes 4718624 | tf_op jit(solution)/shard_map/all_to_all | solution.py:158
  310.3 6.6 %all-to-all-start.4 = ((bf16[32,36,2048]{2,1,0:T(8,128)(2,1)}), bf16[32,36,2048]{2,1,0:T(8,128)(2,1)}, u32[]{:S(2)}, u32[]{:S(2)}) async-start(bf16[32,36,2048]{2,1,0:T(8,128)(2,1)} %multiply_convert_fusion), calls=%async_computation.4 | async-start | bytes 10485760 | tf_op jit(solution)/shard_map/all_to_all | solution.py:159
  316.9 7.2 %reshape.275 = bf16[1152,2048]{1,0:T(8,128)(2,1)} reshape(bf16[32,36,2048]{2,1,0:T(8,128)(2,1)} %all-to-all-done.2) | data formatting | bytes 9437184 | tf_op jit(solution)/shard_map/reshape | solution.py:162
  324.1 6.8 %fusion.11 = f32[1152,768]{1,0:T(8,128)S(1)} fusion(bf16[1152,2048]{1,0:T(8,128)(2,1)} %reshape.275, bf16[1,2048,768]{2,1,0:T(8,128)(2,1)} %param.24), kind=kOutput, calls=%fused_computation.24 | convolution fusion | flops 3623878656 | bytes 11403264 | tf_op jit(solution)/shard_map/dot_general | solution.py:50
  330.9 4.2 fusion.6
  336.4 3.9 fusion.8
  340.2 3.5 fusion.3
  343.8 7.2 %reshape.276 = bf16[32,36,2048]{2,1,0:T(8,128)(2,1)} reshape(bf16[1152,2048]{1,0:T(8,128)(2,1)} %fusion.3) | data formatting | bytes 9437184 | tf_op jit(solution)/shard_map/reshape | solution.py:171
  351.0 80.4 %all-to-all-done.4 = bf16[32,36,2048]{2,1,0:T(8,128)(2,1)} async-done(((bf16[32,36,2048]{2,1,0:T(8,128)(2,1)}), bf16[32,36,2048]{2,1,0:T(8,128)(2,1)}, u32[]{:S(2)}, u32[]{:S(2)}) %all-to-all-start.4) | async-done | bytes 4718624 | tf_op jit(solution)/shard_map/all_to_all | solution.py:159
  431.4 6.6 %all-to-all-start.3 = ((bf16[32,36,2048]{2,1,0:T(8,128)(2,1)}), bf16[32,36,2048]{2,1,0:T(8,128)(2,1)}, u32[]{:S(2)}, u32[]{:S(2)}) async-start(bf16[32,36,2048]{2,1,0:T(8,128)(2,1)} %reshape.276), calls=%async_computation.3 | async-start | bytes 10485760 | tf_op jit(solution)/shard_map/all_to_all | solution.py:170
  438.0 7.2 %reshape.279 = bf16[1152,2048]{1,0:T(8,128)(2,1)} reshape(bf16[32,36,2048]{2,1,0:T(8,128)(2,1)} %all-to-all-done.4) | data formatting | bytes 9437184 | tf_op jit(solution)/shard_map/reshape | solution.py:163
  445.3 4.0 fusion.13
  449.2 5.4 fusion.23
  454.7 97.9 %all-to-all-done.3 = bf16[32,36,2048]{2,1,0:T(8,128)(2,1)} async-done(((bf16[32,36,2048]{2,1,0:T(8,128)(2,1)}), bf16[32,36,2048]{2,1,0:T(8,128)(2,1)}, u32[]{:S(2)}, u32[]{:S(2)}) %all-to-all-start.3) | async-done | bytes 4718624 | tf_op jit(solution)/shard_map/all_to_all | solution.py:170
  552.5 7.2 %reshape.277 = bf16[1152,2048]{1,0:T(8,128)(2,1)} reshape(bf16[32,36,2048]{2,1,0:T(8,128)(2,1)} %all-to-all-done.3) | data formatting | bytes 9437184 | tf_op jit(solution)/shard_map/reshape | solution.py:177
  559.8 11.8 %gather_fusion.1 = bf16[1024,2048]{1,0:T(8,128)(2,1)} fusion(bf16[1152,2048]{1,0:T(8,128)(2,1)} %reshape.277, s32[1024]{0:T(1024)S(1)} %broadcast_clamp_fusion), kind=kCustom, calls=%fused_computation.1 | custom fusion | bytes 8392704 | tf_op jit(solution)/shard_map/gather | solution.py:177
  571.6 5.0 fusion.4
  577.4 7.3 %multiply_reduce_fusion = bf16[128,2048]{1,0:T(8,128)(2,1)} fusion(bf16[1024,2048]{1,0:T(8,128)(2,1)} %gather_fusion.1, f32[128,8]{1,0:T(8,128)S(1)} %copy.35), kind=kLoop, calls=%fused_computation.10 | loop fusion | flops 6029312 | bytes 4722688 | tf_op jit(solution)/shard_map/reduce_sum | solution.py:180
  (70 shorter events, 6.4 us)
Async XLA Ops:
  7.2 329.2 %copy-start = (bf16[1,768,2048]{2,1,0:T(8,128)(2,1)S(1)}, bf16[1,768,2048]{2,1,0:T(8,128)(2,1)}, u32[]{:S(2)}) copy-start(bf16[1,768,2048]{2,1,0:T(8,128)(2,1)} %param.26) | copy-start | bytes 9437188
  7.2 8.2 %copy-start.10 = (s32[1,128,8]{1,2,0:T(8,128)S(1)}, s32[1,128,8]{1,2,0:T(8,128)}, u32[]{:S(2)}) copy-start(s32[1,128,8]{1,2,0:T(8,128)} %param.22) | copy-start | bytes 12292
  7.2 8.6 %copy-start.7 = (bf16[1,128,256]{2,1,0:T(8,128)(2,1)S(1)}, bf16[1,128,256]{2,1,0:T(8,128)(2,1)}, u32[]{:S(2)}) copy-start(bf16[1,128,256]{2,1,0:T(8,128)(2,1)} %param.17) | copy-start | bytes 196612
  7.2 9.3 %copy-start.6 = (f32[1,128,8]{1,2,0:T(8,128)S(1)}, f32[1,128,8]{1,2,0:T(8,128)}, u32[]{:S(2)}) copy-start(f32[1,128,8]{1,2,0:T(8,128)} %param.23) | copy-start | bytes 12292
  7.2 25.3 %copy-start.5 = (bf16[1,128,256]{2,1,0:T(8,128)(2,1)S(1)}, bf16[1,128,256]{2,1,0:T(8,128)(2,1)}, u32[]{:S(2)}) copy-start(bf16[1,128,256]{2,1,0:T(8,128)(2,1)} %param.16) | copy-start | bytes 196612
  7.2 36.0 %copy-start.9 = (s32[1,1024]{1,0:T(1,128)S(1)}, s32[1,1024]{1,0:T(1,128)}, u32[]{:S(2)}) copy-start(s32[1,1024]{1,0:T(1,128)} %param.18) | copy-start | bytes 12292
  7.2 154.8 %all-gather.4.cloned.1.call-start = ((), (), s32[]{:S(2)}) async-start(), calls=%async_computation.5 | async-start | bytes 10485760 | tf_op jit(solution)/shard_map/all_gather | solution.py:127
  10.2 35.2 %all-to-all-start = ((bf16[128,8,256]{2,0,1:T(8,128)(2,1)}), bf16[128,8,256]{2,0,1:T(8,128)(2,1)}, u32[]{:S(2)}, u32[]{:S(2)}) async-start(bf16[128,8,256]{2,0,1:T(8,128)(2,1)} %copy.39), calls=%async_computation | async-start | bytes 1048576 | tf_op jit(solution)/shard_map/all_to_all | solution.py:115
  48.0 2.0 copy-start.4
  67.6 14.4 %all-to-all-start.1 = ((bf16[8,128,256]{2,1,0:T(8,128)(2,1)}), bf16[8,128,256]{2,1,0:T(8,128)(2,1)}, u32[]{:S(2)}, u32[]{:S(2)}) async-start(bf16[8,128,256]{2,1,0:T(8,128)(2,1)} %bitcast.159), calls=%async_computation.1 | async-start | bytes 1048576 | tf_op jit(solution)/shard_map/all_to_all | solution.py:124
  162.0 5.0 copy-start.11
  192.2 118.1 %all-to-all-start.2 = ((bf16[32,36,2048]{2,1,0:T(8,128)(2,1)}), bf16[32,36,2048]{2,1,0:T(8,128)(2,1)}, u32[]{:S(2)}, u32[]{:S(2)}) async-start(bf16[32,36,2048]{2,1,0:T(8,128)(2,1)} %broadcast_select_fusion), calls=%async_computation.2 | async-start | bytes 10485760 | tf_op jit(solution)/shard_map/all_to_all | solution.py:158
  310.3 121.1 %all-to-all-start.4 = ((bf16[32,36,2048]{2,1,0:T(8,128)(2,1)}), bf16[32,36,2048]{2,1,0:T(8,128)(2,1)}, u32[]{:S(2)}, u32[]{:S(2)}) async-start(bf16[32,36,2048]{2,1,0:T(8,128)(2,1)} %multiply_convert_fusion), calls=%async_computation.4 | async-start | bytes 10485760 | tf_op jit(solution)/shard_map/all_to_all | solution.py:159
  324.1 6.8 %copy-start.2 = (bf16[1152,2048]{1,0:T(8,128)(2,1)S(1)}, bf16[1152,2048]{1,0:T(8,128)(2,1)}, u32[]{:S(2)}) copy-start(bf16[1152,2048]{1,0:T(8,128)(2,1)} %reshape.275) | copy-start | bytes 14155780
  324.1 6.8 %copy-start.12 = (bf16[1,2048,768]{2,1,0:T(8,128)(2,1)S(1)}, bf16[1,2048,768]{2,1,0:T(8,128)(2,1)}, u32[]{:S(2)}) copy-start(bf16[1,2048,768]{2,1,0:T(8,128)(2,1)} %param.25) | copy-start | bytes 9437188
  330.9 4.2 copy-start.8
  335.1 1.2 copy-start.1
  336.4 3.9 copy-start.3
  431.4 121.1 %all-to-all-start.3 = ((bf16[32,36,2048]{2,1,0:T(8,128)(2,1)}), bf16[32,36,2048]{2,1,0:T(8,128)(2,1)}, u32[]{:S(2)}, u32[]{:S(2)}) async-start(bf16[32,36,2048]{2,1,0:T(8,128)(2,1)} %reshape.276), calls=%async_computation.3 | async-start | bytes 10485760 | tf_op jit(solution)/shard_map/all_to_all | solution.py:170
Sparse Core Ops, SparseCore 0:
  9.6 152.3 all-gather.3
where the time goes:
time: 601 us; the launch traced here: 592 us
  waiting for transfers between devices  349 us (58%)
  local copies, waits for them, and re-layouts  102 us (17%)
  matrix products  52 us (9%)
  starting transfers between devices  26.6 us (4%)
  other arithmetic  25.4 us (4%)
  blocking collectives  22.2 us (4%)
  between operations  14.6 us (2%)
    all_to_all x1, waiting for transfers between devices, shards(): lax.all_to_all(layer_outputs.reshape(all_devices, capacity, model_width),...  97.9 us
    all_to_all x1, waiting for transfers between devices, shards(): lax.all_to_all(layer_inputs, ('seq', 'expert'), split_axis=0, concat_axis...  87.8 us
    all_to_all x1, waiting for transfers between devices, shards(): lax.all_to_all(scaled_rows, ('seq', 'expert'), split_axis=0, concat_axis=...  80.4 us
    all_gather x1, waiting for transfers between devices, shards(): lax.all_gather(output_projection, 'expert', axis=1, tiled=True)  77.9 us
    gather x2, local copies, waits for them, and re-layouts, shards(): hidden[token_rows]  19 us
  transfers between devices with their start and end apart: 6, of which 5 were waited for; matrix products, arithmetic and copies ran while one was open for 20% of the time, Pallas kernels for 0%

commit v1 on v0

v1 whole, which is shorter than its diff:
```python
import math

import jax
import jax.numpy as jnp
from jax import lax
from jax.experimental import pallas as pl
from jax.experimental.pallas import tpu as pltpu
from jax.sharding import PartitionSpec as P

QUERY_HEADS = 16
KEY_VALUE_HEADS = 2
HEAD_SIZE = 128
PICKS_PER_TOKEN = 8

adapter_scale = 2.0
norm_eps = 1e-06
BF16 = jnp.bfloat16
F32 = jnp.float32


def dot(a, b):
    return jnp.dot(a, b, preferred_element_type=F32)


def dot_t(a, b):
    return lax.dot_general(a, b, (((1,), (1,)), ((), ())), preferred_element_type=F32)


def attend_kernel(start_ref, query_ref, kv_ref, bias_ref, out_ref):
    tokens = query_ref.shape[0]
    window = bias_ref.shape[1]
    start = pl.multiple_of(start_ref[0] * tokens, tokens)
    bias = bias_ref[...]
    group = QUERY_HEADS // KEY_VALUE_HEADS
    width = KEY_VALUE_HEADS * HEAD_SIZE
    factor = math.log2(math.e) / math.sqrt(HEAD_SIZE)
    for kv_head in range(KEY_VALUE_HEADS):
        first = kv_head * HEAD_SIZE
        key_rows = kv_ref[pl.ds(start, window), first : first + HEAD_SIZE]
        value_rows = kv_ref[pl.ds(start, window), width + first : width + first + HEAD_SIZE]
        for pair in range(group // 2):
            at = (kv_head * group + pair * 2) * HEAD_SIZE
            rows = jnp.concatenate(
                [
                    query_ref[:, at : at + HEAD_SIZE],
                    query_ref[:, at + HEAD_SIZE : at + 2 * HEAD_SIZE],
                ],
                axis=0,
            )
            scores = dot_t(rows, key_rows).reshape(2, tokens, window) + bias[None]
            highest = jnp.max(scores, axis=-1, keepdims=True)
            raised = jnp.exp2((scores - highest) * factor)
            total = jnp.sum(raised, axis=-1, keepdims=True)
            mixed = dot(raised.astype(BF16).reshape(2 * tokens, window), value_rows)
            mixed = (mixed.reshape(2, tokens, HEAD_SIZE) / total).astype(BF16)
            out_ref[:, at : at + HEAD_SIZE] = mixed[0]
            out_ref[:, at + HEAD_SIZE : at + 2 * HEAD_SIZE] = mixed[1]


def attend(queries, kv_all, documents):
    tokens = queries.shape[0]
    length = kv_all.shape[0]
    place = lax.axis_index("seq")
    window = min(length, length // 2 + tokens)
    first_block = jnp.clip(place + 1 - window // tokens, 0, (length - window) // tokens)
    mine = place * tokens + jnp.arange(tokens)
    there = first_block * tokens + jnp.arange(window)
    doc_mine = lax.dynamic_slice_in_dim(documents, place * tokens, tokens)
    doc_there = lax.dynamic_slice_in_dim(documents, first_block * tokens, window)
    allowed = (there[None, :] <= mine[:, None]) & (doc_there[None, :] == doc_mine[:, None])
    bias = jnp.where(allowed, 0.0, -jnp.inf).astype(F32)
    return pl.pallas_call(
        attend_kernel,
        out_shape=jax.ShapeDtypeStruct(queries.shape, BF16),
        in_specs=[
            pl.BlockSpec(memory_space=pltpu.SMEM),
            pl.BlockSpec(memory_space=pltpu.VMEM),
            pl.BlockSpec(memory_space=pltpu.VMEM),
            pl.BlockSpec(memory_space=pltpu.VMEM),
        ],
        out_specs=pl.BlockSpec(memory_space=pltpu.VMEM),
        compiler_params=pltpu.CompilerParams(vmem_limit_bytes=32 << 20),
        name="attend",
    )(first_block.reshape(1).astype(jnp.int32), queries, kv_all, bias)


def shards(
    queries,
    keys,
    values,
    document_index,
    residual,
    output_projection,
    norm_gain_weight,
    routed_experts,
    router_logits,
    gate_weight,
    up_weight,
    down_weight,
    adapter_down,
    adapter_up,
    cotangent,
):
    seq_devices = lax.axis_size("seq")
    columns = lax.axis_size("expert")
    column = lax.axis_index("expert")
    tokens = queries.shape[1]
    width = queries.shape[2]
    experts = seq_devices * columns
    rank = adapter_up.shape[1]
    near = columns * tokens

    kv_all = lax.all_gather(
        jnp.concatenate([keys[0], values[0]], axis=1), "seq", axis=0, tiled=True
    )
    gate_probs = jax.nn.softmax(router_logits[0], axis=-1)
    routing = lax.all_gather(
        jnp.concatenate([gate_probs, routed_experts[0].astype(F32)], axis=1),
        "expert",
        axis=0,
        tiled=True,
    )
    projection = lax.all_gather(output_projection, "expert", axis=0)
    up_factors = lax.all_gather(adapter_up[0], "seq", axis=0, tiled=True)
    upstream = lax.all_gather(cotangent[0], "expert", axis=0, tiled=True)

    capacity = columns * (9 * tokens * PICKS_PER_TOKEN // (8 * experts))
    capacity = -(-capacity // 16) * 16
    near_probs = routing[:, :PICKS_PER_TOKEN]
    near_picks = routing[:, PICKS_PER_TOKEN:].astype(jnp.int32)
    plane_experts = jnp.arange(seq_devices) * columns + column
    hits = near_picks[:, :, None] == plane_experts[None, None, :]
    member = jnp.any(hits, axis=1)
    gates = jnp.sum(jnp.where(hits, near_probs[:, :, None], 0.0), axis=1)
    inner = jnp.arange(near)
    lower = (inner[None, :] < inner[:, None]).astype(BF16)
    ranks = dot(lower, member.astype(BF16)).astype(jnp.int32)
    slot = jnp.where(member, ranks, capacity)
    picker = (slot.T[:, None, :] == jnp.arange(capacity)[None, :, None]).reshape(
        seq_devices * capacity, near
    )
    onehot = picker.astype(BF16)
    weighted = (
        jnp.where(picker.reshape(seq_devices, capacity, near), gates.T[:, None, :], 0.0)
        .astype(BF16)
        .reshape(seq_devices * capacity, near)
    )

    back_all = dot_t(upstream, up_factors).reshape(near, seq_devices, rank)
    back_all = (back_all * gates[:, :, None]).astype(BF16)
    back_slots = jnp.einsum(
        "jct,tjr->jcr",
        onehot.reshape(seq_devices, capacity, near),
        back_all,
        preferred_element_type=F32,
    ).astype(BF16)
    back_low = lax.all_to_all(back_slots, "seq", split_axis=0, concat_axis=0, tiled=True)
    back_low = back_low.reshape(seq_devices * capacity, rank)
    upstream_slots = dot(onehot, upstream).astype(BF16)

    attended = attend(queries[0], kv_all, document_index[0])
    projected = jnp.einsum("tk,zkn->tzn", attended, projection, preferred_element_type=F32)
    stream = residual[0].astype(F32) + projected.reshape(tokens, width)
    spread = jnp.mean(stream * stream, axis=-1, keepdims=True)
    hidden = (stream * lax.rsqrt(spread + norm_eps) * norm_gain_weight).astype(BF16)

    hidden_near = lax.all_gather(hidden, "expert", axis=0, tiled=True)
    sent = dot(onehot, hidden_near).astype(BF16).reshape(seq_devices, capacity, width)
    rows = lax.all_to_all(sent, "seq", split_axis=0, concat_axis=0, tiled=True)
    rows = rows.reshape(seq_devices * capacity, width)

    gate_part = dot(rows, gate_weight[0])
    up_part = dot(rows, up_weight[0])
    active = (jax.nn.silu(gate_part) * up_part).astype(BF16)
    low_rank = dot(active, adapter_down[0]).astype(BF16)
    outputs = (dot(active, down_weight[0]) + adapter_scale * dot(low_rank, adapter_up[0])).astype(
        BF16
    )
    down_factor_gradient = adapter_scale * lax.dot_general(
        active, back_low, (((0,), (0,)), ((), ())), preferred_element_type=F32
    )
    low_near = lax.all_to_all(
        low_rank.reshape(seq_devices, capacity, rank), "seq", split_axis=0, concat_axis=0, tiled=True
    )
    returned = lax.all_to_all(
        outputs.reshape(seq_devices, capacity, width),
        "seq",
        split_axis=0,
        concat_axis=0,
        tiled=True,
    ).reshape(seq_devices * capacity, width)

    low_weighted = jnp.einsum(
        "jct,jcr->jrt",
        weighted.reshape(seq_devices, capacity, near),
        low_near,
        preferred_element_type=F32,
    ).astype(BF16)
    up_parts = dot(low_weighted.reshape(seq_devices * rank, near), upstream)
    up_factor_gradient = adapter_scale * lax.psum_scatter(
        up_parts, "seq", scatter_dimension=0, tiled=True
    )

    combined = lax.dot_general(
        weighted, returned, (((0,), (0,)), ((), ())), preferred_element_type=F32
    )
    slot_dots = jnp.sum(returned.astype(F32) * upstream_slots.astype(F32), axis=-1)
    plane_dots = jnp.sum(
        jnp.where(
            picker.reshape(seq_devices, capacity, near),
            slot_dots.reshape(seq_devices, capacity, 1),
            0.0,
        ),
        axis=1,
    )
    all_dots = lax.all_to_all(
        plane_dots.T.reshape(columns, tokens, seq_devices),
        "expert",
        split_axis=0,
        concat_axis=0,
        tiled=True,
    )
    combined_output = lax.psum_scatter(
        combined.astype(BF16), "expert", scatter_dimension=0, tiled=True
    )
    by_expert = all_dots.transpose(1, 2, 0).reshape(tokens, experts)
    own_hits = routed_experts[0][:, :, None] == jnp.arange(experts)[None, None, :]
    picked_products = jnp.sum(jnp.where(own_hits, by_expert[:, None, :], 0.0), axis=-1)
    router_logit_gradient = gate_probs * (
        picked_products - jnp.sum(gate_probs * picked_products, axis=-1, keepdims=True)
    )
    return (
        combined_output.astype(BF16)[None],
        down_factor_gradient[None],
        up_factor_gradient[None],
        router_logit_gradient[None],
    )


def solution(mesh):
    return jax.shard_map(
        shards,
        mesh=mesh,
        in_specs=(
            P(("groups", "expert"), "seq", None),
            P(("groups", "expert"), "seq", None),
            P(("groups", "expert"), "seq", None),
            P(("groups", "expert"), None),
            P(("groups", "expert"), "seq", None),
            P(None, "expert"),
            P(),
            P(("groups", "expert"), "seq", None),
            P(("groups", "expert"), "seq", None),
            P(("seq", "expert"), None, None),
            P(("seq", "expert"), None, None),
            P(("seq", "expert"), None, None),
            P(("seq", "expert"), None, None),
            P(("seq", "expert"), None, None),
            P(("groups", "expert"), "seq", None),
        ),
        out_specs=(
            P(("groups", "expert"), "seq", None),
            P(("groups", "seq", "expert"), None, None),
            P(("groups", "seq", "expert"), None, None),
            P(("groups", "expert"), "seq", None),
        ),
        check_vma=False,
    )
```

time: 601 us -> 477 us (0.79); the launches traced: 592 us -> 476 us
  local copies, waits for them, and re-layouts: 102 us -> 12.5 us
  other arithmetic: 25.4 us -> 9.25 us
  starting transfers between devices: 26.6 us -> 16.5 us
  waiting for transfers between devices: 349 us -> 341 us
    all_to_all x5 -> x4, waiting for transfers between devices: 271 us -> 112 us  [the longest x1 54.2 us: shards(): rows = lax.all_to_all(sent, 'seq', split_axis=0, concat_axis=0, tiled=True)]
    all_gather x1 -> x5, waiting for transfers between devices: 77.9 us -> 197 us  [the longest x1 145 us: shards(): projection = lax.all_gather(output_projection, 'expert', axis=0)]
    gather x5 -> x0, local copies, waits for them, and re-layouts: 47.2 us -> none  [the longest x2 19 us: shards(): hidden[token_rows]]
    reshape x6 -> x3, local copies, waits for them, and re-layouts: 31.8 us -> 1.08 us  [the longest x2 0.91 us: shards(): low_rank.reshape(seq_devices, capacity, rank)]
    reduce_scatter x0 -> x2, waiting for transfers between devices: none -> 30.3 us  [the longest x1 30.3 us: shards(): lax.psum_scatter(combined.astype(BF16), 'expert', scatter_dimension=0, ti...]
    dot_general x13 -> x15, matrix products: 45.2 us -> 56.5 us  [the longest x9 39.4 us: dot(): return jnp.dot(a, b, preferred_element_type=F32)]
    all_to_all x5 -> x4, starting transfers between devices: 26.5 us -> 15.8 us  [the longest x1 4.6 us: shards(): lax.all_to_all(outputs.reshape(seq_devices, capacity, width), 'seq', spli...]
    all_to_all x0 -> x1, blocking collectives: none -> 8.99 us  [shards(): lax.all_to_all(back_slots, 'seq', split_axis=0, concat_axis=0, tiled=True)]
  transfers between devices with their start and end apart: 6 -> 11, of which waited for: 5 -> 7; matrix products, arithmetic and copies ran while one was open for 20% -> 11% of each run, Pallas kernels for 0% -> 1%
where the time goes in v1:
time: 477 us; the launch traced here: 476 us
  waiting for transfers between devices  341 us (71%)
  matrix products  56.5 us (12%)
  blocking collectives  22.3 us (5%)
  starting transfers between devices  16.5 us (3%)
  between operations  14.4 us (3%)
  local copies, waits for them, and re-layouts  12.5 us (3%)
  other arithmetic  9.25 us (2%)
    all_gather x1, waiting for transfers between devices, shards(): projection = lax.all_gather(output_projection, 'expert', axis=0)  145 us
    all_to_all x1, waiting for transfers between devices, shards(): rows = lax.all_to_all(sent, 'seq', split_axis=0, concat_axis=0, tiled=True)  54.2 us
    all_to_all x1, waiting for transfers between devices, shards(): lax.all_to_all(outputs.reshape(seq_devices, capacity, width), 'seq', spli...  53.9 us
    dot_general x9, matrix products, dot(): return jnp.dot(a, b, preferred_element_type=F32)  39.4 us
    reduce_scatter x1, waiting for transfers between devices, shards(): lax.psum_scatter(combined.astype(BF16), 'expert', scatter_dimension=0, ti...  30.3 us
    all_gather x1, waiting for transfers between devices, shards(): hidden_near = lax.all_gather(hidden, 'expert', axis=0, tiled=True)  29.6 us
    all_gather x1, waiting for transfers between devices, shards(): lax.all_gather(jnp.concatenate([keys[0], values[0]], axis=1), 'seq', axis...  22.5 us
    all_gather x1, blocking collectives, shards(): lax.all_gather(jnp.concatenate([gate_probs, routed_experts[0].astype(F32)...  13.3 us
  transfers between devices with their start and end apart: 11, of which 7 were waited for; matrix products, arithmetic and copies ran while one was open for 11% of the time, Pallas kernels for 1%

profile of v1, /device:TPU:0, one launch (start us, length us, event | category | flops | bytes accessed | tf_op | source)
XLA Modules:
  0.0 475.8 jit_solution(14456205074021475824)
XLA Ops:
  7.2 1.7 pad_maximum_fusion
  9.0 0.7 all-gather.13.cloned.1.call-update
  9.8 2.0 copy.33
  11.8 2.2 copy.35
  14.2 22.5 %all-gather.9.cloned.1.call-done.kv_ref = bf16[1024,512]{1,0:T(8,128)(2,1)} async-done(((bf16[128,512]{1,0:T(8,128)(2,1)}), bf16[1024,512]{1,0:T(8,128)(2,1)}) %all-gather.9.cloned.1.call-update) | async-done | bytes 1048592 | tf_op jit(solution)/shard_map/all_gather | solution.py:113
  36.7 1.2 copy-done.3
  37.9 1.0 copy-done.4
  39.0 3.4 attend.1
  42.4 0.8 copy-done.2
  43.2 144.7 %all-gather.13.cloned.1.call-done = bf16[8192,512]{1,0:T(8,128)(2,1)} async-done(((bf16[2048,512]{1,0:T(8,128)(2,1)}), bf16[8192,512]{1,0:T(8,128)(2,1)}) %all-gather.13.cloned.1.call-update) | async-done | bytes 8388624 | tf_op jit(solution)/shard_map/all_gather | solution.py:123
  187.9 6.0 %multiply_reduce_fusion = (f32[128]{0:T(128)S(1)}, f32[128,4,512]{2,0,1:T(8,128)}) fusion(f32[128,4,512]{2,0,1:T(8,128)} %copy.35, bf16[4,2048,512]{2,1,0:T(8,128)(2,1)} %bitcast.110, bf16[128,2048]{1,0:T(8,128)(2,1)} %copy-done.2), kind=kOutput, calls=%fused_computation.45 | convolution fusion | flops 1074528128 | bytes 11010560 | tf_op jit(solution)/shard_map/tk,zkn->tzn/dot_general | solution.py:162
  194.0 2.5 copy.34
  196.5 2.5 fusion.30
  199.2 13.3 %all_gather.21 = f32[512,16]{0,1:T(8,128)S(1)} all-gather(f32[128,16]{0,1:T(8,128)S(1)} %pad_maximum_fusion.1), channel_id=1, replica_groups=mesh['groups'=1,'seq'=8,'expert'=4] {'expert'}, dimensions={0}, use_global_device_ids=true | all-gather | bytes 40960 | tf_op jit(solution)/shard_map/all_gather | solution.py:117
  212.6 0.2 fusion.26
  212.9 1.2 bitcast_compare_fusion
  214.1 29.6 %all-gather.11.cloned.1.call-done = bf16[512,2048]{0,1:T(8,128)(2,1)} async-done(((bf16[128,2048]{0,1:T(8,128)(2,1)}), bf16[512,2048]{0,1:T(8,128)(2,1)}) %all-gather.11.cloned.1.call-update) | async-done | bytes 2097168 | tf_op jit(solution)/shard_map/all_gather | solution.py:167
  243.7 6.6 %convolution_convert_fusion.1 = bf16[1152,2048]{1,0:T(8,128)(2,1)} fusion(pred[1152,512]{1,0:T(32,128)(4,1)} %bitcast_compare_fusion, bf16[512,2048]{0,1:T(8,128)(2,1)} %all-gather.11.cloned.1.call-done), kind=kOutput, calls=%fused_computation.6 | convolution fusion | flops 2418278400 | bytes 7405568 | tf_op jit(solution)/shard_map/dot_general | solution.py:22
  250.3 4.6 all-to-all-start
  255.1 0.3 all-gather.15.cloned.1.call-update
  255.5 54.2 %all-to-all-done = bf16[8,144,2048]{2,1,0:T(8,128)(2,1)} async-done(((bf16[8,144,2048]{2,1,0:T(8,128)(2,1)}), bf16[8,144,2048]{2,1,0:T(8,128)(2,1)}, u32[]{:S(2)}, u32[]{:S(2)}) %all-to-all-start) | async-done | bytes 4718624 | tf_op jit(solution)/shard_map/all_to_all | solution.py:169
  309.6 6.8 %fusion.7 = f32[1152,768]{1,0:T(8,128)S(1)} fusion(bf16[1152,2048]{1,0:T(8,128)(2,1)} %bitcast.16, bf16[1,2048,768]{2,1,0:T(8,128)(2,1)} %param.24), kind=kOutput, calls=%fused_computation.13 | convolution fusion | flops 3623878656 | bytes 11403264 | tf_op jit(solution)/shard_map/dot_general | solution.py:22
  316.4 6.5 %fusion.3 = bf16[1152,768]{1,0:T(8,128)(2,1)S(1)} fusion(bf16[1152,2048]{1,0:T(8,128)(2,1)} %bitcast.16, f32[1152,768]{1,0:T(8,128)S(1)} %fusion.7, bf16[1,2048,768]{2,1,0:T(8,128)(2,1)S(1)} %copy-done.13), kind=kOutput, calls=%fused_computation.9 | convolution fusion | flops 3629187072 | bytes 13172736 | tf_op jit(solution)/shard_map/dot_general | solution.py:22
  323.0 1.2 copy-done.5
  324.2 0.6 convolution_convert_fusion.2
  324.8 0.2 reshape.130
  325.0 0.7 copy.37
  325.7 3.4 all-to-all-start.3
  329.1 5.4 %fusion.4 = f32[1152,2048]{1,0:T(8,128)S(1)} fusion(bf16[1152,768]{1,0:T(8,128)(2,1)} %copy-done.5, bf16[1,768,2048]{2,1,0:T(8,128)(2,1)S(1)} %copy-done), kind=kOutput, calls=%fused_computation.10 | convolution fusion | flops 3623878656 | bytes 14352384 | tf_op jit(solution)/shard_map/dot_general | solution.py:22
  334.5 3.6 fusion.2
  338.1 4.6 all-to-all-start.1
  342.8 0.5 all-gather.17.cloned.1.call-update
  343.4 0.3 fusion.16
  343.8 3.7 fusion.11
  347.5 0.3 reduce-scatter.3.cloned.1.call-start
  347.8 53.9 %all-to-all-done.1 = bf16[8,144,2048]{2,1,0:T(8,128)(2,1)} async-done(((bf16[8,144,2048]{2,1,0:T(8,128)(2,1)}), bf16[8,144,2048]{2,1,0:T(8,128)(2,1)}, u32[]{:S(2)}, u32[]{:S(2)}) %all-to-all-start.1) | async-done | bytes 4718624 | tf_op jit(solution)/shard_map/all_to_all | solution.py:185
  401.7 6.4 %bitcast_convert_fusion = bf16[512,2048]{1,0:T(8,128)(2,1)} fusion(bf16[8,144,2048]{2,1,0:T(8,128)(2,1)} %all-to-all-done.1, f32[8,512]{1,0:T(8,128)S(1)} %bitcast.120, s32[8,512]{1,0:T(8,128)S(1)} %fusion.26), kind=kOutput, calls=%fused_computation.7 | convolution fusion | flops 2418147328 | bytes 6848512 | tf_op jit(solution)/shard_map/dot_general | solution.py:204
  408.2 2.8 fusion.13
  411.0 0.5 fusion.24
  411.5 9.0 %all_to_all.25 = bf16[8,144,32]{1,2,0:T(8,128)(2,1)S(1)} all-to-all(bf16[8,144,32]{1,2,0:T(8,128)(2,1)S(1)} %fusion.24), channel_id=1, replica_groups=mesh['groups'=1,'seq'=8,'expert'=4] {'seq'}, dimensions={0} | all-to-all | bytes 147456 | tf_op jit(solution)/shard_map/all_to_all | solution.py:157
  420.7 1.0 fusion.25
  421.7 6.0 %fusion.1 = f32[1152]{0:T(1024)S(1)} fusion(bf16[8,144,2048]{2,1,0:T(8,128)(2,1)} %all-to-all-done.1, pred[1152,512]{1,0:T(32,128)(4,1)} %bitcast_compare_fusion, bf16[1,512,2048]{2,1,0:T(8,128)(2,1)} %all-gather.15.cloned.1.call-done), kind=kOutput, calls=%fused_computation.3 | convolution fusion | flops 2427714560 | bytes 7410176 | tf_op jit(solution)/shard_map/dot_general | solution.py:22
  427.9 1.1 select_reduce_fusion
  429.0 3.2 all-to-all-start.4
  432.3 1.7 multiply_bitcast_fusion
  433.9 4.0 all-to-all-done.4
  438.0 0.6 fusion.37
  438.6 30.3 %reduce-scatter.3.cloned.1.call-done = bf16[128,2048]{1,0:T(8,128)(2,1)} async-done(((bf16[512,2048]{1,0:T(8,128)(2,1)}), bf16[128,2048]{1,0:T(8,128)(2,1)}) %reduce-scatter.3.cloned.1.call-update) | async-done | bytes 524304 | tf_op jit(solution)/shard_map/reduce_scatter | solution.py:223
  (61 shorter events, 1.5 us)
Async XLA Ops:
  7.2 321.9 %copy-start = (bf16[1,768,2048]{2,1,0:T(8,128)(2,1)S(1)}, bf16[1,768,2048]{2,1,0:T(8,128)(2,1)}, u32[]{:S(2)}) copy-start(bf16[1,768,2048]{2,1,0:T(8,128)(2,1)} %param.26) | copy-start | bytes 9437188
  7.2 6.8 %copy-start.12 = (s32[1,1024]{1,0:T(1,128)S(1)}, s32[1,1024]{1,0:T(1,128)}, u32[]{:S(2)}) copy-start(s32[1,1024]{1,0:T(1,128)} %param.18) | copy-start | bytes 12292
  7.2 29.5 %all-gather.9.cloned.1.call-start = ((), (), s32[]{:S(2)}) async-start(), calls=%async_computation.7 | async-start | bytes 1179648 | tf_op jit(solution)/shard_map/all_gather | solution.py:113
  9.0 179.0 %all-gather.13.cloned.1.call-start = ((), (), s32[]{:S(2)}) async-start(), calls=%async_computation.11 | async-start | bytes 10485760 | tf_op jit(solution)/shard_map/all_gather | solution.py:123
  9.7 234.0 %all-gather.11.cloned.1.call-start = ((), (), s32[]{:S(2)}) async-start(), calls=%async_computation.8 | async-start | bytes 2621440 | tf_op jit(solution)/shard_map/all_gather | solution.py:167
  36.7 1.2 copy-start.3
  37.9 1.0 copy-start.4
  42.4 0.8 copy-start.2
  187.9 8.6 %copy-start.11 = (f32[2048]{0:T(1024)S(1)}, f32[2048]{0:T(1024)}, u32[]{:S(2)}) copy-start(f32[2048]{0:T(1024)} %param.21) | copy-start | bytes 24580
  194.0 5.2 %copy-start.8 = (f32[1,128,8]{1,2,0:T(8,128)S(1)}, f32[1,128,8]{1,2,0:T(8,128)}, u32[]{:S(2)}) copy-start(f32[1,128,8]{1,2,0:T(8,128)} %param.23) | copy-start | bytes 12292
  194.0 5.2 %copy-start.10 = (s32[1,128,8]{1,2,0:T(8,128)S(1)}, s32[1,128,8]{1,2,0:T(8,128)}, u32[]{:S(2)}) copy-start(s32[1,128,8]{1,2,0:T(8,128)} %param.22) | copy-start | bytes 12292
  250.3 59.3 %all-to-all-start = ((bf16[8,144,2048]{2,1,0:T(8,128)(2,1)}), bf16[8,144,2048]{2,1,0:T(8,128)(2,1)}, u32[]{:S(2)}, u32[]{:S(2)}) async-start(bf16[8,144,2048]{2,1,0:T(8,128)(2,1)} %bitcast.113), calls=%async_computation | async-start | bytes 9437184 | tf_op jit(solution)/shard_map/all_to_all | solution.py:169
  254.9 88.9 %all-gather.15.cloned.1.call-start = ((), (), s32[]{:S(2)}) async-start(), calls=%async_computation.12 | async-start | bytes 2621440 | tf_op jit(solution)/shard_map/all_gather | solution.py:125
  309.6 6.8 %copy-start.13 = (bf16[1,2048,768]{2,1,0:T(8,128)(2,1)S(1)}, bf16[1,2048,768]{2,1,0:T(8,128)(2,1)}, u32[]{:S(2)}) copy-start(bf16[1,2048,768]{2,1,0:T(8,128)(2,1)} %param.25) | copy-start | bytes 9437188
  316.4 7.8 %copy-start.9 = (bf16[1,768,32]{1,2,0:T(8,128)(2,1)S(1)}, bf16[1,768,32]{1,2,0:T(8,128)(2,1)}, u32[]{:S(2)}) copy-start(bf16[1,768,32]{1,2,0:T(8,128)(2,1)} %param.27) | copy-start | bytes 147460
  322.9 1.2 copy-start.5
  325.7 12.4 %all-to-all-start.3 = ((bf16[8,144,32]{1,2,0:T(8,128)(2,1)}), bf16[8,144,32]{1,2,0:T(8,128)(2,1)S(1)}, u32[]{:S(2)}, u32[]{:S(2)}) async-start(bf16[8,144,32]{1,2,0:T(8,128)(2,1)} %copy.37), calls=%async_computation.4 | async-start | bytes 262144 | tf_op jit(solution)/shard_map/all_to_all | solution.py:182
  329.1 5.4 %copy-start.7 = (bf16[1,32,2048]{2,1,0:T(8,128)(2,1)S(1)}, bf16[1,32,2048]{2,1,0:T(8,128)(2,1)}, u32[]{:S(2)}) copy-start(bf16[1,32,2048]{2,1,0:T(8,128)(2,1)} %param.28) | copy-start | bytes 393220
  338.1 63.6 %all-to-all-start.1 = ((bf16[8,144,2048]{2,1,0:T(8,128)(2,1)}), bf16[8,144,2048]{2,1,0:T(8,128)(2,1)}, u32[]{:S(2)}, u32[]{:S(2)}) async-start(bf16[8,144,2048]{2,1,0:T(8,128)(2,1)} %bitcast.111), calls=%async_computation.1 | async-start | bytes 9437184 | tf_op jit(solution)/shard_map/all_to_all | solution.py:185
  342.7 65.5 %all-gather.17.cloned.1.call-start = ((), (), s32[]{:S(2)}) async-start(), calls=%async_computation.13 | async-start | bytes 1179648 | tf_op jit(solution)/shard_map/all_gather | solution.py:124
  343.3 89.0 %reduce-scatter.5.cloned.1.call-start = ((), (), s32[]{:S(2)}) async-start(), calls=%async_computation.10 | async-start | bytes 2359296 | tf_op jit(solution)/shard_map/reduce_scatter | solution.py:200
  347.5 121.4 %reduce-scatter.3.cloned.1.call-start = ((), (), s32[]{:S(2)}) async-start(), calls=%async_computation.9 | async-start | bytes 2621440 | tf_op jit(solution)/shard_map/reduce_scatter | solution.py:223
  408.1 12.6 %copy-start.6 = (bf16[1152,768]{1,0:T(8,128)(2,1)S(1)}, bf16[1152,768]{1,0:T(8,128)(2,1)}, u32[]{:S(2)}) copy-start(bf16[1152,768]{1,0:T(8,128)(2,1)} %copy-done.5) | copy-start | bytes 5308420
  421.7 47.2 %copy-start.1 = (bf16[1,768,2048]{2,1,0:T(8,128)(2,1)S(1)}, bf16[1,768,2048]{2,1,0:T(8,128)(2,1)}, u32[]{:S(2)}) copy-start(bf16[1,768,2048]{2,1,0:T(8,128)(2,1)} %param.26) | copy-start | bytes 9437188
  429.0 9.0 %all-to-all-start.4 = ((f32[4,128,8]{1,2,0:T(8,128)}), f32[4,128,8]{1,2,0:T(8,128)S(1)}, u32[]{:S(2)}, u32[]{:S(2)}) async-start(f32[4,128,8]{1,2,0:T(8,128)} %bitcast.33), calls=%async_computation.6 | async-start | bytes 32768 | tf_op jit(solution)/shard_map/all_to_all | solution.py:216
Sparse Core Ops, SparseCore 0:
  10.5 26.1 all-gather.8
  38.3 149.6 all-gather.12
  199.2 44.5 all-gather.10
  257.0 44.7 all-gather.14
  345.1 35.6 all-gather.16
  383.9 38.5 reduce-scatter.4
  425.5 43.3 reduce-scatter.2

commit v2 on v1

v2 whole, which is shorter than its diff:
```python
import math

import jax
import jax.numpy as jnp
from jax import lax
from jax.experimental import pallas as pl
from jax.experimental.pallas import tpu as pltpu
from jax.sharding import PartitionSpec as P

QUERY_HEADS = 16
KEY_VALUE_HEADS = 2
HEAD_SIZE = 128
PICKS_PER_TOKEN = 8

adapter_scale = 2.0
norm_eps = 1e-06
BF16 = jnp.bfloat16
F32 = jnp.float32


def dot(a, b):
    return jnp.dot(a, b, preferred_element_type=F32)


def dot_t(a, b):
    return lax.dot_general(a, b, (((1,), (1,)), ((), ())), preferred_element_type=F32)


def attend_kernel(start_ref, query_ref, kv_ref, bias_ref, *refs):
    out_ref = refs[-1]
    tokens = query_ref.shape[0]
    window = bias_ref.shape[1]
    start = pl.multiple_of(start_ref[0] * tokens, tokens)
    bias = bias_ref[...]
    group = QUERY_HEADS // KEY_VALUE_HEADS
    width = KEY_VALUE_HEADS * HEAD_SIZE
    factor = math.log2(math.e) / math.sqrt(HEAD_SIZE)
    for kv_head in range(KEY_VALUE_HEADS):
        first = kv_head * HEAD_SIZE
        key_rows = kv_ref[pl.ds(start, window), first : first + HEAD_SIZE]
        value_rows = kv_ref[pl.ds(start, window), width + first : width + first + HEAD_SIZE]
        for pair in range(group // 2):
            at = (kv_head * group + pair * 2) * HEAD_SIZE
            rows = jnp.concatenate(
                [
                    query_ref[:, at : at + HEAD_SIZE],
                    query_ref[:, at + HEAD_SIZE : at + 2 * HEAD_SIZE],
                ],
                axis=0,
            )
            scores = dot_t(rows, key_rows).reshape(2, tokens, window) + bias[None]
            highest = jnp.max(scores, axis=-1, keepdims=True)
            raised = jnp.exp2((scores - highest) * factor)
            total = jnp.sum(raised, axis=-1, keepdims=True)
            mixed = dot(raised.astype(BF16).reshape(2 * tokens, window), value_rows)
            mixed = (mixed.reshape(2, tokens, HEAD_SIZE) / total).astype(BF16)
            out_ref[:, at : at + HEAD_SIZE] = mixed[0]
            out_ref[:, at + HEAD_SIZE : at + 2 * HEAD_SIZE] = mixed[1]


def attend(queries, kv_all, documents, earlier):
    tokens = queries.shape[0]
    length = kv_all.shape[0]
    place = lax.axis_index("seq")
    window = min(length, length // 2 + tokens)
    first_block = jnp.clip(place + 1 - window // tokens, 0, (length - window) // tokens)
    mine = place * tokens + jnp.arange(tokens)
    there = first_block * tokens + jnp.arange(window)
    doc_mine = lax.dynamic_slice_in_dim(documents, place * tokens, tokens)
    doc_there = lax.dynamic_slice_in_dim(documents, first_block * tokens, window)
    allowed = (there[None, :] <= mine[:, None]) & (doc_there[None, :] == doc_mine[:, None])
    bias = jnp.where(allowed, 0.0, -jnp.inf).astype(F32)
    return pl.pallas_call(
        attend_kernel,
        out_shape=jax.ShapeDtypeStruct(queries.shape, BF16),
        in_specs=[
            pl.BlockSpec(memory_space=pltpu.SMEM),
            pl.BlockSpec(memory_space=pltpu.VMEM),
            pl.BlockSpec(memory_space=pltpu.VMEM),
            pl.BlockSpec(memory_space=pltpu.VMEM),
        ]
        + [anywhere()] * len(earlier),
        out_specs=pl.BlockSpec(memory_space=pltpu.VMEM),
        compiler_params=params(),
        name="attend",
    )(first_block.reshape(1).astype(jnp.int32), queries, kv_all, bias, *earlier)


def vmem():
    return pl.BlockSpec(memory_space=pltpu.VMEM)


def anywhere():
    return pl.BlockSpec(memory_space=pl.ANY)


def smem():
    return pl.BlockSpec(memory_space=pltpu.SMEM)


def params(mebibytes=56):
    return pltpu.CompilerParams(vmem_limit_bytes=mebibytes << 20)


def cost(flops, bytes_accessed):
    return pl.CostEstimate(flops=flops, bytes_accessed=bytes_accessed, transcendentals=0)


def project_kernel(*refs, blocks, chunks):
    attended, residuals = refs[:blocks], refs[blocks : 2 * blocks]
    own_ref, pair_ref, gain_ref = refs[2 * blocks : 2 * blocks + 3]
    outs = refs[2 * blocks + 3 :]
    cols = own_ref.shape[1]
    tokens = residuals[0].shape[0]
    rows = jnp.concatenate([ref[...] for ref in attended], axis=0)
    square = None
    for side, weight_ref in enumerate((own_ref, pair_ref)):
        at = side * cols
        stream = dot(rows, weight_ref[...])
        stream += jnp.concatenate([ref[:, at : at + cols] for ref in residuals], axis=0).astype(F32)
        scaled = (stream * gain_ref[:, at : at + cols]).astype(BF16)
        for out_ref, (start, size) in zip(outs, chunks):
            out_ref[: blocks * tokens, side * size : (side + 1) * size] = scaled[
                :, start : start + size
            ]
        for lane in range(0, cols, 128):
            piece = stream[:, lane : lane + 128]
            square = piece * piece if square is None else square + piece * piece
    square = jnp.sum(square.T, axis=0, keepdims=True)
    square = jnp.concatenate(
        [square[:, i * tokens : (i + 1) * tokens] for i in range(blocks)], axis=0
    )
    high = square.astype(BF16).astype(F32)
    rest = jnp.zeros((16 - 2 * blocks, tokens), F32)
    outs[0][blocks * tokens :, :] = jnp.zeros((16, outs[0].shape[1]), BF16)
    outs[0][blocks * tokens :, :tokens] = jnp.concatenate(
        [high, square - high, rest], axis=0
    ).astype(BF16)


def project(attended, residuals, own_weight, pair_weight, gain, chunks):
    blocks = len(attended)
    tokens, width = attended[0].shape
    cols = own_weight.shape[1]
    rows = blocks * tokens
    return pl.pallas_call(
        lambda *refs: project_kernel(*refs, blocks=blocks, chunks=chunks),
        in_specs=[vmem()] * (2 * blocks + 3),
        out_specs=[vmem()] * len(chunks),
        out_shape=[
            jax.ShapeDtypeStruct((rows + (0 if number else 16), 2 * size), BF16)
            for number, (_, size) in enumerate(chunks)
        ],
        compiler_params=params(),
        cost_estimate=cost(4 * rows * width * cols, 4 * width * cols),
        name="project",
    )(*attended, *residuals, own_weight, pair_weight, gain.reshape(1, 2 * cols))


def all_hits(slot_ref, capacity):
    groups, near = slot_ref.shape
    places = lax.broadcasted_iota(jnp.int32, (capacity, near), 0)
    return jnp.concatenate(
        [places == slot_ref[group : group + 1, :] for group in range(groups)], axis=0
    )


def pick_kernel(column_ref, slot_ref, *refs, count, width, first):
    blocks = refs[:count]
    out_ref = refs[-2] if first else refs[-1]
    groups, capacity, cols = out_ref.shape
    near = slot_ref.shape[1]
    tokens = near // count
    half = cols // count
    hits = all_hits(slot_ref, capacity)
    if first:
        inverses = []
        for b in range(count):
            total = jnp.zeros((1, tokens), F32)
            for r in range(b % 2, count, 2):
                table = blocks[r][count // 2 * tokens :, :tokens].astype(F32)
                row = (r ^ b) // 2
                total += table[row : row + 1] + table[count // 2 + row : count // 2 + row + 1]
            inverses.append(lax.rsqrt(total / width + norm_eps))
        inverse = jnp.concatenate(inverses, axis=1)
        refs[-1][...] = inverse
    else:
        inverse = refs[count][...]
    factors = jnp.sum(jnp.where(hits, inverse, 0.0), axis=1, keepdims=True)
    rows = []
    for c in range(count):
        pieces = []
        for b in range(count):
            r = (c // 2) * 2 + b % 2
            q = (r ^ b) // 2
            at = 0 if c == r else half
            pieces.append(blocks[r][q * tokens : (q + 1) * tokens, at : at + half])
        rows.append(jnp.concatenate(pieces, axis=0))
    picked = dot(hits.astype(BF16), jnp.concatenate(rows, axis=1))
    picked = (picked * factors).astype(BF16).reshape(groups, capacity, cols)
    for c in range(count):
        at = pl.multiple_of((column_ref[0] ^ c) * half, 128)
        out_ref[:, :, pl.ds(at, half)] = picked[:, :, c * half : (c + 1) * half]


def pick(column, slots, blocks, capacity, width, inverse=None, earlier=()):
    groups, near = slots.shape
    count = len(blocks)
    first = inverse is None
    cols = blocks[0].shape[1] * count // 2
    out_specs = [vmem()]
    out_shape = [jax.ShapeDtypeStruct((groups, capacity, cols), BF16)]
    if first:
        out_specs.append(vmem())
        out_shape.append(jax.ShapeDtypeStruct((1, near), F32))
    more = () if first else (inverse,)
    made = pl.pallas_call(
        lambda *refs: pick_kernel(
            *refs[: 2 + count + len(more)],
            *refs[2 + count + len(more) + len(earlier) :],
            count=count,
            width=width,
            first=first,
        ),
        in_specs=[smem()]
        + [vmem()] * (1 + len(blocks) + len(more))
        + [anywhere()] * len(earlier),
        out_specs=out_specs,
        out_shape=out_shape,
        compiler_params=params(),
        cost_estimate=cost(2 * groups * capacity * near * cols, 2 * groups * capacity * cols),
        name="pick",
    )(column.reshape(1), slots, *blocks, *more, *earlier)
    return made if first else (made[0], inverse)


def joined(refs):
    return jnp.concatenate(
        [jnp.concatenate([ref[...] for ref in part], axis=0) for part in refs], axis=1
    )


def split(refs, parts):
    count = len(refs) // parts
    return [refs[i * count : (i + 1) * count] for i in range(parts)]


def fill_kernel(slot_ref, *refs, parts):
    out_ref = refs[-1]
    hits = all_hits(slot_ref, out_ref.shape[0] // slot_ref.shape[0]).astype(BF16)
    for number, blocks in enumerate(split(refs[:-1], parts)):
        cols = blocks[0].shape[1]
        rows = jnp.concatenate([ref[...] for ref in blocks], axis=0)
        out_ref[:, number * cols : (number + 1) * cols] = dot(hits, rows).astype(BF16)


def fill(slots, upstream, capacity, earlier):
    groups, near = slots.shape
    blocks = [x for part in upstream for x in part]
    rows, cols = groups * capacity, sum(part[0].shape[1] for part in upstream)
    return pl.pallas_call(
        lambda *refs: fill_kernel(*refs[: 1 + len(blocks)], refs[-1], parts=len(upstream)),
        in_specs=[vmem()] * (1 + len(blocks)) + [anywhere()],
        out_specs=vmem(),
        out_shape=jax.ShapeDtypeStruct((rows, cols), BF16),
        compiler_params=params(),
        cost_estimate=cost(2 * rows * near * cols, 2 * rows * cols),
        name="fill",
    )(slots, *blocks, earlier)


def back_kernel(slot_ref, gate_ref, factor_ref, *refs, parts, capacity):
    out_ref = refs[-1]
    rows = joined(split(refs[:-1], parts))
    groups, rank, _ = out_ref.shape
    made = dot_t(factor_ref[...], rows)
    hits = all_hits(slot_ref, capacity).astype(BF16)
    out_ref[...] = jnp.zeros(out_ref.shape, BF16)
    for group in range(groups):
        mine = made[group * rank : (group + 1) * rank] * gate_ref[group : group + 1, :]
        slots = hits[group * capacity : (group + 1) * capacity]
        out_ref[group, :, :capacity] = dot_t(mine.astype(BF16), slots).astype(BF16)


def back_slots_of(slots, gates, factors, upstream, capacity, earlier):
    groups, near = slots.shape
    blocks = [x for part in upstream for x in part]
    rank = factors.shape[0] // groups
    return pl.pallas_call(
        lambda *refs: back_kernel(
            *refs[: 3 + len(blocks)], refs[-1], parts=len(upstream), capacity=capacity
        ),
        in_specs=[vmem()] * (3 + len(blocks)) + [anywhere()],
        out_specs=vmem(),
        out_shape=jax.ShapeDtypeStruct((groups, rank, capacity + -capacity % 128), BF16),
        compiler_params=params(),
        cost_estimate=cost(2 * near * factors.size, 4 * factors.size),
        name="back_low",
    )(slots, gates, factors, *blocks, earlier)


def gradient_kernel(low_ref, weight_ref, back_ref, *refs, parts, rank):
    out_ref = refs[-1]
    groups, capacity, _ = low_ref.shape
    rows = joined(split(refs[:-1], parts))
    width = rows.shape[1]
    low = low_ref[...].reshape(groups * capacity, low_ref.shape[2]).astype(F32).T[:rank]
    low = jnp.concatenate([low] * groups, axis=0)
    group = lax.broadcasted_iota(jnp.int32, low.shape, 0) // rank
    place = lax.broadcasted_iota(jnp.int32, low.shape, 1) - group * capacity
    low = jnp.where((place >= 0) & (place < capacity), low, 0.0).astype(BF16)
    weighted = dot_t(low, weight_ref[...]).astype(BF16)
    made = dot(weighted, rows).astype(BF16)
    out_ref[:, :, :width] = made.reshape(groups, rank, width)
    out_ref[:, :, width:] = back_ref[...]


def gradient_parts(back, at, weights, back_slots, upstream):
    groups, capacity, _ = back.shape
    near = weights.shape[0]
    rank, wide = back_slots.shape[1:]
    blocks = [x for part in upstream for x in part]
    width = sum(part[0].shape[1] for part in upstream)

    def whole(x):
        return pl.BlockSpec(x.shape, lambda i: (0,) * x.ndim)

    return pl.pallas_call(
        lambda *refs: gradient_kernel(*refs, parts=len(upstream), rank=rank),
        grid=(1,),
        in_specs=[
            pl.BlockSpec((groups, capacity, 128), lambda i: (0, 0, at // 128)),
            whole(weights),
            whole(back_slots),
        ]
        + [whole(x) for x in blocks],
        out_specs=pl.BlockSpec((groups, rank, width + wide), lambda i: (0, 0, 0)),
        out_shape=jax.ShapeDtypeStruct((groups, rank, width + wide), BF16),
        compiler_params=params(),
        cost_estimate=cost(2 * near * groups * rank * (width + groups * capacity), 4 * near * width),
        name="gradient",
    )(back, weights, back_slots, *blocks)


def half_kernel(rows_ref, gate_ref, up_ref, *refs):
    out_gate, out_up = refs[-2:]
    rows = rows_ref[...]
    rows = rows.reshape(rows.shape[0] * rows.shape[1], rows.shape[2])
    gate_weight, up_weight = gate_ref[...], up_ref[...]
    shape = (rows.shape[1], gate_weight.shape[2])
    gate, up = dot(rows, gate_weight.reshape(shape)), dot(rows, up_weight.reshape(shape))
    if len(refs) == 4:
        gate, up = gate + refs[0][...], up + refs[1][...]
    out_gate[...] = gate
    out_up[...] = up


def last_kernel(rows_ref, gate_ref, up_ref, gate_in, up_in, factor_ref, out_active, out_low):
    rows = rows_ref[...]
    rows = rows.reshape(rows.shape[0] * rows.shape[1], rows.shape[2])
    gate_weight, up_weight = gate_ref[...], up_ref[...]
    shape = (rows.shape[1], gate_weight.shape[2])
    gate = dot(rows, gate_weight.reshape(shape)) + gate_in[...]
    up = dot(rows, up_weight.reshape(shape)) + up_in[...]
    active = (gate / (1.0 + jnp.exp(-gate)) * up).astype(BF16)
    out_active[...] = active
    out_low[...] = dot(active, factor_ref[...]).astype(BF16)


def hidden_units(rows, at, gate_weight, up_weight, so_far, factor, earlier=()):
    groups, capacity, cols = rows.shape
    blocks, _, units = gate_weight.shape
    together = max(1, groups // 4)
    step = together * capacity
    part = cols // blocks
    weight = pl.BlockSpec((blocks, part, units), lambda i: (0, at // part, 0))
    sums = pl.BlockSpec((step, units), lambda i: (i, 0))
    in_specs = [pl.BlockSpec((together, capacity, cols), lambda i: (i, 0, 0)), weight, weight]
    in_specs += [sums] * len(so_far)
    more = ()
    if factor is None:
        out_specs = [sums, sums]
        out_shape = [jax.ShapeDtypeStruct((groups * capacity, units), F32)] * 2
    else:
        more = (factor,)
        rank = factor.shape[1]
        in_specs.append(pl.BlockSpec(factor.shape, lambda i: (0, 0)))
        out_specs = [sums, pl.BlockSpec((step, rank), lambda i: (i, 0))]
        out_shape = [
            jax.ShapeDtypeStruct((groups * capacity, units), BF16),
            jax.ShapeDtypeStruct((groups * capacity, rank), BF16),
        ]
    count = 3 + len(so_far) + len(more)
    in_specs += [anywhere()] * len(earlier)
    body = half_kernel if factor is None else last_kernel
    return pl.pallas_call(
        lambda *refs: body(*refs[:count], *refs[count + len(earlier) :]),
        grid=(groups // together,),
        in_specs=in_specs,
        out_specs=out_specs,
        out_shape=out_shape,
        compiler_params=params(),
        cost_estimate=cost(
            4 * groups * capacity * cols * units, 4 * cols * units + 16 * groups * capacity * units
        ),
        name="units",
    )(rows, gate_weight, up_weight, *so_far, *more, *earlier)


def down_kernel(active_ref, low_ref, down_ref, up_ref, out_ref, *, cols):
    low = low_ref[...]
    rows = dot(active_ref[...], down_ref[...]) + adapter_scale * dot(low, up_ref[...])
    together, capacity, wide = out_ref.shape
    out_ref[:, :, :cols] = rows.astype(BF16).reshape(together, capacity, cols)
    if wide > cols:
        out_ref[:, :, cols:] = jnp.zeros((together, capacity, wide - cols), BF16)
        out_ref[:, :, cols : cols + low.shape[1]] = low.reshape(together, capacity, low.shape[1])


def down(active, low, groups, at, cols, extra, down_weight, up_factor, earlier=()):
    rows, units = active.shape
    capacity = rows // groups
    rank = low.shape[1]
    together = max(1, groups // 4)
    step = together * capacity
    return pl.pallas_call(
        lambda *refs: down_kernel(*refs[:4], refs[-1], cols=cols),
        grid=(groups // together,),
        in_specs=[
            pl.BlockSpec((step, units), lambda i: (i, 0)),
            pl.BlockSpec((step, rank), lambda i: (i, 0)),
            pl.BlockSpec((units, cols), lambda i: (0, at // cols)),
            pl.BlockSpec((rank, cols), lambda i: (0, at // cols)),
        ]
        + [anywhere()] * len(earlier),
        out_specs=pl.BlockSpec((together, capacity, cols + extra), lambda i: (i, 0, 0)),
        out_shape=jax.ShapeDtypeStruct((groups, capacity, cols + extra), BF16),
        compiler_params=params(),
        cost_estimate=cost(2 * rows * cols * units, 2 * cols * (units + rows)),
        name="down",
    )(active, low, down_weight, up_factor, *earlier)


def combine_kernel(back_ref, weight_ref, upstream_ref, *refs, cols, blocks, last, first):
    groups, capacity, _ = back_ref.shape
    back = back_ref[:, :, :cols].reshape(groups * capacity, cols)
    dots = jnp.sum(back.astype(F32) * upstream_ref[...].astype(F32), axis=1, keepdims=True)
    if not first:
        dots += refs[0][...]
    outs = refs[-blocks:] if last else refs[-blocks - 1 : -1]
    total = dot(weight_ref[...], back).astype(BF16)
    near = total.shape[0]
    tokens = near // blocks
    for block in range(blocks):
        outs[block][:, :cols] = total[block * tokens : (block + 1) * tokens]
    if not last:
        refs[-1][...] = dots
        return
    slot_ref = refs[1]
    places = lax.broadcasted_iota(jnp.int32, (capacity, near), 0)
    found = []
    for group in range(groups):
        mine = dots[group * capacity : (group + 1) * capacity]
        hits = places == slot_ref[group : group + 1, :]
        found.append(jnp.sum(jnp.where(hits, mine, 0.0), axis=0, keepdims=True))
    found = jnp.concatenate(found, axis=0)
    high = found.astype(BF16).astype(F32)
    rest = jnp.zeros((128 - 2 * groups, near), F32)
    table = jnp.concatenate([high, found - high, rest], axis=0).T.astype(BF16)
    for block in range(blocks):
        outs[block][:, cols:] = table[block * tokens : (block + 1) * tokens]


def combine(back, at, cols, weights, upstream, dots, slots, blocks, last, earlier):
    groups, capacity, wide = back.shape
    near = weights.shape[0]
    tokens = near // blocks
    out_shape = [jax.ShapeDtypeStruct((tokens, cols + (128 if last else 0)), BF16)] * blocks
    if not last:
        out_shape.append(jax.ShapeDtypeStruct((groups * capacity, 1), F32))

    def whole(shape):
        return pl.BlockSpec(shape, lambda i: (0,) * len(shape))

    first = dots is None
    more = () if first else ((dots, slots) if last else (dots,))
    return pl.pallas_call(
        lambda *refs: combine_kernel(
            *refs[: 3 + len(more)],
            *refs[3 + len(more) + len(earlier) :],
            cols=cols,
            blocks=blocks,
            last=last,
            first=first,
        ),
        grid=(1,),
        in_specs=[
            whole(back.shape),
            whole(weights.shape),
            pl.BlockSpec((groups * capacity, cols), lambda i: (0, at // cols)),
        ]
        + [whole(x.shape) for x in more]
        + [anywhere()] * len(earlier),
        out_specs=[whole(s.shape) for s in out_shape],
        out_shape=out_shape,
        compiler_params=params(),
        cost_estimate=cost(
            2 * groups * capacity * near * cols, 2 * cols * (groups * capacity + near)
        ),
        name="combine",
    )(back, weights, upstream, *more, *earlier)


def exchange(xs, axis):
    size = lax.axis_size(axis)
    return [xs[0]] + [
        lax.ppermute(xs[r], axis, [(i, i ^ r) for i in range(size)]) for r in range(1, size)
    ]


def across(x, axis):
    return exchange([x] * lax.axis_size(axis), axis)


def from_plane(x, r):
    size = lax.axis_size("expert")
    return lax.ppermute(x, "expert", [(i, i ^ r) for i in range(size)])


def columns_of(x, r, size):
    return lax.dynamic_slice_in_dim(x, (lax.axis_index("expert") ^ r) * size, size, 1)


def swap(x):
    return lax.all_to_all(x, "seq", split_axis=0, concat_axis=0, tiled=True)


def spread(x):
    count = lax.axis_size("seq")
    return swap(jnp.broadcast_to(x[None], (count,) + x.shape)).reshape(-1, x.shape[-1])


def after(x, *earlier):
    return pl.pallas_call(
        lambda *refs: None,
        in_specs=[anywhere()] * (1 + len(earlier)),
        out_specs=anywhere(),
        out_shape=jax.ShapeDtypeStruct(x.shape, x.dtype),
        input_output_aliases={0: 0},
        name="after",
    )(x, *earlier)


def finish_kernel(*refs, sizes, blocks, groups):
    parts = len(sizes) * blocks
    pieces = refs[:parts]
    probs_ref, ids_ref, names_ref, out_ref, grad_ref = refs[parts:]
    at = 0
    for number, size in enumerate(sizes):
        mine = pieces[number * blocks : (number + 1) * blocks]
        total = mine[0][:, :size].astype(F32)
        for ref in mine[1:]:
            total += ref[:, :size].astype(F32)
        out_ref[:, at : at + size] = total.astype(BF16)
        at += size
    dots = []
    for ref in pieces[-blocks:]:
        table = ref[:, sizes[-1] :].astype(F32)
        dots.append(table[:, :groups] + table[:, groups : 2 * groups])
    dots = jnp.concatenate(dots, axis=1)
    probs, ids, names = probs_ref[...], ids_ref[...], names_ref[...]
    picked = [
        jnp.sum(jnp.where(ids[:, k : k + 1] == names, dots, 0.0), axis=1, keepdims=True)
        for k in range(ids.shape[1])
    ]
    picked = jnp.concatenate(picked, axis=1)
    grad = probs * (picked - jnp.sum(probs * picked, axis=1, keepdims=True))
    rest = jnp.zeros((grad.shape[0], 128 - grad.shape[1]), F32)
    grad_ref[...] = jnp.concatenate([grad, rest], axis=1).T[: grad.shape[1]]


def finish(home, sizes, probs, ids, names, groups):
    tokens = probs.shape[0]
    blocks = len(home[0])
    return pl.pallas_call(
        lambda *refs: finish_kernel(*refs, sizes=sizes, blocks=blocks, groups=groups),
        in_specs=[vmem()] * (blocks * len(sizes) + 3),
        out_specs=[vmem()] * 2,
        out_shape=[
            jax.ShapeDtypeStruct((tokens, sum(sizes)), BF16),
            jax.ShapeDtypeStruct(probs.shape[::-1], F32),
        ],
        compiler_params=params(),
        name="finish",
    )(*[x for pieces in home for x in pieces], probs, ids, names)


def shards(
    queries,
    keys,
    values,
    document_index,
    residual,
    output_projection,
    norm_gain_weight,
    routed_experts,
    router_logits,
    gate_weight,
    up_weight,
    down_weight,
    adapter_down,
    adapter_up,
    cotangent,
):
    seq_devices = lax.axis_size("seq")
    columns = lax.axis_size("expert")
    column = lax.axis_index("expert")
    place = lax.axis_index("seq")
    tokens = queries.shape[1]
    width = queries.shape[2]
    experts = seq_devices * columns
    rank = adapter_up.shape[1]
    near = columns * tokens
    block = width // columns

    kv_own = jnp.concatenate([keys[0], values[0]], axis=1)
    kv_all = spread(kv_own)
    share = output_projection.shape[0] // seq_devices
    pair_share = after(
        lax.dynamic_slice_in_dim(output_projection, place * share, share, 0), kv_own
    )
    pair_share = from_plane(pair_share, 1)
    router_logits = after(router_logits, kv_own)
    gate_probs = jax.nn.softmax(router_logits[0], axis=-1)
    routing = across(
        jnp.concatenate([gate_probs, routed_experts[0].astype(F32)], axis=1),
        "expert",
    )
    residuals = [
        jnp.concatenate([columns_of(residual[0], r, block), columns_of(residual[0], r + 1, block)], 1)
        for r in range(0, columns, 2)
    ]
    residuals = [residuals[0]] + [
        from_plane(after(residuals[r // 2], kv_own), r) for r in range(2, columns, 2)
    ]
    pair_projection = spread(after(pair_share, *residuals[1:], *routing[1:]))
    up_factors = spread(after(adapter_up[0], pair_projection))

    attended = attend(queries[0], kv_all, document_index[0], ())
    attended = [attended] + [from_plane(attended, r) for r in range(2, columns, 2)]

    capacity = columns * (9 * tokens * PICKS_PER_TOKEN // (8 * experts))
    capacity = -(-capacity // 16) * 16
    routing = jnp.concatenate(routing, axis=0)
    near_probs = routing[:, :PICKS_PER_TOKEN]
    near_picks = routing[:, PICKS_PER_TOKEN:].astype(jnp.int32)
    plane_experts = jnp.arange(seq_devices) * columns + column
    hits = near_picks[:, :, None] == plane_experts[None, None, :]
    member = jnp.any(hits, axis=1)
    gates = jnp.sum(jnp.where(hits, near_probs[:, :, None], 0.0), axis=1)
    inner = jnp.arange(near)
    lower = (inner[None, :] < inner[:, None]).astype(BF16)
    ranks = dot(lower, member.astype(BF16)).astype(jnp.int32)
    slot_rows = jnp.where(member, ranks, capacity)
    slots = slot_rows.T
    numbers = jnp.arange(seq_devices * capacity)
    named = jnp.where(member, ranks + jnp.arange(seq_devices)[None, :] * capacity, -1)
    weights = jnp.sum(
        jnp.where(named[:, None, :] == numbers[None, :, None], gates[:, None, :], 0.0), axis=2
    ).astype(BF16)

    chunks = [(0, block // 2), (block // 2, block // 2)]
    gain = norm_gain_weight[None]
    scaled = project(
        attended,
        residuals,
        output_projection,
        pair_projection,
        jnp.concatenate([columns_of(gain, 0, block), columns_of(gain, 1, block)], 1),
        chunks,
    )
    rows, crossed = [], []
    inverse = None
    for number, piece in enumerate(scaled):
        blocks = across(piece, "expert")
        crossed.append(blocks)
        earlier = (up_factors, weights) if number == 0 else ()
        picked, inverse = pick(column, slots, blocks, capacity, width, inverse, earlier)
        rows.append(swap(picked))
    half = width // 2
    upstream = [across(after(cotangent[0, :, :half], *crossed[-1][1:]), "expert")]
    so_far = ()
    for number, (at, cols) in enumerate(chunks):
        last = number == len(chunks) - 1
        so_far = hidden_units(
            rows[number],
            at,
            gate_weight[0].reshape(columns, block, -1),
            up_weight[0].reshape(columns, block, -1),
            so_far,
            adapter_down[0] if last else None,
            tuple(upstream[0][1:]) if last else (),
        )
    active, low_rank = so_far
    upstream.append(across(after(cotangent[0, :, half:], *upstream[0][1:]), "expert"))

    chunks = ((0, half), (half, half))
    adapters = (down_weight[0], adapter_up[0])
    outputs = [down(active, low_rank, seq_devices, 0, half, 128, *adapters)]
    upstream_slots = fill(slots, upstream, capacity, outputs[0])
    back_slots = back_slots_of(slots, gates.T, up_factors, upstream, capacity, outputs[0])
    dots, home, backs = None, [], []
    for number, (at, cols) in enumerate(chunks):
        if number > 0:
            earlier = (outputs[0],)
            outputs.append(down(active, low_rank, seq_devices, at, cols, 0, *adapters, earlier))
        backs.append(swap(after(outputs[number], upstream_slots) if number else outputs[0]))
        last = number == len(chunks) - 1
        *sums, more = combine(
            backs[-1],
            at,
            cols,
            weights,
            upstream_slots,
            dots,
            slots,
            columns,
            last,
            home[-1][1:] if home else [weights],
        )
        if last:
            sums.append(more)
        else:
            dots = more
        home.append(exchange(sums, "expert"))

    parts = gradient_parts(backs[0], half, weights, back_slots, upstream)
    parts = swap(after(parts, home[-1][0]))
    up_factor_gradient = adapter_scale * jnp.sum(parts[:, :, :width].astype(F32), axis=0)
    down_factor_gradient = adapter_scale * jnp.einsum(
        "jcf,jrc->fr",
        active.reshape(seq_devices, capacity, -1),
        parts[:, :, width : width + capacity],
        preferred_element_type=F32,
    )

    names = (
        jnp.arange(seq_devices)[None, :] * columns
        + (column ^ jnp.arange(columns, dtype=jnp.int32))[:, None]
    )
    combined_output, router_logit_gradient = finish(
        home,
        [cols for _, cols in chunks],
        gate_probs,
        routed_experts[0],
        names.reshape(1, experts),
        seq_devices,
    )
    return (
        combined_output[None],
        down_factor_gradient[None],
        up_factor_gradient[None],
        router_logit_gradient.T[None],
    )


def solution(mesh):
    return jax.shard_map(
        shards,
        mesh=mesh,
        in_specs=(
            P(("groups", "expert"), "seq", None),
            P(("groups", "expert"), "seq", None),
            P(("groups", "expert"), "seq", None),
            P(("groups", "expert"), None),
            P(("groups", "expert"), "seq", None),
            P(None, "expert"),
            P(),
            P(("groups", "expert"), "seq", None),
            P(("groups", "expert"), "seq", None),
            P(("seq", "expert"), None, None),
            P(("seq", "expert"), None, None),
            P(("seq", "expert"), None, None),
            P(("seq", "expert"), None, None),
            P(("seq", "expert"), None, None),
            P(("groups", "expert"), "seq", None),
        ),
        out_specs=(
            P(("groups", "expert"), "seq", None),
            P(("groups", "seq", "expert"), None, None),
            P(("groups", "seq", "expert"), None, None),
            P(("groups", "expert"), "seq", None),
        ),
        check_vma=False,
    )
```

time: 477 us -> 323 us (0.68)
  waiting for transfers between devices: 341 us -> 123 us
  Pallas kernels: 3.4 us -> 77.6 us
  matrix products: 56.5 us -> 1.92 us
  starting transfers between devices: 16.5 us -> 69.8 us
  blocking collectives: 22.3 us -> 0 us
  local copies, waits for them, and re-layouts: 12.5 us -> 29.7 us
  between operations: 14.4 us -> 1.08 us
  other arithmetic: 9.25 us -> 15.9 us
    all_gather x5 -> x0, waiting for transfers between devices: 197 us -> none  [the longest x1 145 us: shards(): projection = lax.all_gather(output_projection, 'expert', axis=0)]
    ppermute x0 -> x24, waiting for transfers between devices: none -> 94.1 us  [the longest x21 89.9 us: exchange(): lax.ppermute(xs[r], axis, [(i, i ^ r) for i in range(size)])]
    all_to_all x4 -> x8, waiting for transfers between devices: 112 us -> 29 us  [swap(): return lax.all_to_all(x, 'seq', split_axis=0, concat_axis=0, tiled=True)]
    pallas_call x0 -> x22, Pallas kernels: none -> 71.9 us  [the longest x2 16.8 us: hidden_units(): pl.pallas_call(lambda *refs: body(*refs[:count], *refs[count + len(earlie...]
    ppermute x0 -> x24, starting transfers between devices: none -> 39.1 us  [the longest x21 32.5 us: exchange(): lax.ppermute(xs[r], axis, [(i, i ^ r) for i in range(size)])]
    dot_general x9 -> x1, matrix products: 39.4 us -> 0.86 us  [dot(): return jnp.dot(a, b, preferred_element_type=F32)]
    reduce_scatter x2 -> x0, waiting for transfers between devices: 30.3 us -> none  [the longest x1 30.3 us: shards(): lax.psum_scatter(combined.astype(BF16), 'expert', scatter_dimension=0, ti...]
    dot_general x6 -> x1, matrix products: 17.1 us -> 1.06 us  [shards(): jnp.einsum('jcf,jrc->fr', active.reshape(seq_devices, capacity, -1), part...]
  transfers between devices with their start and end apart: 11 -> 32, of which waited for: 7 -> 16; matrix products, arithmetic and copies ran while one was open for 11% -> 8% of each run, Pallas kernels for 1% -> 16%
where the time goes in v2:
time: 323 us; the launch traced here: 319 us
  waiting for transfers between devices  123 us (38%)
  Pallas kernels  77.6 us (24%)
  starting transfers between devices  69.8 us (22%)
  local copies, waits for them, and re-layouts  29.7 us (9%)
  other arithmetic  15.9 us (5%)
    ppermute x21, waiting for transfers between devices, exchange(): lax.ppermute(xs[r], axis, [(i, i ^ r) for i in range(size)])  89.9 us
    ppermute x21, starting transfers between devices, exchange(): lax.ppermute(xs[r], axis, [(i, i ^ r) for i in range(size)])  32.5 us
    all_to_all x8, starting transfers between devices, swap(): return lax.all_to_all(x, 'seq', split_axis=0, concat_axis=0, tiled=True)  30.7 us
    all_to_all x8, waiting for transfers between devices, swap(): return lax.all_to_all(x, 'seq', split_axis=0, concat_axis=0, tiled=True)  29 us
    pallas_call x2, Pallas kernels, hidden_units(): pl.pallas_call(lambda *refs: body(*refs[:count], *refs[count + len(earlie...  16.8 us
    unnamed x96, local copies, waits for them, and re-layouts  15.3 us
    pallas_call x2, Pallas kernels, down(): pl.pallas_call(lambda *refs: down_kernel(*refs[:4], refs[-1], cols=cols),...  12.1 us
    pallas_call x2, Pallas kernels, combine(): pl.pallas_call(lambda *refs: combine_kernel(*refs[:3 + len(more)], *refs[...  11.5 us
  transfers between devices with their start and end apart: 32, of which 16 were waited for; matrix products, arithmetic and copies ran while one was open for 8% of the time, Pallas kernels for 16%

profile of v2, /device:TPU:0, one launch (start us, length us, event | category | flops | bytes accessed | tf_op | source)
XLA Modules:
  0.0 319.0 jit_solution(6081336630129908574)
XLA Ops:
  3.9 3.0 collective-permute-start.5
  8.9 3.9 %all-to-all-start = ((bf16[8,128,512]{2,1,0:T(8,128)(2,1)}), bf16[8,128,512]{2,1,0:T(8,128)(2,1)S(1)}, u32[]{:S(2)}, u32[]{:S(2)}) async-start(bf16[8,128,512]{2,1,0:T(8,128)(2,1)} %broadcast_in_dim.52), calls=%async_computation | async-start | bytes 2097152 | tf_op jit(solution)/shard_map/all_to_all | solution.py:535
  14.3 2.6 collective-permute-start.4
  22.8 2.5 collective-permute-start
  25.2 2.4 collective-permute-done.2.refs_4_
  27.7 7.6 %collective-permute-done.1.refs_3_ = f32[128,16]{1,0:T(8,128)S(1)} collective-permute-done((f32[128,16]{1,0:T(8,128)S(1)}, f32[128,16]{1,0:T(8,128)S(1)}, u32[]{:S(2)}, u32[]{:S(2)}) %collective-permute-start.1) | collective-permute-done | bytes 8224 | tf_op jit(solution)/shard_map/ppermute | solution.py:517
  36.7 2.6 broadcast_in_dim.55
  39.4 4.0 %all-to-all-start.1 = ((bf16[8,256,512]{2,1,0:T(8,128)(2,1)}), bf16[8,256,512]{2,1,0:T(8,128)(2,1)S(1)}, u32[]{:S(2)}, u32[]{:S(2)}) async-start(bf16[8,256,512]{2,1,0:T(8,128)(2,1)} %broadcast_in_dim.55), calls=%async_computation.1 | async-start | bytes 4194304 | tf_op jit(solution)/shard_map/all_to_all | solution.py:535
  50.0 5.7 %attend.1.refs_0_ = bf16[128,2048]{1,0:T(8,128)(2,1)} custom-call(s32[1]{0:T(128)} %bitcast.6.start_ref, bf16[128,2048]{1,0:T(8,128)(2,1)} %bitcast.76, bf16[1024,512]{1,0:T(8,128)(2,1)} %bitcast.64, f32[128,640]{1,0:T(8,128)} %and_select_fusion.bias_ref), custom_call_target="tpu_custom_call" | custom-call | tf_op jit(solution)/shard_map/attend/pallas_call | solution.py:73
  56.8 13.2 %all-to-all-done.1 = bf16[8,256,512]{2,1,0:T(8,128)(2,1)S(1)} async-done(((bf16[8,256,512]{2,1,0:T(8,128)(2,1)}), bf16[8,256,512]{2,1,0:T(8,128)(2,1)S(1)}, u32[]{:S(2)}, u32[]{:S(2)}) %all-to-all-start.1) | async-done | bytes 2097184 | tf_op jit(solution)/shard_map/all_to_all | solution.py:535
  71.3 2.0 broadcast_in_dim.90
  73.3 3.6 %all-to-all-start.2 = ((bf16[8,32,2048]{2,1,0:T(8,128)(2,1)}), bf16[8,32,2048]{2,1,0:T(8,128)(2,1)S(1)}, u32[]{:S(2)}, u32[]{:S(2)}) async-start(bf16[8,32,2048]{2,1,0:T(8,128)(2,1)} %broadcast_in_dim.90), calls=%async_computation.2 | async-start | bytes 2097152 | tf_op jit(solution)/shard_map/all_to_all | solution.py:535
  78.1 4.2 %collective-permute-done.3.refs_1_ = bf16[128,2048]{1,0:T(8,128)(2,1)S(1)} collective-permute-done((bf16[128,2048]{1,0:T(8,128)(2,1)}, bf16[128,2048]{1,0:T(8,128)(2,1)S(1)}, u32[]{:S(2)}, u32[]{:S(2)}) %collective-permute-start.3) | collective-permute-done | bytes 524320 | tf_op jit(solution)/shard_map/ppermute | solution.py:527
  83.1 4.9 %project.1 = (bf16[272,512]{1,0:T(8,128)(2,1)}, bf16[256,512]{1,0:T(8,128)(2,1)}) custom-call(bf16[128,2048]{1,0:T(8,128)(2,1)} %attend.1.refs_0_, bf16[128,2048]{1,0:T(8,128)(2,1)} %copy-done.23, bf16[128,1024]{1,0:T(8,128)(2,1)} %pad_maximum_fusion.refs_2_, bf16[128,1024]{1,0:T(8,128)(2,1)} %copy-done.19, bf16[2048,512]{1,0:T(8,128)(2,1)} %refs_4_.1, ...), custom_call_target="tpu_custom_call" | custom-call | flops 1073741824 | bytes 4194304 | tf_op jit(solution)/shard_map/project/pallas_call | solution.py:146
  89.9 2.4 collective-permute-start.9
  92.4 7.3 %select_reduce_fusion.refs_7_.refs_1_.refs_3_ = bf16[512,1152]{1,0:T(8,128)(2,1)} fusion(f32[512,8]{1,0:T(8,128)S(1)} %copy.55, s32[512,8]{1,0:T(8,128)S(1)} %copy.54), kind=kLoop, calls=%fused_computation | loop fusion | flops 13565952 | bytes 1212416 | tf_op jit(solution)/shard_map/reduce_sum | solution.py:668
  99.6 13.8 %collective-permute-done.10.refs_4_ = bf16[272,512]{1,0:T(8,128)(2,1)S(1)} collective-permute-done((bf16[272,512]{1,0:T(8,128)(2,1)}, bf16[272,512]{1,0:T(8,128)(2,1)S(1)}, u32[]{:S(2)}, u32[]{:S(2)}) %collective-permute-start.10) | collective-permute-done | bytes 278560 | tf_op jit(solution)/shard_map/ppermute | solution.py:517
  114.6 4.3 %pick.2 = (bf16[8,144,1024]{2,1,0:T(8,128)(2,1)}, f32[1,512]{1,0:T(1,128)}) custom-call(s32[1]{0:T(128)} %bitcast.refs_0_, s32[8,512]{1,0:T(8,128)} %get-tuple-element.51.refs_1_.refs_0_.refs_4_, bf16[272,512]{1,0:T(8,128)(2,1)} %get-tuple-element.24.refs_2_, bf16[272,512]{1,0:T(8,128)(2,1)} %copy-done.44, bf16[272,512]{1,0:T(8,128)(2,1)} %copy-done.43, ...), custom_call_target="tpu_custom_call" | custom-call | flops 1207959552 | bytes 2359296 | tf_op jit(solution)/shard_map/pick/pallas_call | solution.py:217
  118.9 3.9 %all-to-all-start.4 = ((bf16[8,144,1024]{2,1,0:T(8,128)(2,1)}), bf16[8,144,1024]{2,1,0:T(8,128)(2,1)S(1)}, u32[]{:S(2)}, u32[]{:S(2)}) async-start(bf16[8,144,1024]{2,1,0:T(8,128)(2,1)} %get-tuple-element.26), calls=%async_computation.4 | async-start | bytes 4718592 | tf_op jit(solution)/shard_map/all_to_all | solution.py:535
  124.7 2.5 collective-permute-start.6
  127.3 6.7 %collective-permute-done.8.refs_5_.refs_3_ = bf16[256,512]{1,0:T(8,128)(2,1)S(1)} collective-permute-done((bf16[256,512]{1,0:T(8,128)(2,1)S(1)}, bf16[256,512]{1,0:T(8,128)(2,1)S(1)}, u32[]{:S(2)}, u32[]{:S(2)}) %collective-permute-start.8) | collective-permute-done | bytes 262176 | tf_op jit(solution)/shard_map/ppermute | solution.py:517
  133.9 13.0 %collective-permute-done.7.refs_4_.refs_2_ = bf16[256,512]{1,0:T(8,128)(2,1)S(1)} collective-permute-done((bf16[256,512]{1,0:T(8,128)(2,1)S(1)}, bf16[256,512]{1,0:T(8,128)(2,1)S(1)}, u32[]{:S(2)}, u32[]{:S(2)}) %collective-permute-start.7) | collective-permute-done | bytes 262176 | tf_op jit(solution)/shard_map/ppermute | solution.py:517
  147.8 4.3 %pick.3 = bf16[8,144,1024]{2,1,0:T(8,128)(2,1)} custom-call(s32[1]{0:T(128)} %bitcast.refs_0_, s32[8,512]{1,0:T(8,128)} %get-tuple-element.51.refs_1_.refs_0_.refs_4_, bf16[256,512]{1,0:T(8,128)(2,1)} %get-tuple-element.23.refs_2_, bf16[256,512]{1,0:T(8,128)(2,1)} %copy-done.32, bf16[256,512]{1,0:T(8,128)(2,1)} %copy-done.31, bf16[256,512]{1,0:T(8,128)(2,1)} %copy-done.30, ...), custom_call_target="tpu_custom_call" | custom-call | flops 1207959552 | bytes 2359296 | tf_op jit(solution)/shard_map/pick/pallas_call | solution.py:217
  153.7 3.8 %all-to-all-start.3 = ((bf16[8,144,1024]{2,1,0:T(8,128)(2,1)}), bf16[8,144,1024]{2,1,0:T(8,128)(2,1)S(1)}, u32[]{:S(2)}, u32[]{:S(2)}) async-start(bf16[8,144,1024]{2,1,0:T(8,128)(2,1)} %pick.3), calls=%async_computation.3 | async-start | bytes 4718592 | tf_op jit(solution)/shard_map/all_to_all | solution.py:535
  161.0 2.5 collective-permute-start.12
  163.5 7.7 %units.2 = (f32[1152,768]{1,0:T(8,128)}, f32[1152,768]{1,0:T(8,128)}) custom-call(bf16[8,144,1024]{2,1,0:T(8,128)(2,1)} %copy-done.14, bf16[4,512,768]{2,1,0:T(8,128)(2,1)} %bitcast.67, bf16[4,512,768]{2,1,0:T(8,128)(2,1)} %bitcast.69), custom_call_target="tpu_custom_call" | custom-call | flops 3623878656 | bytes 17301504 | tf_op jit(solution)/shard_map/units/pallas_call | solution.py:396
  171.3 12.1 %collective-permute-done.13.refs_7_.refs_2_.refs_3_.refs_5_ = bf16[128,1024]{1,0:T(8,128)(2,1)S(1)} collective-permute-done((bf16[128,1024]{1,0:T(8,128)(2,1)}, bf16[128,1024]{1,0:T(8,128)(2,1)S(1)}, u32[]{:S(2)}, u32[]{:S(2)}) %collective-permute-start.13) | collective-permute-done | bytes 262176 | tf_op jit(solution)/shard_map/ppermute | solution.py:517
  183.4 3.4 %all-to-all-done.3.refs_0_ = bf16[8,144,1024]{2,1,0:T(8,128)(2,1)S(1)} async-done(((bf16[8,144,1024]{2,1,0:T(8,128)(2,1)}), bf16[8,144,1024]{2,1,0:T(8,128)(2,1)S(1)}, u32[]{:S(2)}, u32[]{:S(2)}) %all-to-all-start.3) | async-done | bytes 2359328 | tf_op jit(solution)/shard_map/all_to_all | solution.py:535
  188.3 9.1 %units.3 = (bf16[1152,768]{1,0:T(8,128)(2,1)}, bf16[1152,32]{1,0:T(8,128)(2,1)}) custom-call(bf16[8,144,1024]{2,1,0:T(8,128)(2,1)} %copy-done.5, bf16[4,512,768]{2,1,0:T(8,128)(2,1)} %bitcast.68, bf16[4,512,768]{2,1,0:T(8,128)(2,1)} %bitcast.70, f32[1152,768]{1,0:T(8,128)} %get-tuple-element.27.refs_3_, f32[1152,768]{1,0:T(8,128)} %get-tuple-element.28.refs_4_, ...), custom_call_target="tpu_custom_call" | custom-call | flops 3623878656 | bytes 17301504 | tf_op jit(solution)/shard_map/units/pallas_call | solution.py:396
  197.4 6.1 %down.2.refs_9_.refs_4_.refs_11_ = bf16[8,144,1152]{2,1,0:T(8,128)(2,1)} custom-call(bf16[1152,768]{1,0:T(8,128)(2,1)} %get-tuple-element.29.refs_0_, bf16[1152,32]{1,0:T(8,128)(2,1)} %get-tuple-element.30.refs_1_, bf16[768,2048]{1,0:T(8,128)(2,1)} %bitcast.62, bf16[32,2048]{1,0:T(8,128)(2,1)} %bitcast.71), custom_call_target="tpu_custom_call" | custom-call | flops 1811939328 | bytes 3932160 | tf_op jit(solution)/shard_map/down/pallas_call | solution.py:426
  203.5 3.6 %all-to-all-start.5 = ((bf16[8,144,1152]{2,1,0:T(8,128)(2,1)}), bf16[8,144,1152]{2,1,0:T(8,128)(2,1)S(1)}, u32[]{:S(2)}, u32[]{:S(2)}) async-start(bf16[8,144,1152]{2,1,0:T(8,128)(2,1)} %down.2.refs_9_.refs_4_.refs_11_), calls=%async_computation.5 | async-start | bytes 5308416 | tf_op jit(solution)/shard_map/all_to_all | solution.py:535
  207.1 2.0 collective-permute-start.17
  209.1 2.4 collective-permute-start.15
  211.6 6.0 %down.3.refs_0_ = bf16[8,144,1024]{2,1,0:T(8,128)(2,1)} custom-call(bf16[1152,768]{1,0:T(8,128)(2,1)} %get-tuple-element.29.refs_0_, bf16[1152,32]{1,0:T(8,128)(2,1)} %get-tuple-element.30.refs_1_, bf16[768,2048]{1,0:T(8,128)(2,1)} %bitcast.63, bf16[32,2048]{1,0:T(8,128)(2,1)} %bitcast.72, bf16[8,144,1152]{2,1,0:T(8,128)(2,1)} %down.2.refs_9_.refs_4_.refs_11_), custom_call_target="tpu_custom_call" | custom-call | flops 1811939328 | bytes 3932160 | tf_op jit(solution)/shard_map/down/pallas_call | solution.py:426
  218.4 12.9 %collective-permute-done.16.refs_7_.refs_9_ = bf16[128,1024]{1,0:T(8,128)(2,1)S(1)} collective-permute-done((bf16[128,1024]{1,0:T(8,128)(2,1)}, bf16[128,1024]{1,0:T(8,128)(2,1)S(1)}, u32[]{:S(2)}, u32[]{:S(2)}) %collective-permute-start.16) | collective-permute-done | bytes 262176 | tf_op jit(solution)/shard_map/ppermute | solution.py:517
  232.8 6.3 %fill.1.refs_2_.refs_1_ = bf16[1152,2048]{1,0:T(8,128)(2,1)} custom-call(s32[8,512]{1,0:T(8,128)} %get-tuple-element.51.refs_1_.refs_0_.refs_4_, bf16[128,1024]{1,0:T(8,128)(2,1)} %after.14.refs_1_.refs_3_, bf16[128,1024]{1,0:T(8,128)(2,1)} %copy-done.8, bf16[128,1024]{1,0:T(8,128)(2,1)} %copy-done.7, bf16[128,1024]{1,0:T(8,128)(2,1)} %copy-done.6, ...), custom_call_target="tpu_custom_call" | custom-call | flops 2415919104 | bytes 4718592 | tf_op jit(solution)/shard_map/fill/pallas_call | solution.py:261
  241.2 4.4 %all-to-all-start.6 = ((bf16[8,144,1024]{2,1,0:T(8,128)(2,1)}), bf16[8,144,1024]{2,1,0:T(8,128)(2,1)}, u32[]{:S(2)}, u32[]{:S(2)}) async-start(bf16[8,144,1024]{2,1,0:T(8,128)(2,1)} %after.16), calls=%async_computation.6 | async-start | bytes 4718592 | tf_op jit(solution)/shard_map/all_to_all | solution.py:535
  245.6 5.6 %combine.2 = (bf16[128,1024]{1,0:T(8,128)(2,1)}, bf16[128,1024]{1,0:T(8,128)(2,1)}, bf16[128,1024]{1,0:T(8,128)(2,1)}, bf16[128,1024]{1,0:T(8,128)(2,1)}, f32[1152,1]{1,0:T(8,128)}) custom-call(bf16[8,144,1152]{2,1,0:T(8,128)(2,1)} %copy-done.2, bf16[512,1152]{1,0:T(8,128)(2,1)} %select_reduce_fusion.refs_7_.refs_1_.refs_3_, ...), custom_call_target="tpu_custom_call" | custom-call | flops 1207959552 | bytes 3407872 | tf_op jit(solution)/shard_map/combine/pallas_call | solution.py:487
  251.2 2.5 collective-permute-start.19
  255.6 3.6 %back_low.1.refs_2_ = bf16[8,32,256]{2,1,0:T(8,128)(2,1)} custom-call(s32[8,512]{1,0:T(8,128)} %get-tuple-element.51.refs_1_.refs_0_.refs_4_, f32[8,512]{1,0:T(8,128)} %bitcast.77, bf16[256,2048]{1,0:T(8,128)(2,1)} %bitcast.66, bf16[128,1024]{1,0:T(8,128)(2,1)} %after.14.refs_1_.refs_3_, bf16[128,1024]{1,0:T(8,128)(2,1)} %copy-done.8, ...), custom_call_target="tpu_custom_call" | custom-call | flops 536870912 | bytes 2097152 | tf_op jit(solution)/shard_map/back_low/pallas_call | solution.py:289
  259.2 4.3 %gradient.1.refs_0_ = bf16[8,32,2304]{2,1,0:T(8,128)(2,1)} custom-call(bf16[8,144,1152]{2,1,0:T(8,128)(2,1)} %copy-done.2, bf16[512,1152]{1,0:T(8,128)(2,1)} %select_reduce_fusion.refs_7_.refs_1_.refs_3_, bf16[8,32,256]{2,1,0:T(8,128)(2,1)} %back_low.1.refs_2_, bf16[128,1024]{1,0:T(8,128)(2,1)} %after.14.refs_1_.refs_3_, bf16[128,1024]{1,0:T(8,128)(2,1)} %copy-done.8, ...), custom_call_target="tpu_custom_call" | custom-call | flops 838860800 | bytes 4194304 | tf_op jit(solution)/shard_map/gradient/pallas_call | solution.py:328
  263.5 11.6 %all-to-all-done.6.refs_0_ = bf16[8,144,1024]{2,1,0:T(8,128)(2,1)} async-done(((bf16[8,144,1024]{2,1,0:T(8,128)(2,1)}), bf16[8,144,1024]{2,1,0:T(8,128)(2,1)}, u32[]{:S(2)}, u32[]{:S(2)}) %all-to-all-start.6) | async-done | bytes 2359328 | tf_op jit(solution)/shard_map/all_to_all | solution.py:535
  275.9 5.9 %combine.3 = (bf16[128,1152]{1,0:T(8,128)(2,1)}, bf16[128,1152]{1,0:T(8,128)(2,1)}, bf16[128,1152]{1,0:T(8,128)(2,1)}, bf16[128,1152]{1,0:T(8,128)(2,1)}) custom-call(bf16[8,144,1024]{2,1,0:T(8,128)(2,1)} %all-to-all-done.6.refs_0_, bf16[512,1152]{1,0:T(8,128)(2,1)} %select_reduce_fusion.refs_7_.refs_1_.refs_3_, bf16[1152,2048]{1,0:T(8,128)(2,1)} %fill.1.refs_2_.refs_1_, ...), custom_call_target="tpu_custom_call" | custom-call | flops 1207959552 | bytes 3407872 | tf_op jit(solution)/shard_map/combine/pallas_call | solution.py:487
  281.8 3.6 %all-to-all-start.7 = ((bf16[8,32,2304]{2,1,0:T(8,128)(2,1)}), bf16[8,32,2304]{2,1,0:T(8,128)(2,1)S(1)}, u32[]{:S(2)}, u32[]{:S(2)}) async-start(bf16[8,32,2304]{2,1,0:T(8,128)(2,1)} %after.17), calls=%async_computation.7 | async-start | bytes 2359296 | tf_op jit(solution)/shard_map/all_to_all | solution.py:535
  285.4 3.5 %collective-permute-start.21 = (bf16[128,1152]{1,0:T(8,128)(2,1)}, bf16[128,1152]{1,0:T(8,128)(2,1)S(1)}, u32[]{:S(2)}, u32[]{:S(2)}) collective-permute-start(bf16[128,1152]{1,0:T(8,128)(2,1)} %get-tuple-element.37), channel_id=1, source_target_pairs={{0,1},{1,0},{2,3},{3,2},{4,5},{5,4},{6,7},{7,6},{8,9},{9,8},{10,11... | collective-permute-start | bytes 884744 | tf_op jit(solution)/shard_map/ppermute | solution.py:517
  292.0 10.4 %collective-permute-done.21.refs_5_ = bf16[128,1152]{1,0:T(8,128)(2,1)S(1)} collective-permute-done((bf16[128,1152]{1,0:T(8,128)(2,1)}, bf16[128,1152]{1,0:T(8,128)(2,1)S(1)}, u32[]{:S(2)}, u32[]{:S(2)}) %collective-permute-start.21) | collective-permute-done | bytes 294944 | tf_op jit(solution)/shard_map/ppermute | solution.py:517
  302.5 10.1 %collective-permute-done.22.refs_6_ = bf16[128,1152]{1,0:T(8,128)(2,1)S(1)} collective-permute-done((bf16[128,1152]{1,0:T(8,128)(2,1)}, bf16[128,1152]{1,0:T(8,128)(2,1)S(1)}, u32[]{:S(2)}, u32[]{:S(2)}) %collective-permute-start.22) | collective-permute-done | bytes 294944 | tf_op jit(solution)/shard_map/ppermute | solution.py:517
  313.3 3.8 %finish.1 = (bf16[128,2048]{1,0:T(8,128)(2,1)}, f32[8,128]{1,0:T(8,128)}) custom-call(bf16[128,1024]{1,0:T(8,128)(2,1)} %get-tuple-element.31.refs_0_, bf16[128,1024]{1,0:T(8,128)(2,1)} %copy-done.16, bf16[128,1024]{1,0:T(8,128)(2,1)} %copy-done.17, bf16[128,1024]{1,0:T(8,128)(2,1)} %copy-done.18, bf16[128,1152]{1,0:T(8,128)(2,1)} %get-tuple-element.36.refs_4_.refs_1_, ...), custom_call_target="tpu_custom_call" | custom-call | tf_op jit(solution)/shard_map/finish/pallas_call | solution.py:585
  (177 shorter events, 50.3 us)
Async XLA Ops:
  0.6 44.3 %copy-start = (s32[1,1024]{1,0:T(1,128)S(1)}, s32[1,1024]{1,0:T(1,128)}, u32[]{:S(2)}) copy-start(s32[1,1024]{1,0:T(1,128)} %param.18) | copy-start | bytes 12292
  0.7 12.1 %copy-start.24 = (bf16[1,128,2048]{2,1,0:T(8,128)(2,1)S(1)}, bf16[1,128,2048]{2,1,0:T(8,128)(2,1)}, u32[]{:S(2)}) copy-start(bf16[1,128,2048]{2,1,0:T(8,128)(2,1)} %param.19) | copy-start | bytes 1572868
  3.9 31.3 %collective-permute-start.5 = (bf16[256,512]{1,0:T(8,128)(2,1)}, bf16[256,512]{1,0:T(8,128)(2,1)S(1)}, u32[]{:S(2)}, u32[]{:S(2)}) collective-permute-start(bf16[256,512]{1,0:T(8,128)(2,1)} %after.11), channel_id=1, source_target_pairs={{0,1},{1,0},{2,3},{3,2},{4,5},{5,4},{6,7},{7,6},{8,9},{9,8},{10,11... | collective-permute-start | bytes 786440 | tf_op jit(solution)/shard_map/ppermute | solution.py:527
  8.9 7.9 %copy-start.39 = (s32[1,128,8]{1,2,0:T(8,128)S(1)}, s32[1,128,8]{1,2,0:T(8,128)}, u32[]{:S(2)}) copy-start(s32[1,128,8]{1,2,0:T(8,128)} %param.22) | copy-start | bytes 12292
  8.9 8.0 %copy-start.40 = (f32[1,128,8]{1,2,0:T(8,128)S(1)}, f32[1,128,8]{1,2,0:T(8,128)}, u32[]{:S(2)}) copy-start(f32[1,128,8]{1,2,0:T(8,128)} %param.23) | copy-start | bytes 12292
  8.9 27.7 %all-to-all-start = ((bf16[8,128,512]{2,1,0:T(8,128)(2,1)}), bf16[8,128,512]{2,1,0:T(8,128)(2,1)S(1)}, u32[]{:S(2)}, u32[]{:S(2)}) async-start(bf16[8,128,512]{2,1,0:T(8,128)(2,1)} %broadcast_in_dim.52), calls=%async_computation | async-start | bytes 2097152 | tf_op jit(solution)/shard_map/all_to_all | solution.py:535
  14.3 21.0 %collective-permute-start.4 = (bf16[128,1024]{1,0:T(8,128)(2,1)}, bf16[128,1024]{1,0:T(8,128)(2,1)S(1)}, u32[]{:S(2)}, u32[]{:S(2)}) collective-permute-start(bf16[128,1024]{1,0:T(8,128)(2,1)} %after.10), channel_id=1, source_target_pairs={{0,2},{1,3},{2,0},{3,1},{4,6},{5,7},{6,4},{7,5},{8,10},{9,11},{10,... | collective-permute-start | bytes 786440 | tf_op jit(solution)/shard_map/ppermute | solution.py:527
  17.0 19.7 %copy-start.22 = (s32[1,128,8]{2,1,0:T(8,128)}, s32[1,128,8]{2,1,0:T(8,128)S(1)}, u32[]{:S(2)}) copy-start(s32[1,128,8]{2,1,0:T(8,128)S(1)} %copy.49) | copy-start | bytes 12292
  20.7 16.0 %copy-start.21 = (f32[128,8]{1,0:T(8,128)}, f32[128,8]{1,0:T(8,128)S(1)}, u32[]{:S(2)}) copy-start(f32[128,8]{1,0:T(8,128)S(1)} %fusion.5.refs_8_) | copy-start | bytes 12292
  20.8 18.6 %copy-start.33 = (f32[128,16]{1,0:T(8,128)}, f32[128,16]{1,0:T(8,128)S(1)}, u32[]{:S(2)}) copy-start(f32[128,16]{1,0:T(8,128)S(1)} %pad_maximum_fusion.3) | copy-start | bytes 24580
  20.8 6.9 %collective-permute-start.2 = (f32[128,16]{1,0:T(8,128)S(1)}, f32[128,16]{1,0:T(8,128)S(1)}, u32[]{:S(2)}, u32[]{:S(2)}) collective-permute-start(f32[128,16]{1,0:T(8,128)S(1)} %pad_maximum_fusion.3), channel_id=1, source_target_pairs={{0,3},{1,2},{2,1},{3,0},{4,7},{5,6},{6,5},{7,4},{8,11},{9,10},{10,... | collective-permute-start | bytes 24584 | tf_op jit(solution)/shard_map/ppermute | solution.py:517
  21.1 14.1 %collective-permute-start.1 = (f32[128,16]{1,0:T(8,128)S(1)}, f32[128,16]{1,0:T(8,128)S(1)}, u32[]{:S(2)}, u32[]{:S(2)}) collective-permute-start(f32[128,16]{1,0:T(8,128)S(1)} %pad_maximum_fusion.3), channel_id=1, source_target_pairs={{0,2},{1,3},{2,0},{3,1},{4,6},{5,7},{6,4},{7,5},{8,10},{9,11},{10,... | collective-permute-start | bytes 24584 | tf_op jit(solution)/shard_map/ppermute | solution.py:517
  22.8 12.5 %collective-permute-start = (f32[128,16]{1,0:T(8,128)S(1)}, f32[128,16]{1,0:T(8,128)S(1)}, u32[]{:S(2)}, u32[]{:S(2)}) collective-permute-start(f32[128,16]{1,0:T(8,128)S(1)} %pad_maximum_fusion.3), channel_id=1, source_target_pairs={{0,1},{1,0},{2,3},{3,2},{4,5},{5,4},{6,7},{7,6},{8,9},{9,8},{10,11... | collective-permute-start | bytes 24584 | tf_op jit(solution)/shard_map/ppermute | solution.py:517
  27.7 7.6 %copy-start.34 = (f32[128,16]{1,0:T(8,128)}, f32[128,16]{1,0:T(8,128)S(1)}, u32[]{:S(2)}) copy-start(f32[128,16]{1,0:T(8,128)S(1)} %collective-permute-done.2.refs_4_) | copy-start | bytes 24580
  39.3 6.4 %copy-start.27 = (bf16[128,512]{1,0:T(8,128)(2,1)S(1)}, bf16[128,512]{1,0:T(8,128)(2,1)}, u32[]{:S(2)}) copy-start(bf16[128,512]{1,0:T(8,128)(2,1)} %get-tuple-element.46) | copy-start | bytes 393220
  39.4 30.6 %all-to-all-start.1 = ((bf16[8,256,512]{2,1,0:T(8,128)(2,1)}), bf16[8,256,512]{2,1,0:T(8,128)(2,1)S(1)}, u32[]{:S(2)}, u32[]{:S(2)}) async-start(bf16[8,256,512]{2,1,0:T(8,128)(2,1)} %broadcast_in_dim.55), calls=%async_computation.1 | async-start | bytes 4194304 | tf_op jit(solution)/shard_map/all_to_all | solution.py:535
  55.7 26.6 %collective-permute-start.3 = (bf16[128,2048]{1,0:T(8,128)(2,1)}, bf16[128,2048]{1,0:T(8,128)(2,1)S(1)}, u32[]{:S(2)}, u32[]{:S(2)}) collective-permute-start(bf16[128,2048]{1,0:T(8,128)(2,1)} %attend.1.refs_0_), channel_id=1, source_target_pairs={{0,2},{1,3},{2,0},{3,1},{4,6},{5,7},{6,4},{7,5},{8,10},{9,11},{10,... | collective-permute-start | bytes 1572872 | tf_op jit(solution)/shard_map/ppermute | solution.py:527
  73.3 40.1 %all-to-all-start.2 = ((bf16[8,32,2048]{2,1,0:T(8,128)(2,1)}), bf16[8,32,2048]{2,1,0:T(8,128)(2,1)S(1)}, u32[]{:S(2)}, u32[]{:S(2)}) async-start(bf16[8,32,2048]{2,1,0:T(8,128)(2,1)} %broadcast_in_dim.90), calls=%async_computation.2 | async-start | bytes 2097152 | tf_op jit(solution)/shard_map/all_to_all | solution.py:535
  78.0 10.0 %copy-start.37 = (f32[512,8]{0,1:T(8,128)}, f32[512,8]{0,1:T(8,128)S(1)}, u32[]{:S(2)}) copy-start(f32[512,8]{0,1:T(8,128)S(1)} %fusion.2) | copy-start | bytes 49156
  88.0 11.7 %collective-permute-start.11 = (bf16[272,512]{1,0:T(8,128)(2,1)}, bf16[272,512]{1,0:T(8,128)(2,1)S(1)}, u32[]{:S(2)}, u32[]{:S(2)}) collective-permute-start(bf16[272,512]{1,0:T(8,128)(2,1)} %get-tuple-element.24.refs_2_), channel_id=1, source_target_pairs={{0,3},{1,2},{2,1},{3,0},{4,7},{5,6},{6,5},{7,4},{8,11},{9,10},{10,... | collective-permute-start | bytes 835592 | tf_op jit(solution)/shard_map/ppermute | solution.py:517
  89.9 23.5 %collective-permute-start.10 = (bf16[272,512]{1,0:T(8,128)(2,1)}, bf16[272,512]{1,0:T(8,128)(2,1)S(1)}, u32[]{:S(2)}, u32[]{:S(2)}) collective-permute-start(bf16[272,512]{1,0:T(8,128)(2,1)} %get-tuple-element.24.refs_2_), channel_id=1, source_target_pairs={{0,2},{1,3},{2,0},{3,1},{4,6},{5,7},{6,4},{7,5},{8,10},{9,11},{10,... | collective-permute-start | bytes 835592 | tf_op jit(solution)/shard_map/ppermute | solution.py:517
  89.9 23.5 %collective-permute-start.9 = (bf16[272,512]{1,0:T(8,128)(2,1)}, bf16[272,512]{1,0:T(8,128)(2,1)S(1)}, u32[]{:S(2)}, u32[]{:S(2)}) collective-permute-start(bf16[272,512]{1,0:T(8,128)(2,1)} %get-tuple-element.24.refs_2_), channel_id=1, source_target_pairs={{0,1},{1,0},{2,3},{3,2},{4,5},{5,4},{6,7},{7,6},{8,9},{9,8},{10,11... | collective-permute-start | bytes 835592 | tf_op jit(solution)/shard_map/ppermute | solution.py:517
  99.6 13.8 %copy-start.42 = (bf16[272,512]{1,0:T(8,128)(2,1)}, bf16[272,512]{1,0:T(8,128)(2,1)S(1)}, u32[]{:S(2)}) copy-start(bf16[272,512]{1,0:T(8,128)(2,1)S(1)} %collective-permute-done.11.refs_5_) | copy-start | bytes 835588
  118.9 33.4 %all-to-all-start.4 = ((bf16[8,144,1024]{2,1,0:T(8,128)(2,1)}), bf16[8,144,1024]{2,1,0:T(8,128)(2,1)S(1)}, u32[]{:S(2)}, u32[]{:S(2)}) async-start(bf16[8,144,1024]{2,1,0:T(8,128)(2,1)} %get-tuple-element.26), calls=%async_computation.4 | async-start | bytes 4718592 | tf_op jit(solution)/shard_map/all_to_all | solution.py:535
  122.8 11.1 %collective-permute-start.8 = (bf16[256,512]{1,0:T(8,128)(2,1)S(1)}, bf16[256,512]{1,0:T(8,128)(2,1)S(1)}, u32[]{:S(2)}, u32[]{:S(2)}) collective-permute-start(bf16[256,512]{1,0:T(8,128)(2,1)S(1)} %copy-done.45), channel_id=1, source_target_pairs={{0,3},{1,2},{2,1},{3,0},{4,7},{5,6},{6,5},{7,4},{8,11},{9,10},{10,... | collective-permute-start | bytes 786440 | tf_op jit(solution)/shard_map/ppermute | solution.py:517
  124.7 22.2 %collective-permute-start.7 = (bf16[256,512]{1,0:T(8,128)(2,1)S(1)}, bf16[256,512]{1,0:T(8,128)(2,1)S(1)}, u32[]{:S(2)}, u32[]{:S(2)}) collective-permute-start(bf16[256,512]{1,0:T(8,128)(2,1)S(1)} %copy-done.45), channel_id=1, source_target_pairs={{0,2},{1,3},{2,0},{3,1},{4,6},{5,7},{6,4},{7,5},{8,10},{9,11},{10,... | collective-permute-start | bytes 786440 | tf_op jit(solution)/shard_map/ppermute | solution.py:517
  124.7 22.2 %collective-permute-start.6 = (bf16[256,512]{1,0:T(8,128)(2,1)S(1)}, bf16[256,512]{1,0:T(8,128)(2,1)S(1)}, u32[]{:S(2)}, u32[]{:S(2)}) collective-permute-start(bf16[256,512]{1,0:T(8,128)(2,1)S(1)} %copy-done.45), channel_id=1, source_target_pairs={{0,1},{1,0},{2,3},{3,2},{4,5},{5,4},{6,7},{7,6},{8,9},{9,8},{10,11... | collective-permute-start | bytes 786440 | tf_op jit(solution)/shard_map/ppermute | solution.py:517
  133.9 13.0 %copy-start.30 = (bf16[256,512]{1,0:T(8,128)(2,1)}, bf16[256,512]{1,0:T(8,128)(2,1)S(1)}, u32[]{:S(2)}) copy-start(bf16[256,512]{1,0:T(8,128)(2,1)S(1)} %collective-permute-done.8.refs_5_.refs_3_) | copy-start | bytes 786436
  153.7 33.1 %all-to-all-start.3 = ((bf16[8,144,1024]{2,1,0:T(8,128)(2,1)}), bf16[8,144,1024]{2,1,0:T(8,128)(2,1)S(1)}, u32[]{:S(2)}, u32[]{:S(2)}) async-start(bf16[8,144,1024]{2,1,0:T(8,128)(2,1)} %pick.3), calls=%async_computation.3 | async-start | bytes 4718592 | tf_op jit(solution)/shard_map/all_to_all | solution.py:535
  159.1 12.1 %collective-permute-start.14 = (bf16[128,1024]{1,0:T(8,128)(2,1)}, bf16[128,1024]{1,0:T(8,128)(2,1)S(1)}, u32[]{:S(2)}, u32[]{:S(2)}) collective-permute-start(bf16[128,1024]{1,0:T(8,128)(2,1)} %after.14.refs_1_.refs_3_), channel_id=1, source_target_pairs={{0,3},{1,2},{2,1},{3,0},{4,7},{5,6},{6,5},{7,4},{8,11},{9,10},{10,... | collective-permute-start | bytes 786440 | tf_op jit(solution)/shard_map/ppermute | solution.py:517
  161.0 22.4 %collective-permute-start.13 = (bf16[128,1024]{1,0:T(8,128)(2,1)}, bf16[128,1024]{1,0:T(8,128)(2,1)S(1)}, u32[]{:S(2)}, u32[]{:S(2)}) collective-permute-start(bf16[128,1024]{1,0:T(8,128)(2,1)} %after.14.refs_1_.refs_3_), channel_id=1, source_target_pairs={{0,2},{1,3},{2,0},{3,1},{4,6},{5,7},{6,4},{7,5},{8,10},{9,11},{10,... | collective-permute-start | bytes 786440 | tf_op jit(solution)/shard_map/ppermute | solution.py:517
  161.0 22.4 %collective-permute-start.12 = (bf16[128,1024]{1,0:T(8,128)(2,1)}, bf16[128,1024]{1,0:T(8,128)(2,1)S(1)}, u32[]{:S(2)}, u32[]{:S(2)}) collective-permute-start(bf16[128,1024]{1,0:T(8,128)(2,1)} %after.14.refs_1_.refs_3_), channel_id=1, source_target_pairs={{0,1},{1,0},{2,3},{3,2},{4,5},{5,4},{6,7},{7,6},{8,9},{9,8},{10,11... | collective-permute-start | bytes 786440 | tf_op jit(solution)/shard_map/ppermute | solution.py:517
  171.3 15.6 %copy-start.6 = (bf16[128,1024]{1,0:T(8,128)(2,1)}, bf16[128,1024]{1,0:T(8,128)(2,1)S(1)}, u32[]{:S(2)}) copy-start(bf16[128,1024]{1,0:T(8,128)(2,1)S(1)} %collective-permute-done.14.refs_8_.refs_3_.refs_4_.refs_6_) | copy-start | bytes 786436
  203.5 36.2 %all-to-all-start.5 = ((bf16[8,144,1152]{2,1,0:T(8,128)(2,1)}), bf16[8,144,1152]{2,1,0:T(8,128)(2,1)S(1)}, u32[]{:S(2)}, u32[]{:S(2)}) async-start(bf16[8,144,1152]{2,1,0:T(8,128)(2,1)} %down.2.refs_9_.refs_4_.refs_11_), calls=%async_computation.5 | async-start | bytes 5308416 | tf_op jit(solution)/shard_map/all_to_all | solution.py:535
  207.1 11.3 %collective-permute-start.17 = (bf16[128,1024]{1,0:T(8,128)(2,1)}, bf16[128,1024]{1,0:T(8,128)(2,1)S(1)}, u32[]{:S(2)}, u32[]{:S(2)}) collective-permute-start(bf16[128,1024]{1,0:T(8,128)(2,1)} %after.15.refs_5_.refs_7_), channel_id=1, source_target_pairs={{0,3},{1,2},{2,1},{3,0},{4,7},{5,6},{6,5},{7,4},{8,11},{9,10},{10,... | collective-permute-start | bytes 786440 | tf_op jit(solution)/shard_map/ppermute | solution.py:517
  209.1 22.2 %collective-permute-start.16 = (bf16[128,1024]{1,0:T(8,128)(2,1)}, bf16[128,1024]{1,0:T(8,128)(2,1)S(1)}, u32[]{:S(2)}, u32[]{:S(2)}) collective-permute-start(bf16[128,1024]{1,0:T(8,128)(2,1)} %after.15.refs_5_.refs_7_), channel_id=1, source_target_pairs={{0,2},{1,3},{2,0},{3,1},{4,6},{5,7},{6,4},{7,5},{8,10},{9,11},{10,... | collective-permute-start | bytes 786440 | tf_op jit(solution)/shard_map/ppermute | solution.py:517
  209.1 22.2 %collective-permute-start.15 = (bf16[128,1024]{1,0:T(8,128)(2,1)}, bf16[128,1024]{1,0:T(8,128)(2,1)S(1)}, u32[]{:S(2)}, u32[]{:S(2)}) collective-permute-start(bf16[128,1024]{1,0:T(8,128)(2,1)} %after.15.refs_5_.refs_7_), channel_id=1, source_target_pairs={{0,1},{1,0},{2,3},{3,2},{4,5},{5,4},{6,7},{7,6},{8,9},{9,8},{10,11... | collective-permute-start | bytes 786440 | tf_op jit(solution)/shard_map/ppermute | solution.py:517
  218.4 12.9 %copy-start.11 = (bf16[128,1024]{1,0:T(8,128)(2,1)}, bf16[128,1024]{1,0:T(8,128)(2,1)S(1)}, u32[]{:S(2)}) copy-start(bf16[128,1024]{1,0:T(8,128)(2,1)S(1)} %collective-permute-done.17.refs_8_.refs_10_) | copy-start | bytes 786436
  241.2 33.8 %all-to-all-start.6 = ((bf16[8,144,1024]{2,1,0:T(8,128)(2,1)}), bf16[8,144,1024]{2,1,0:T(8,128)(2,1)}, u32[]{:S(2)}, u32[]{:S(2)}) async-start(bf16[8,144,1024]{2,1,0:T(8,128)(2,1)} %after.16), calls=%async_computation.6 | async-start | bytes 4718592 | tf_op jit(solution)/shard_map/all_to_all | solution.py:535
  251.2 23.8 %collective-permute-start.18 = (bf16[128,1024]{1,0:T(8,128)(2,1)}, bf16[128,1024]{1,0:T(8,128)(2,1)S(1)}, u32[]{:S(2)}, u32[]{:S(2)}) collective-permute-start(bf16[128,1024]{1,0:T(8,128)(2,1)} %get-tuple-element.32), channel_id=1, source_target_pairs={{0,1},{1,0},{2,3},{3,2},{4,5},{5,4},{6,7},{7,6},{8,9},{9,8},{10,11... | collective-permute-start | bytes 786440 | tf_op jit(solution)/shard_map/ppermute | solution.py:517
  251.2 23.9 %collective-permute-start.19 = (bf16[128,1024]{1,0:T(8,128)(2,1)}, bf16[128,1024]{1,0:T(8,128)(2,1)S(1)}, u32[]{:S(2)}, u32[]{:S(2)}) collective-permute-start(bf16[128,1024]{1,0:T(8,128)(2,1)} %get-tuple-element.33), channel_id=1, source_target_pairs={{0,2},{1,3},{2,0},{3,1},{4,6},{5,7},{6,4},{7,5},{8,10},{9,11},{10,... | collective-permute-start | bytes 786440 | tf_op jit(solution)/shard_map/ppermute | solution.py:517
  253.7 21.3 %collective-permute-start.20 = (bf16[128,1024]{1,0:T(8,128)(2,1)}, bf16[128,1024]{1,0:T(8,128)(2,1)S(1)}, u32[]{:S(2)}, u32[]{:S(2)}) collective-permute-start(bf16[128,1024]{1,0:T(8,128)(2,1)} %get-tuple-element.34), channel_id=1, source_target_pairs={{0,3},{1,2},{2,1},{3,0},{4,7},{5,6},{6,5},{7,4},{8,11},{9,10},{10,... | collective-permute-start | bytes 786440 | tf_op jit(solution)/shard_map/ppermute | solution.py:517
  281.8 35.2 %all-to-all-start.7 = ((bf16[8,32,2304]{2,1,0:T(8,128)(2,1)}), bf16[8,32,2304]{2,1,0:T(8,128)(2,1)S(1)}, u32[]{:S(2)}, u32[]{:S(2)}) async-start(bf16[8,32,2304]{2,1,0:T(8,128)(2,1)} %after.17), calls=%async_computation.7 | async-start | bytes 2359296 | tf_op jit(solution)/shard_map/all_to_all | solution.py:535
  285.4 32.5 %copy-start.4 = (bf16[1152,768]{1,0:T(8,128)(2,1)S(1)}, bf16[1152,768]{1,0:T(8,128)(2,1)}, u32[]{:S(2)}) copy-start(bf16[1152,768]{1,0:T(8,128)(2,1)} %get-tuple-element.29.refs_0_) | copy-start | bytes 5308420
  285.4 17.0 %collective-permute-start.21 = (bf16[128,1152]{1,0:T(8,128)(2,1)}, bf16[128,1152]{1,0:T(8,128)(2,1)S(1)}, u32[]{:S(2)}, u32[]{:S(2)}) collective-permute-start(bf16[128,1152]{1,0:T(8,128)(2,1)} %get-tuple-element.37), channel_id=1, source_target_pairs={{0,1},{1,0},{2,3},{3,2},{4,5},{5,4},{6,7},{7,6},{8,9},{9,8},{10,11... | collective-permute-start | bytes 884744 | tf_op jit(solution)/shard_map/ppermute | solution.py:517
  288.9 23.6 %collective-permute-start.22 = (bf16[128,1152]{1,0:T(8,128)(2,1)}, bf16[128,1152]{1,0:T(8,128)(2,1)S(1)}, u32[]{:S(2)}, u32[]{:S(2)}) collective-permute-start(bf16[128,1152]{1,0:T(8,128)(2,1)} %get-tuple-element.38), channel_id=1, source_target_pairs={{0,2},{1,3},{2,0},{3,1},{4,6},{5,7},{6,4},{7,5},{8,10},{9,11},{10,... | collective-permute-start | bytes 884744 | tf_op jit(solution)/shard_map/ppermute | solution.py:517
  289.5 23.1 %collective-permute-start.23 = (bf16[128,1152]{1,0:T(8,128)(2,1)}, bf16[128,1152]{1,0:T(8,128)(2,1)}, u32[]{:S(2)}, u32[]{:S(2)}) collective-permute-start(bf16[128,1152]{1,0:T(8,128)(2,1)} %get-tuple-element.39), channel_id=1, source_target_pairs={{0,3},{1,2},{2,1},{3,0},{4,7},{5,6},{6,5},{7,4},{8,11},{9,10},{10,... | collective-permute-start | bytes 884744 | tf_op jit(solution)/shard_map/ppermute | solution.py:517
  302.5 10.1 %copy-start.28 = (bf16[128,1152]{1,0:T(8,128)(2,1)}, bf16[128,1152]{1,0:T(8,128)(2,1)S(1)}, u32[]{:S(2)}) copy-start(bf16[128,1152]{1,0:T(8,128)(2,1)S(1)} %collective-permute-done.21.refs_5_) | copy-start | bytes 884740
  (30 other events, 65.7 us)

commit v3 on v1

v3 whole, which is shorter than its diff:
```python
import math

import jax
import jax.numpy as jnp
from jax import lax
from jax.experimental import pallas as pl
from jax.experimental.pallas import tpu as pltpu
from jax.sharding import PartitionSpec as P

QUERY_HEADS = 16
KEY_VALUE_HEADS = 2
HEAD_SIZE = 128
PICKS_PER_TOKEN = 8

adapter_scale = 2.0
norm_eps = 1e-06
BF16 = jnp.bfloat16
F32 = jnp.float32


def dot(a, b):
    return jnp.dot(a, b, preferred_element_type=F32)


def dot_t(a, b):
    return lax.dot_general(a, b, (((1,), (1,)), ((), ())), preferred_element_type=F32)


def attend_kernel(start_ref, query_ref, kv_ref, bias_ref, *refs):
    out_ref = refs[-1]
    tokens = query_ref.shape[0]
    window = bias_ref.shape[1]
    start = pl.multiple_of(start_ref[0] * tokens, tokens)
    bias = bias_ref[...]
    group = QUERY_HEADS // KEY_VALUE_HEADS
    width = KEY_VALUE_HEADS * HEAD_SIZE
    factor = math.log2(math.e) / math.sqrt(HEAD_SIZE)
    for kv_head in range(KEY_VALUE_HEADS):
        first = kv_head * HEAD_SIZE
        key_rows = kv_ref[pl.ds(start, window), first : first + HEAD_SIZE]
        value_rows = kv_ref[pl.ds(start, window), width + first : width + first + HEAD_SIZE]
        for pair in range(group // 2):
            at = (kv_head * group + pair * 2) * HEAD_SIZE
            rows = jnp.concatenate(
                [
                    query_ref[:, at : at + HEAD_SIZE],
                    query_ref[:, at + HEAD_SIZE : at + 2 * HEAD_SIZE],
                ],
                axis=0,
            )
            scores = dot_t(rows, key_rows).reshape(2, tokens, window) + bias[None]
            highest = jnp.max(scores, axis=-1, keepdims=True)
            raised = jnp.exp2((scores - highest) * factor)
            total = jnp.sum(raised, axis=-1, keepdims=True)
            mixed = dot(raised.astype(BF16).reshape(2 * tokens, window), value_rows)
            mixed = (mixed.reshape(2, tokens, HEAD_SIZE) / total).astype(BF16)
            out_ref[:, at : at + HEAD_SIZE] = mixed[0]
            out_ref[:, at + HEAD_SIZE : at + 2 * HEAD_SIZE] = mixed[1]


def attend(queries, kv_all, documents, earlier):
    tokens = queries.shape[0]
    length = kv_all.shape[0]
    place = lax.axis_index("seq")
    window = min(length, length // 2 + tokens)
    first_block = jnp.clip(place + 1 - window // tokens, 0, (length - window) // tokens)
    mine = place * tokens + jnp.arange(tokens)
    there = first_block * tokens + jnp.arange(window)
    doc_mine = lax.dynamic_slice_in_dim(documents, place * tokens, tokens)
    doc_there = lax.dynamic_slice_in_dim(documents, first_block * tokens, window)
    allowed = (there[None, :] <= mine[:, None]) & (doc_there[None, :] == doc_mine[:, None])
    bias = jnp.where(allowed, 0.0, -jnp.inf).astype(F32)
    return pl.pallas_call(
        attend_kernel,
        out_shape=jax.ShapeDtypeStruct(queries.shape, BF16),
        in_specs=[
            pl.BlockSpec(memory_space=pltpu.SMEM),
            pl.BlockSpec(memory_space=pltpu.VMEM),
            pl.BlockSpec(memory_space=pltpu.VMEM),
            pl.BlockSpec(memory_space=pltpu.VMEM),
        ]
        + [anywhere()] * len(earlier),
        out_specs=pl.BlockSpec(memory_space=pltpu.VMEM),
        compiler_params=params(),
        name="attend",
    )(first_block.reshape(1).astype(jnp.int32), queries, kv_all, bias, *earlier)


def vmem():
    return pl.BlockSpec(memory_space=pltpu.VMEM)


def anywhere():
    return pl.BlockSpec(memory_space=pl.ANY)


def smem():
    return pl.BlockSpec(memory_space=pltpu.SMEM)


def params(mebibytes=24):
    return pltpu.CompilerParams(vmem_limit_bytes=mebibytes << 20)


def cost(flops, bytes_accessed):
    return pl.CostEstimate(flops=flops, bytes_accessed=bytes_accessed, transcendentals=0)


def project_kernel(*refs, blocks, chunks):
    attended, residuals = refs[:blocks], refs[blocks : 2 * blocks]
    own_ref, pair_ref, gain_ref, routing_ref = refs[2 * blocks : 2 * blocks + 4]
    outs = refs[2 * blocks + 4 :]
    cols = own_ref.shape[1]
    tokens = residuals[0].shape[0]
    rows = jnp.concatenate([ref[...] for ref in attended], axis=0)
    square = None
    for side, weight_ref in enumerate((own_ref, pair_ref)):
        at = side * cols
        stream = dot(rows, weight_ref[...])
        stream += jnp.concatenate([ref[:, at : at + cols] for ref in residuals], axis=0).astype(F32)
        scaled = (stream * gain_ref[:, at : at + cols]).astype(BF16)
        for out_ref, (start, size) in zip(outs, chunks):
            out_ref[: blocks * tokens, side * size : (side + 1) * size] = scaled[
                :, start : start + size
            ]
        for lane in range(0, cols, 128):
            piece = stream[:, lane : lane + 128]
            square = piece * piece if square is None else square + piece * piece
    square = jnp.sum(square.T, axis=0, keepdims=True)
    square = jnp.concatenate(
        [square[:, i * tokens : (i + 1) * tokens] for i in range(blocks)], axis=0
    )
    high = square.astype(BF16).astype(F32)
    routing = routing_ref[...]
    picks = routing.shape[0] // 2
    gates = routing[:picks].astype(BF16).astype(F32)
    rest = outs[0].shape[0] - blocks * tokens - 3 * picks - 2 * blocks
    rest = [jnp.zeros((rest, tokens), F32)] if rest else []
    outs[0][blocks * tokens :, tokens:] = jnp.zeros(
        (outs[0].shape[0] - blocks * tokens, outs[0].shape[1] - tokens), BF16
    )
    outs[0][blocks * tokens :, :tokens] = jnp.concatenate(
        [gates, routing[:picks] - gates, routing[picks:], high, square - high, *rest], axis=0
    ).astype(BF16)


def project(attended, residuals, own_weight, pair_weight, gain, routing, chunks):
    blocks = len(attended)
    tokens, width = attended[0].shape
    cols = own_weight.shape[1]
    rows = blocks * tokens
    more = 3 * routing.shape[0] // 2 + 2 * blocks
    more = -(-more // 16) * 16
    return pl.pallas_call(
        lambda *refs: project_kernel(*refs, blocks=blocks, chunks=chunks),
        in_specs=[vmem()] * (2 * blocks + 4),
        out_specs=[vmem()] * len(chunks),
        out_shape=[
            jax.ShapeDtypeStruct((rows + (0 if number else more), 2 * size), BF16)
            for number, (_, size) in enumerate(chunks)
        ],
        compiler_params=params(),
        cost_estimate=cost(4 * rows * width * cols, 4 * width * cols),
        name="project",
    )(*attended, *residuals, own_weight, pair_weight, gain.reshape(1, 2 * cols), routing)


def hits_of(slots, capacity):
    groups, near = slots.shape
    places = lax.broadcasted_iota(jnp.int32, (capacity, near), 0)
    return jnp.concatenate(
        [
            jnp.where(places == slots[group : group + 1, :], 1.0, 0.0).astype(F32)
            for group in range(groups)
        ],
        axis=0,
    )


def route_kernel(column_ref, *refs, capacity, picks, columns, width):
    blocks = refs[:-4]
    slot_ref, gate_ref, weight_ref, inverse_ref = refs[-4:]
    groups, near = slot_ref.shape
    count = len(blocks)
    tokens = near // count
    tables = [block[near:, :tokens].astype(F32) for block in blocks]
    table = jnp.concatenate(tables, axis=1)
    probs = table[:picks] + table[picks : 2 * picks]
    ids = table[2 * picks : 3 * picks].astype(jnp.int32)
    member, gates = [], []
    for group in range(groups):
        hit = ids == group * columns + column_ref[0]
        member.append(jnp.sum(hit.astype(F32), axis=0, keepdims=True))
        gates.append(jnp.sum(jnp.where(hit, probs, 0.0), axis=0, keepdims=True))
    member = jnp.concatenate(member, axis=0)
    earlier = lax.broadcasted_iota(jnp.int32, (near, near), 0) < lax.broadcasted_iota(
        jnp.int32, (near, near), 1
    )
    ranks = dot(member.astype(BF16), earlier.astype(BF16)).astype(jnp.int32)
    slots = jnp.where(member > 0.0, ranks, capacity)
    slot_ref[...] = slots
    gate_ref[...] = jnp.concatenate(gates, axis=0)
    places = lax.broadcasted_iota(jnp.int32, (capacity, near), 0)
    weights = [
        jnp.where(places == slots[group : group + 1], gates[group], 0.0) for group in range(groups)
    ]
    rows = groups * capacity
    if rows % 128:
        weights.append(jnp.zeros((-rows % 128, near), F32))
    weight_ref[...] = jnp.concatenate(weights, axis=0).T[:, :rows].astype(BF16)
    inverses = []
    for b in range(count):
        total = jnp.zeros((1, tokens), F32)
        for i in range(count):
            row = 3 * picks + (i ^ b)
            total += tables[i][row : row + 1]
            total += tables[i][count + row : count + row + 1]
        inverses.append(lax.rsqrt(total / width + norm_eps))
    inverse_ref[...] = jnp.concatenate(inverses, axis=1)


def route(column, blocks, groups, capacity, tokens, picks, columns, width):
    near = len(blocks) * tokens
    return pl.pallas_call(
        lambda *refs: route_kernel(
            *refs, capacity=capacity, picks=picks, columns=columns, width=width
        ),
        in_specs=[smem()] + [vmem()] * len(blocks),
        out_specs=[vmem()] * 4,
        out_shape=[
            jax.ShapeDtypeStruct((groups, near), jnp.int32),
            jax.ShapeDtypeStruct((groups, near), F32),
            jax.ShapeDtypeStruct((near, groups * capacity), BF16),
            jax.ShapeDtypeStruct((1, near), F32),
        ],
        compiler_params=params(),
        name="route",
    )(column.reshape(1), *blocks)


def pick_kernel(first_ref, slot_ref, inverse_ref, *refs, count, capacity):
    blocks = refs[:count]
    out_ref = refs[-1]
    near = slot_ref.shape[1]
    tokens = near // count
    half = blocks[0].shape[1] // 2
    hits = hits_of(slot_ref[...], capacity)
    factors = jnp.sum(hits * inverse_ref[...], axis=1, keepdims=True)
    hits = hits.astype(BF16)
    for i, block in enumerate(blocks):
        rows = jnp.concatenate(
            [block[(i ^ b) * tokens : ((i ^ b) + 1) * tokens, :] for b in range(count)], axis=0
        )
        picked = (dot(hits, rows) * factors).astype(BF16)
        for side in range(2):
            at = pl.multiple_of((first_ref[0] ^ (2 * i + side)) * half, 128)
            out_ref[:, pl.ds(at, half)] = picked[:, side * half : (side + 1) * half]


def pick(first, slots, inverse, blocks, capacity, earlier):
    groups, near = slots.shape
    count = len(blocks)
    cols = blocks[0].shape[1] * count
    rows = groups * capacity
    return pl.pallas_call(
        lambda *refs: pick_kernel(*refs[: 3 + count], refs[-1], count=count, capacity=capacity),
        in_specs=[smem()] + [vmem()] * (2 + count) + [anywhere()] * len(earlier),
        out_specs=vmem(),
        out_shape=jax.ShapeDtypeStruct((rows, cols), BF16),
        compiler_params=params(),
        cost_estimate=cost(2 * rows * near * cols, 2 * rows * cols),
        name="pick",
    )(first.reshape(1), slots, inverse, *blocks, *earlier)


def fill_kernel(slot_ref, *refs, capacity):
    blocks, out_ref = refs[:-1], refs[-1]
    rows = jnp.concatenate([block[...] for block in blocks], axis=0)
    out_ref[...] = dot(hits_of(slot_ref[...], capacity).astype(BF16), rows).astype(BF16)


def fill(slots, blocks, capacity, earlier):
    groups, near = slots.shape
    rows, cols = groups * capacity, blocks[0].shape[1]
    return pl.pallas_call(
        lambda *refs: fill_kernel(*refs[: 1 + len(blocks)], refs[-1], capacity=capacity),
        in_specs=[vmem()] * (1 + len(blocks)) + [anywhere()],
        out_specs=vmem(),
        out_shape=jax.ShapeDtypeStruct((rows, cols), BF16),
        compiler_params=params(),
        cost_estimate=cost(2 * rows * near * cols, 2 * rows * cols),
        name="fill",
    )(slots, *blocks, earlier)


def back_kernel(factor_ref, *refs, capacity, count):
    out_ref = refs[-1]
    groups, rank, wide = out_ref.shape
    halves = 2
    part = wide // halves
    out_ref[...] = jnp.zeros(out_ref.shape, BF16)
    for half in range(halves):
        slot_ref, gate_ref, *blocks = refs[half * (2 + count) : (half + 1) * (2 + count)]
        rows = jnp.concatenate([block[...] for block in blocks], axis=0)
        made = dot_t(factor_ref[...], rows)
        hits = hits_of(slot_ref[...], capacity)
        for group in range(groups):
            mine = made[group * rank : (group + 1) * rank] * gate_ref[group : group + 1, :]
            slots = hits[group * capacity : (group + 1) * capacity].astype(BF16)
            out_ref[group, :, half * part : half * part + capacity] = dot_t(
                mine.astype(BF16), slots
            ).astype(BF16)


def back_slots_of(factors, halves, capacity, earlier):
    operands = [x for slots, gates, blocks in halves for x in (slots, gates, *blocks)]
    count = len(halves[0][2])
    groups, near = halves[0][0].shape
    rank = factors.shape[0] // groups
    part = capacity + -capacity % 128
    return pl.pallas_call(
        lambda *refs: back_kernel(
            *refs[: 1 + len(operands)], refs[-1], capacity=capacity, count=count
        ),
        in_specs=[vmem()] * (1 + len(operands)) + [anywhere()],
        out_specs=vmem(),
        out_shape=jax.ShapeDtypeStruct((groups, rank, 2 * part), BF16),
        compiler_params=params(),
        cost_estimate=cost(4 * near * factors.size, 4 * factors.size),
        name="back_low",
    )(factors, *operands, earlier)


def gradient_kernel(back_ref, *refs, count, rank):
    out_ref = refs[-1]
    groups = back_ref.shape[0]
    made = 0.0
    for half in range(2):
        low_ref, weight_ref, *blocks = refs[half * (2 + count) : (half + 1) * (2 + count)]
        rows = jnp.concatenate([block[...] for block in blocks], axis=0)
        low = low_ref[...].astype(F32)
        slots = low.shape[0]
        if slots % 128:
            low = jnp.concatenate([low, jnp.zeros((-slots % 128, low.shape[1]), F32)], axis=0)
        low = low.T[:rank, :slots]
        low = jnp.concatenate([low] * groups, axis=0)
        capacity = slots // groups
        group = lax.broadcasted_iota(jnp.int32, low.shape, 0) // rank
        place = lax.broadcasted_iota(jnp.int32, low.shape, 1) - group * capacity
        low = jnp.where((place >= 0) & (place < capacity), low, 0.0).astype(BF16)
        made += dot(dot_t(low, weight_ref[...]).astype(BF16), rows)
    width = made.shape[1]
    out_ref[:, :, :width] = made.astype(BF16).reshape(groups, rank, width)
    out_ref[:, :, width:] = back_ref[...]


def gradient_parts(back_slots, halves, earlier):
    groups, rank, wide = back_slots.shape
    width = halves[0][2][0].shape[1]
    count = len(halves[0][2])
    near = halves[0][1].shape[0]
    operands, in_specs = [back_slots], [pl.BlockSpec(back_slots.shape, lambda i: (0, 0, 0))]
    for back, weights, blocks in halves:
        operands += [back, weights, *blocks]
        in_specs.append(pl.BlockSpec((back.shape[0], 128), lambda i: (0, width // 128)))
        in_specs += [pl.BlockSpec(x.shape, lambda i: (0, 0)) for x in (weights, *blocks)]
    return pl.pallas_call(
        lambda *refs: gradient_kernel(*refs[: len(operands)], refs[-1], count=count, rank=rank),
        grid=(1,),
        in_specs=in_specs + [anywhere()],
        out_specs=pl.BlockSpec((groups, rank, width + wide), lambda i: (0, 0, 0)),
        out_shape=jax.ShapeDtypeStruct((groups, rank, width + wide), BF16),
        compiler_params=params(),
        cost_estimate=cost(4 * near * groups * rank * width, 4 * near * width),
        name="gradient",
    )(*operands, earlier)


def expert_kernel(
    rows_ref, gate_ref, up_ref, factor_ref, down_ref, up_factor_ref, out_active, out_ref
):
    rows = rows_ref[...]
    gate = dot(rows, gate_ref[...])
    up = dot(rows, up_ref[...])
    active = (gate / (1.0 + jnp.exp(-gate)) * up).astype(BF16)
    out_active[...] = active
    low = dot(active, factor_ref[...]).astype(BF16)
    made = dot(active, down_ref[...]) + adapter_scale * dot(low, up_factor_ref[...])
    cols, rank = made.shape[1], low.shape[1]
    out_ref[:, :cols] = made.astype(BF16)
    out_ref[:, cols:] = jnp.zeros((rows.shape[0], out_ref.shape[1] - cols), BF16)
    out_ref[:, cols : cols + rank] = low


def expert(rows, gate_weight, up_weight, factor, down_weight, up_factor, earlier):
    count, width = rows.shape
    units = gate_weight.shape[1]
    step = count // 2

    def whole(x):
        return pl.BlockSpec(x.shape, lambda i: (0, 0))

    weights = (gate_weight, up_weight, factor, down_weight, up_factor)
    return pl.pallas_call(
        lambda *refs: expert_kernel(*refs[:6], *refs[-2:]),
        grid=(count // step,),
        in_specs=[pl.BlockSpec((step, width), lambda i: (i, 0))]
        + [whole(x) for x in weights]
        + [anywhere()] * len(earlier),
        out_specs=[
            pl.BlockSpec((step, units), lambda i: (i, 0)),
            pl.BlockSpec((step, width + 128), lambda i: (i, 0)),
        ],
        out_shape=[
            jax.ShapeDtypeStruct((count, units), BF16),
            jax.ShapeDtypeStruct((count, width + 128), BF16),
        ],
        compiler_params=params(56),
        cost_estimate=cost(0, 0),
        name="expert",
    )(rows, *weights, *earlier)


def combine_kernel(back_ref, weight_ref, upstream_ref, slot_ref, *outs):
    blocks = len(outs)
    cols = upstream_ref.shape[1]
    groups, near = slot_ref.shape
    tokens = near // blocks
    back = back_ref[:, :cols]
    dots = jnp.sum(back.astype(F32) * upstream_ref[...].astype(F32), axis=1, keepdims=True)
    total = dot(weight_ref[...], back).astype(BF16)
    capacity = back.shape[0] // groups
    places = lax.broadcasted_iota(jnp.int32, (capacity, near), 0)
    found = []
    for group in range(groups):
        mine = dots[group * capacity : (group + 1) * capacity]
        hits = places == slot_ref[group : group + 1, :]
        found.append(jnp.sum(jnp.where(hits, mine, 0.0), axis=0, keepdims=True))
    found = jnp.concatenate(found, axis=0)
    high = found.astype(BF16).astype(F32)
    rest = jnp.zeros((128 - 2 * groups, near), F32)
    table = jnp.concatenate([high, found - high, rest], axis=0).T.astype(BF16)
    for block in range(blocks):
        outs[block][:, :cols] = total[block * tokens : (block + 1) * tokens]
        outs[block][:, cols:] = table[block * tokens : (block + 1) * tokens]


def combine(back, weights, upstream, slots, blocks, earlier):
    rows, cols = upstream.shape
    near = weights.shape[0]
    return pl.pallas_call(
        lambda *refs: combine_kernel(*refs[:4], *refs[4 + len(earlier) :]),
        in_specs=[vmem()] * 4 + [anywhere()] * len(earlier),
        out_specs=[vmem()] * blocks,
        out_shape=[jax.ShapeDtypeStruct((near // blocks, cols + 128), BF16)] * blocks,
        compiler_params=params(56),
        cost_estimate=cost(2 * rows * near * cols, 2 * cols * (rows + near)),
        name="combine",
    )(back, weights, upstream, slots, *earlier)


def from_plane(x, r):
    size = lax.axis_size("expert")
    return lax.ppermute(x, "expert", [(i, i ^ r) for i in range(size)])


def columns_of(x, r, size):
    return lax.dynamic_slice_in_dim(x, (lax.axis_index("expert") ^ r) * size, size, 1)


def swap(x):
    return lax.all_to_all(x, "seq", split_axis=0, concat_axis=0, tiled=True)


def spread(x):
    count = lax.axis_size("seq")
    return swap(jnp.broadcast_to(x[None], (count,) + x.shape)).reshape(-1, x.shape[-1])


def after(x, *earlier):
    return pl.pallas_call(
        lambda *refs: None,
        in_specs=[anywhere()] * (1 + len(earlier)),
        out_specs=anywhere(),
        out_shape=jax.ShapeDtypeStruct(x.shape, x.dtype),
        input_output_aliases={0: 0},
        name="after",
    )(x, *earlier)


def sum_kernel(parts_ref, *refs):
    actives, up_ref, down_ref = refs[:-2], refs[-2], refs[-1]
    groups, _, wide = parts_ref.shape
    width = up_ref.shape[1]
    part = (wide - width) // len(actives)
    up = jnp.zeros(up_ref.shape, F32)
    for group in range(groups):
        up += parts_ref[group, :, :width].astype(F32)
    up_ref[...] = adapter_scale * up
    low = jnp.zeros(down_ref.shape, F32)
    for half, active_ref in enumerate(actives):
        capacity = active_ref.shape[0] // groups
        active = active_ref[...].astype(F32)
        at = width + half * part
        for group in range(groups):
            low += dot(
                parts_ref[group, :, at : at + part][:, :capacity],
                active[group * capacity : (group + 1) * capacity].astype(BF16),
            )
    down_ref[...] = adapter_scale * low


def adapter_gradients(parts, actives, width):
    rank = parts.shape[1]
    return pl.pallas_call(
        sum_kernel,
        in_specs=[vmem()] * (1 + len(actives)),
        out_specs=[vmem()] * 2,
        out_shape=[
            jax.ShapeDtypeStruct((rank, width), F32),
            jax.ShapeDtypeStruct((rank, actives[0].shape[1]), F32),
        ],
        compiler_params=params(),
        name="gradients",
    )(parts, *actives)


def finish_kernel(*refs, groups):
    pieces = refs[:-5]
    probs_ref, ids_ref, names_ref, out_ref, grad_ref = refs[-5:]
    cols = out_ref.shape[1]
    total = pieces[0][:, :cols].astype(F32)
    for ref in pieces[1:]:
        total += ref[:, :cols].astype(F32)
    out_ref[...] = total.astype(BF16)
    dots = []
    for ref in pieces:
        table = ref[:, cols:].astype(F32)
        dots.append(table[:, :groups] + table[:, groups : 2 * groups])
    dots = jnp.concatenate(dots, axis=1)
    probs, ids, names = probs_ref[...], ids_ref[...], names_ref[...]
    picked = [
        jnp.sum(jnp.where(ids[:, k : k + 1] == names, dots, 0.0), axis=1, keepdims=True)
        for k in range(ids.shape[1])
    ]
    picked = jnp.concatenate(picked, axis=1)
    grad = probs * (picked - jnp.sum(probs * picked, axis=1, keepdims=True))
    rest = jnp.zeros((grad.shape[0], 128 - grad.shape[1]), F32)
    grad_ref[...] = jnp.concatenate([grad, rest], axis=1).T[: grad.shape[1]]


def finish(pieces, probs, ids, names, groups, earlier):
    tokens = probs.shape[0]
    count = len(pieces) + 3
    return pl.pallas_call(
        lambda *refs: finish_kernel(*refs[:count], *refs[-2:], groups=groups),
        in_specs=[vmem()] * count + [anywhere()],
        out_specs=[vmem()] * 2,
        out_shape=[
            jax.ShapeDtypeStruct((tokens, pieces[0].shape[1] - 128), BF16),
            jax.ShapeDtypeStruct(probs.shape[::-1], F32),
        ],
        compiler_params=params(56),
        name="finish",
    )(*pieces, probs, ids, names, earlier)


def shards(
    queries,
    keys,
    values,
    document_index,
    residual,
    output_projection,
    norm_gain_weight,
    routed_experts,
    router_logits,
    gate_weight,
    up_weight,
    down_weight,
    adapter_down,
    adapter_up,
    cotangent,
):
    seq_devices = lax.axis_size("seq")
    columns = lax.axis_size("expert")
    column = lax.axis_index("expert")
    place = lax.axis_index("seq")
    tokens = queries.shape[1]
    width = queries.shape[2]
    experts = seq_devices * columns
    rank = adapter_up.shape[1]
    near = columns * tokens
    block = width // columns

    kv_own = jnp.concatenate([keys[0], values[0]], axis=1)
    kv_all = spread(kv_own)
    share = output_projection.shape[0] // seq_devices
    pair_share = after(
        lax.dynamic_slice_in_dim(output_projection, place * share, share, 0), kv_own
    )
    pair_share = from_plane(pair_share, 1)
    gate_probs = jax.nn.softmax(router_logits[0].T, axis=0)
    routing = jnp.concatenate([gate_probs, routed_experts[0].T.astype(F32)], axis=0)
    gate_probs = gate_probs.T
    residuals = [
        jnp.concatenate([columns_of(residual[0], r, block), columns_of(residual[0], r + 1, block)], 1)
        for r in range(0, columns, 2)
    ]
    residuals = [residuals[0]] + [
        from_plane(after(residuals[r // 2], kv_own), r) for r in range(2, columns, 2)
    ]
    attended = attend(queries[0], kv_all, document_index[0], ())
    pair_share = jnp.broadcast_to(pair_share[None], (seq_devices,) + pair_share.shape)
    pair_projection = swap(after(pair_share, attended, *residuals[1:]))
    pair_projection = pair_projection.reshape(-1, block)
    attended = [attended] + [from_plane(attended, r) for r in range(2, columns, 2)]

    gain = norm_gain_weight[None]
    scaled = project(
        attended,
        residuals,
        output_projection,
        pair_projection,
        jnp.concatenate([columns_of(gain, 0, block), columns_of(gain, 1, block)], 1),
        routing,
        [(0, block)],
    )[0]
    capacity = columns // 2 * (9 * tokens * PICKS_PER_TOKEN // (8 * experts))
    up_factors = jnp.broadcast_to(adapter_up[0][None], (seq_devices, rank, width))
    up_factors = swap(after(up_factors, scaled)).reshape(-1, width)
    even = range(2, columns, 2)
    odd = range(1, columns, 2)
    crossed = {0: scaled, **{r: from_plane(scaled, r) for r in even}}
    later = after(scaled, *(crossed[r] for r in even))
    crossed.update({r: from_plane(later, r) for r in odd})
    upstream = {0: cotangent[0]}
    later = after(cotangent[0], *(crossed[r] for r in odd))
    upstream.update({r: from_plane(later, r) for r in even})
    later = after(cotangent[0], *(upstream[r] for r in even))
    upstream.update({r: from_plane(later, r) for r in odd})

    halves = []
    for half in range(2):
        blocks = [crossed[r] for r in range(half, columns, 2)]
        slots, gates, weights, inverse = route(
            column, blocks, seq_devices, capacity, tokens, PICKS_PER_TOKEN, columns, width
        )
        earlier = (up_factors,) if half == 0 else ()
        rows = swap(pick(column ^ half, slots, inverse, blocks, capacity, earlier))
        cotangents = [upstream[r] for r in range(half, columns, 2)]
        halves.append((slots, gates, weights, rows, cotangents))
    made = [
        expert(
            rows,
            gate_weight[0],
            up_weight[0],
            adapter_down[0],
            down_weight[0],
            adapter_up[0],
            (),
        )
        for half, (_, _, _, rows, cotangents) in enumerate(halves)
    ]

    filled = [
        fill(slots, cotangents, capacity, made[1][0]) for slots, _, _, _, cotangents in halves
    ]
    backs, pieces, earlier = [], {}, ()
    for half, (slots, _, weights, _, _) in enumerate(halves):
        sent = after(made[half][1], *(filled if half else [upstream[r] for r in even]))
        backs.append(swap(sent))
        sums = combine(backs[half], weights, filled[half], slots, columns // 2, earlier)
        planes = range(half, columns, 2)
        pieces.update({r: from_plane(x, r) if r else x for r, x in zip(planes, sums)})
        earlier = tuple(pieces[r] for r in planes if r)

    back_slots = back_slots_of(
        up_factors,
        [(slots, gates, cotangents) for slots, gates, _, _, cotangents in halves],
        capacity,
        pieces[0],
    )
    parts = gradient_parts(
        back_slots,
        [(back, half[2], half[4]) for back, half in zip(backs, halves)],
        sums[0],
    )
    up_factor_gradient, down_factor_gradient = adapter_gradients(
        swap(parts), [x[0] for x in made], width
    )

    names = (
        jnp.arange(seq_devices)[None, :] * columns
        + (column ^ jnp.arange(columns, dtype=jnp.int32))[:, None]
    )
    combined_output, router_logit_gradient = finish(
        [pieces[r] for r in range(columns)],
        gate_probs,
        routed_experts[0],
        names.reshape(1, experts),
        seq_devices,
        pieces[0],
    )
    return (
        combined_output[None],
        down_factor_gradient.T[None],
        up_factor_gradient[None],
        router_logit_gradient.T[None],
    )


def solution(mesh):
    return jax.shard_map(
        shards,
        mesh=mesh,
        in_specs=(
            P(("groups", "expert"), "seq", None),
            P(("groups", "expert"), "seq", None),
            P(("groups", "expert"), "seq", None),
            P(("groups", "expert"), None),
            P(("groups", "expert"), "seq", None),
            P(None, "expert"),
            P(),
            P(("groups", "expert"), "seq", None),
            P(("groups", "expert"), "seq", None),
            P(("seq", "expert"), None, None),
            P(("seq", "expert"), None, None),
            P(("seq", "expert"), None, None),
            P(("seq", "expert"), None, None),
            P(("seq", "expert"), None, None),
            P(("groups", "expert"), "seq", None),
        ),
        out_specs=(
            P(("groups", "expert"), "seq", None),
            P(("groups", "seq", "expert"), None, None),
            P(("groups", "seq", "expert"), None, None),
            P(("groups", "expert"), "seq", None),
        ),
        check_vma=False,
    )
```

time: 477 us -> 296 us (0.62)
  waiting for transfers between devices: 341 us -> 159 us
  matrix products: 56.5 us -> 0 us
  Pallas kernels: 3.4 us -> 57.1 us
  starting transfers between devices: 16.5 us -> 49.1 us
  blocking collectives: 22.3 us -> 0 us
  between operations: 14.4 us -> 1.16 us
  local copies, waits for them, and re-layouts: 12.5 us -> 24.5 us
  other arithmetic: 9.25 us -> 3.79 us
    all_gather x5 -> x0, waiting for transfers between devices: 197 us -> none  [the longest x1 145 us: shards(): projection = lax.all_gather(output_projection, 'expert', axis=0)]
    ppermute x0 -> x12, waiting for transfers between devices: none -> 149 us  [from_plane(): return lax.ppermute(x, 'expert', [(i, i ^ r) for i in range(size)])]
    all_to_all x4 -> x8, waiting for transfers between devices: 112 us -> 10.6 us  [swap(): return lax.all_to_all(x, 'seq', split_axis=0, concat_axis=0, tiled=True)]
    dot_general x15 -> x0, matrix products: 56.5 us -> none  [the longest x9 39.4 us: dot(): return jnp.dot(a, b, preferred_element_type=F32)]
    pallas_call x0 -> x24, Pallas kernels: none -> 53.6 us  [the longest x2 25 us: expert(): pl.pallas_call(lambda *refs: expert_kernel(*refs[:6], *refs[-2:]), grid=(...]
    reduce_scatter x2 -> x0, waiting for transfers between devices: 30.3 us -> none  [the longest x1 30.3 us: shards(): lax.psum_scatter(combined.astype(BF16), 'expert', scatter_dimension=0, ti...]
    all_to_all x4 -> x8, starting transfers between devices: 15.8 us -> 33.5 us  [swap(): return lax.all_to_all(x, 'seq', split_axis=0, concat_axis=0, tiled=True)]
    ppermute x0 -> x12, starting transfers between devices: none -> 15.6 us  [from_plane(): return lax.ppermute(x, 'expert', [(i, i ^ r) for i in range(size)])]
  transfers between devices with their start and end apart: 11 -> 20, of which waited for: 7 -> 12; matrix products, arithmetic and copies ran while one was open for 11% -> 3% of each run, Pallas kernels for 1% -> 15%
where the time goes in v3:
time: 296 us; the launch traced here: 295 us
  waiting for transfers between devices  159 us (54%)
  Pallas kernels  57.1 us (19%)
  starting transfers between devices  49.1 us (17%)
  local copies, waits for them, and re-layouts  24.5 us (8%)
  other arithmetic  3.79 us (1%)
    ppermute x12, waiting for transfers between devices, from_plane(): return lax.ppermute(x, 'expert', [(i, i ^ r) for i in range(size)])  149 us
    all_to_all x8, starting transfers between devices, swap(): return lax.all_to_all(x, 'seq', split_axis=0, concat_axis=0, tiled=True)  33.5 us
    pallas_call x2, Pallas kernels, expert(): pl.pallas_call(lambda *refs: expert_kernel(*refs[:6], *refs[-2:]), grid=(...  25 us
    unnamed x109, local copies, waits for them, and re-layouts  18.2 us
    ppermute x12, starting transfers between devices, from_plane(): return lax.ppermute(x, 'expert', [(i, i ^ r) for i in range(size)])  15.6 us
    all_to_all x8, waiting for transfers between devices, swap(): return lax.all_to_all(x, 'seq', split_axis=0, concat_axis=0, tiled=True)  10.6 us
    pallas_call x2, Pallas kernels, combine(): pl.pallas_call(lambda *refs: combine_kernel(*refs[:4], *refs[4 + len(earl...  9.66 us
  transfers between devices with their start and end apart: 20, of which 12 were waited for; matrix products, arithmetic and copies ran while one was open for 3% of the time, Pallas kernels for 15%

profile of v3, /device:TPU:0, one launch (start us, length us, event | category | flops | bytes accessed | tf_op | source)
XLA Modules:
  0.0 294.9 jit_solution(2629601535056608950)
XLA Ops:
  1.6 1.1 broadcast_in_dim.24
  2.7 5.2 %all-to-all-start = ((bf16[8,128,512]{2,1,0:T(8,128)(2,1)}), bf16[8,128,512]{2,1,0:T(8,128)(2,1)S(1)}, u32[]{:S(2)}, u32[]{:S(2)}) async-start(bf16[8,128,512]{2,1,0:T(8,128)(2,1)} %broadcast_in_dim.24), calls=%async_computation | async-start | bytes 2097152 | tf_op jit(solution)/shard_map/all_to_all | solution.py:472
  7.9 1.7 constant_dynamic-slice_fusion.refs_0_
  9.6 1.6 collective-permute-start.2
  12.0 2.6 collective-permute-start.1
  14.7 8.5 %all-to-all-done = bf16[8,128,512]{2,1,0:T(8,128)(2,1)S(1)} async-done(((bf16[8,128,512]{2,1,0:T(8,128)(2,1)}), bf16[8,128,512]{2,1,0:T(8,128)(2,1)S(1)}, u32[]{:S(2)}, u32[]{:S(2)}) %all-to-all-start) | async-done | bytes 1048608 | tf_op jit(solution)/shard_map/all_to_all | solution.py:472
  23.3 3.5 %attend.1.refs_1_.refs_0_ = bf16[128,2048]{1,0:T(8,128)(2,1)S(1)} custom-call(s32[1]{0:T(128)} %bitcast.1.start_ref, bf16[128,2048]{1,0:T(8,128)(2,1)S(1)} %bitcast.70, bf16[1024,512]{1,0:T(8,128)(2,1)S(1)} %bitcast.69, f32[128,640]{1,0:T(8,128)S(1)} %and_select_fusion.bias_ref), custom_call_target="tpu_custom_call" | custom-call | tf_op jit(solution)/shard_map/attend/pallas_call | solution.py:73
  27.6 1.5 broadcast_in_dim.27.refs_0_
  29.1 3.7 %all-to-all-start.1 = ((bf16[8,256,512]{2,1,0:T(8,128)(2,1)}), bf16[8,256,512]{2,1,0:T(8,128)(2,1)S(1)}, u32[]{:S(2)}, u32[]{:S(2)}) async-start(bf16[8,256,512]{2,1,0:T(8,128)(2,1)} %after.11), calls=%async_computation.1 | async-start | bytes 4194304 | tf_op jit(solution)/shard_map/all_to_all | solution.py:472
  33.4 2.6 collective-permute-start
  36.4 23.6 %collective-permute-done.refs_1_ = bf16[128,2048]{1,0:T(8,128)(2,1)} collective-permute-done((bf16[128,2048]{1,0:T(8,128)(2,1)S(1)}, bf16[128,2048]{1,0:T(8,128)(2,1)}, u32[]{:S(2)}, u32[]{:S(2)}) %collective-permute-start) | collective-permute-done | bytes 524320 | tf_op jit(solution)/shard_map/ppermute | solution.py:464
  60.0 1.6 copy-done.27
  61.6 2.5 project.1.refs_1_.refs_3_.refs_0_
  64.9 1.1 broadcast_in_dim.53.refs_0_
  66.1 4.0 %all-to-all-start.2 = ((bf16[8,32,2048]{2,1,0:T(8,128)(2,1)}), bf16[8,32,2048]{2,1,0:T(8,128)(2,1)S(1)}, u32[]{:S(2)}, u32[]{:S(2)}) async-start(bf16[8,32,2048]{2,1,0:T(8,128)(2,1)} %after.12), calls=%async_computation.2 | async-start | bytes 2097152 | tf_op jit(solution)/shard_map/all_to_all | solution.py:472
  70.0 1.8 collective-permute-start.3
  71.8 27.5 %collective-permute-done.3.refs_2_.refs_4_.refs_1_ = bf16[288,1024]{1,0:T(8,128)(2,1)S(1)} collective-permute-done((bf16[288,1024]{1,0:T(8,128)(2,1)S(1)}, bf16[288,1024]{1,0:T(8,128)(2,1)S(1)}, u32[]{:S(2)}, u32[]{:S(2)}) %collective-permute-start.3) | collective-permute-done | bytes 589856 | tf_op jit(solution)/shard_map/ppermute | solution.py:464
  100.4 2.2 pick.2
  102.6 4.4 %all-to-all-start.3 = ((bf16[8,72,2048]{2,1,0:T(8,128)(2,1)}), bf16[8,72,2048]{2,1,0:T(8,128)(2,1)}, u32[]{:S(2)}, u32[]{:S(2)}) async-start(bf16[8,72,2048]{2,1,0:T(8,128)(2,1)} %bitcast.20), calls=%async_computation.3 | async-start | bytes 4718592 | tf_op jit(solution)/shard_map/all_to_all | solution.py:472
  107.0 2.6 collective-permute-start.5
  109.6 15.7 %collective-permute-done.5.refs_2_.refs_4_ = bf16[288,1024]{1,0:T(8,128)(2,1)S(1)} collective-permute-done((bf16[288,1024]{1,0:T(8,128)(2,1)}, bf16[288,1024]{1,0:T(8,128)(2,1)S(1)}, u32[]{:S(2)}, u32[]{:S(2)}) %collective-permute-start.5) | collective-permute-done | bytes 589856 | tf_op jit(solution)/shard_map/ppermute | solution.py:464
  125.3 12.0 %collective-permute-done.4.refs_1_.refs_3_ = bf16[288,1024]{1,0:T(8,128)(2,1)S(1)} collective-permute-done((bf16[288,1024]{1,0:T(8,128)(2,1)}, bf16[288,1024]{1,0:T(8,128)(2,1)S(1)}, u32[]{:S(2)}, u32[]{:S(2)}) %collective-permute-start.4) | collective-permute-done | bytes 589856 | tf_op jit(solution)/shard_map/ppermute | solution.py:464
  138.4 2.2 pick.3
  140.7 4.0 %all-to-all-start.5 = ((bf16[8,72,2048]{2,1,0:T(8,128)(2,1)}), bf16[8,72,2048]{2,1,0:T(8,128)(2,1)S(1)}, u32[]{:S(2)}, u32[]{:S(2)}) async-start(bf16[8,72,2048]{2,1,0:T(8,128)(2,1)} %bitcast.30), calls=%async_computation.5 | async-start | bytes 4718592 | tf_op jit(solution)/shard_map/all_to_all | solution.py:472
  146.9 12.4 %expert.2 = (bf16[576,768]{1,0:T(8,128)(2,1)}, bf16[576,2176]{1,0:T(8,128)(2,1)}) custom-call(bf16[576,2048]{1,0:T(8,128)(2,1)} %bitcast.21.refs_0_, bf16[2048,768]{1,0:T(8,128)(2,1)} %bitcast.71, bf16[2048,768]{1,0:T(8,128)(2,1)} %bitcast.73, bf16[768,32]{1,0:T(8,128)(2,1)} %bitcast.80, bf16[768,2048]{1,0:T(8,128)(2,1)} %bitcast.75, bf16[32,2048]{1,0:T(8,128)(2,1)} %bitcast.82), custom_call_target="tpu_custom_call" | custom-call | tf_op jit(solution)/shard_map/expert/pallas_call | solution.py:404
  159.3 12.9 %collective-permute-done.6.refs_1_.refs_2_.refs_4_ = bf16[128,2048]{1,0:T(8,128)(2,1)S(1)} collective-permute-done((bf16[128,2048]{1,0:T(8,128)(2,1)}, bf16[128,2048]{1,0:T(8,128)(2,1)S(1)}, u32[]{:S(2)}, u32[]{:S(2)}) %collective-permute-start.6) | collective-permute-done | bytes 524320 | tf_op jit(solution)/shard_map/ppermute | solution.py:464
  173.0 1.2 all-to-all-done.5
  174.2 1.4 copy-done.41
  175.6 3.8 %all-to-all-start.4 = ((bf16[8,72,2176]{2,1,0:T(8,128)(2,1)}), bf16[8,72,2176]{2,1,0:T(8,128)(2,1)S(1)}, u32[]{:S(2)}, u32[]{:S(2)}) async-start(bf16[8,72,2176]{2,1,0:T(8,128)(2,1)} %bitcast.78), calls=%async_computation.4 | async-start | bytes 5013504 | tf_op jit(solution)/shard_map/all_to_all | solution.py:472
  180.2 1.6 collective-permute-start.8
  181.8 12.6 %expert.3 = (bf16[576,768]{1,0:T(8,128)(2,1)}, bf16[576,2176]{1,0:T(8,128)(2,1)}) custom-call(bf16[576,2048]{1,0:T(8,128)(2,1)} %bitcast.79, bf16[2048,768]{1,0:T(8,128)(2,1)} %bitcast.72, bf16[2048,768]{1,0:T(8,128)(2,1)} %bitcast.74, bf16[768,32]{1,0:T(8,128)(2,1)} %bitcast.81, bf16[768,2048]{1,0:T(8,128)(2,1)} %bitcast.76, bf16[32,2048]{1,0:T(8,128)(2,1)} %bitcast.83), custom_call_target="tpu_custom_call" | custom-call | tf_op jit(solution)/shard_map/expert/pallas_call | solution.py:404
  194.4 1.2 copy-done.13
  196.4 1.5 copy-done.3
  197.9 9.2 %collective-permute-done.7.refs_1_.refs_7_ = bf16[128,2048]{1,0:T(8,128)(2,1)S(1)} collective-permute-done((bf16[128,2048]{1,0:T(8,128)(2,1)}, bf16[128,2048]{1,0:T(8,128)(2,1)S(1)}, u32[]{:S(2)}, u32[]{:S(2)}) %collective-permute-start.7) | collective-permute-done | bytes 524320 | tf_op jit(solution)/shard_map/ppermute | solution.py:464
  207.9 1.5 copy-done.4
  210.2 1.4 copy-done.1
  211.6 4.4 %all-to-all-start.6 = ((bf16[8,72,2176]{2,1,0:T(8,128)(2,1)}), bf16[8,72,2176]{2,1,0:T(8,128)(2,1)}, u32[]{:S(2)}, u32[]{:S(2)}) async-start(bf16[8,72,2176]{2,1,0:T(8,128)(2,1)} %bitcast.77), calls=%async_computation.6 | async-start | bytes 5013504 | tf_op jit(solution)/shard_map/all_to_all | solution.py:472
  216.1 4.8 %combine.2 = (bf16[128,2176]{1,0:T(8,128)(2,1)}, bf16[128,2176]{1,0:T(8,128)(2,1)}) custom-call(bf16[576,2176]{1,0:T(8,128)(2,1)} %bitcast.59, bf16[256,576]{1,0:T(8,128)(2,1)} %copy-done.28, bf16[576,2048]{1,0:T(8,128)(2,1)} %copy-done.3, s32[8,256]{1,0:T(8,128)} %copy-done.38), custom_call_target="tpu_custom_call" | custom-call | flops 603979776 | bytes 3407872 | tf_op jit(solution)/shard_map/combine/pallas_call | solution.py:451
  222.6 1.7 back_low.1.refs_0_
  224.3 24.6 %collective-permute-done.9.refs_4_.refs_2_ = bf16[128,2176]{1,0:T(8,128)(2,1)S(1)} collective-permute-done((bf16[128,2176]{1,0:T(8,128)(2,1)}, bf16[128,2176]{1,0:T(8,128)(2,1)S(1)}, u32[]{:S(2)}, u32[]{:S(2)}) %collective-permute-start.9) | collective-permute-done | bytes 557088 | tf_op jit(solution)/shard_map/ppermute | solution.py:464
  249.7 4.8 %combine.3 = (bf16[128,2176]{1,0:T(8,128)(2,1)}, bf16[128,2176]{1,0:T(8,128)(2,1)}) custom-call(bf16[576,2176]{1,0:T(8,128)(2,1)} %bitcast.33.refs_0_.refs_5_, bf16[256,576]{1,0:T(8,128)(2,1)} %copy-done.30, bf16[576,2048]{1,0:T(8,128)(2,1)} %copy-done.4, s32[8,256]{1,0:T(8,128)} %copy-done.40, bf16[128,2176]{1,0:T(8,128)(2,1)} %copy-done.42), custom_call_target="tpu_custom_call" | custom-call | flops 603979776 | bytes 3407872 | tf_op jit(solution)/shard_map/combine/pallas_call | solution.py:451
  255.6 3.0 %gradient.1 = bf16[8,32,2304]{2,1,0:T(8,128)(2,1)} custom-call(bf16[8,32,256]{2,1,0:T(8,128)(2,1)S(1)} %back_low.1.refs_0_, bf16[576,2176]{1,0:T(8,128)(2,1)S(1)} %bitcast.60, bf16[256,576]{1,0:T(8,128)(2,1)S(1)} %copy-done.29, bf16[128,2048]{1,0:T(8,128)(2,1)S(1)} %bitcast.65, bf16[128,2048]{1,0:T(8,128)(2,1)S(1)} %copy-done.10, ...), custom_call_target="tpu_custom_call" | custom-call | flops 536870912 | bytes 2097152 | tf_op jit(solution)/shard_map/gradient/pallas_call | solution.py:367
  258.6 4.0 %all-to-all-start.7 = ((bf16[8,32,2304]{2,1,0:T(8,128)(2,1)}), bf16[8,32,2304]{2,1,0:T(8,128)(2,1)S(1)}, u32[]{:S(2)}, u32[]{:S(2)}) async-start(bf16[8,32,2304]{2,1,0:T(8,128)(2,1)} %gradient.1), calls=%async_computation.7 | async-start | bytes 2359296 | tf_op jit(solution)/shard_map/all_to_all | solution.py:472
  262.7 1.5 collective-permute-start.11
  264.9 1.6 fusion.1.refs_4_
  266.5 23.2 %collective-permute-done.11.refs_3_ = bf16[128,2176]{1,0:T(8,128)(2,1)} collective-permute-done((bf16[128,2176]{1,0:T(8,128)(2,1)}, bf16[128,2176]{1,0:T(8,128)(2,1)}, u32[]{:S(2)}, u32[]{:S(2)}) %collective-permute-start.11) | collective-permute-done | bytes 557088 | tf_op jit(solution)/shard_map/ppermute | solution.py:464
  289.8 3.8 %finish.1 = (bf16[128,2048]{1,0:T(8,128)(2,1)}, f32[8,128]{1,0:T(8,128)}) custom-call(bf16[128,2176]{1,0:T(8,128)(2,1)} %get-tuple-element.31.refs_0_.refs_7_.refs_9_, bf16[128,2176]{1,0:T(8,128)(2,1)} %collective-permute-done.10.refs_1_, bf16[128,2176]{1,0:T(8,128)(2,1)} %copy-done.42, bf16[128,2176]{1,0:T(8,128)(2,1)} %collective-permute-done.11.refs_3_, ...), custom_call_target="tpu_custom_call" | custom-call | tf_op jit(solution)/shard_map/finish/pallas_call | solution.py:555
  293.7 1.2 gradients.1
  (153 shorter events, 17.1 us)
Async XLA Ops:
  0.6 13.9 %copy-start = (s32[1,1024]{1,0:T(1,128)S(1)}, s32[1,1024]{1,0:T(1,128)}, u32[]{:S(2)}) copy-start(s32[1,1024]{1,0:T(1,128)} %param.18) | copy-start | bytes 12292
  0.6 10.6 %copy-start.47 = (bf16[1,128,2048]{2,1,0:T(8,128)(2,1)S(1)}, bf16[1,128,2048]{2,1,0:T(8,128)(2,1)}, u32[]{:S(2)}) copy-start(bf16[1,128,2048]{2,1,0:T(8,128)(2,1)} %param.19) | copy-start | bytes 1572868
  1.6 8.0 %copy-start.43 = (bf16[128,512]{1,0:T(8,128)(2,1)}, bf16[128,512]{1,0:T(8,128)(2,1)S(1)}, u32[]{:S(2)}) copy-start(bf16[128,512]{1,0:T(8,128)(2,1)S(1)} %pad_maximum_fusion.2.refs_1_) | copy-start | bytes 393220
  2.7 20.6 %all-to-all-start = ((bf16[8,128,512]{2,1,0:T(8,128)(2,1)}), bf16[8,128,512]{2,1,0:T(8,128)(2,1)S(1)}, u32[]{:S(2)}, u32[]{:S(2)}) async-start(bf16[8,128,512]{2,1,0:T(8,128)(2,1)} %broadcast_in_dim.24), calls=%async_computation | async-start | bytes 2097152 | tf_op jit(solution)/shard_map/all_to_all | solution.py:472
  7.9 15.4 %copy-start.37 = (bf16[1,128,2048]{2,1,0:T(8,128)(2,1)S(1)}, bf16[1,128,2048]{2,1,0:T(8,128)(2,1)}, u32[]{:S(2)}) copy-start(bf16[1,128,2048]{2,1,0:T(8,128)(2,1)} %param.15) | copy-start | bytes 1572868
  9.6 17.9 %collective-permute-start.2 = (bf16[256,512]{1,0:T(8,128)(2,1)}, bf16[256,512]{1,0:T(8,128)(2,1)S(1)}, u32[]{:S(2)}, u32[]{:S(2)}) collective-permute-start(bf16[256,512]{1,0:T(8,128)(2,1)} %after.10), channel_id=1, source_target_pairs={{0,1},{1,0},{2,3},{3,2},{4,5},{5,4},{6,7},{7,6},{8,9},{9,8},{10,11... | collective-permute-start | bytes 786440 | tf_op jit(solution)/shard_map/ppermute | solution.py:464
  12.0 15.6 %collective-permute-start.1 = (bf16[128,1024]{1,0:T(8,128)(2,1)}, bf16[128,1024]{1,0:T(8,128)(2,1)S(1)}, u32[]{:S(2)}, u32[]{:S(2)}) collective-permute-start(bf16[128,1024]{1,0:T(8,128)(2,1)} %after.9), channel_id=1, source_target_pairs={{0,2},{1,3},{2,0},{3,1},{4,6},{5,7},{6,4},{7,5},{8,10},{9,11},{10,... | collective-permute-start | bytes 786440 | tf_op jit(solution)/shard_map/ppermute | solution.py:464
  29.1 3.9 %copy-start.50 = (s32[1,128,8]{1,2,0:T(8,128)S(1)}, s32[1,128,8]{1,2,0:T(8,128)}, u32[]{:S(2)}) copy-start(s32[1,128,8]{1,2,0:T(8,128)} %param.22) | copy-start | bytes 12292
  29.1 4.3 %copy-start.20 = (bf16[128,2048]{1,0:T(8,128)(2,1)S(1)}, bf16[128,2048]{1,0:T(8,128)(2,1)}, u32[]{:S(2)}) copy-start(bf16[128,2048]{1,0:T(8,128)(2,1)} %copy-done.19) | copy-start | bytes 1572868
  29.1 7.1 %copy-start.51 = (f32[2048]{0:T(1024)S(1)}, f32[2048]{0:T(1024)}, u32[]{:S(2)}) copy-start(f32[2048]{0:T(1024)} %param.21) | copy-start | bytes 24580
  29.1 30.9 %copy-start.33 = (bf16[128,1024]{1,0:T(8,128)(2,1)S(1)}, bf16[128,1024]{1,0:T(8,128)(2,1)}, u32[]{:S(2)}) copy-start(bf16[128,1024]{1,0:T(8,128)(2,1)} %copy-done.32) | copy-start | bytes 786436
  29.1 30.9 %all-to-all-start.1 = ((bf16[8,256,512]{2,1,0:T(8,128)(2,1)}), bf16[8,256,512]{2,1,0:T(8,128)(2,1)S(1)}, u32[]{:S(2)}, u32[]{:S(2)}) async-start(bf16[8,256,512]{2,1,0:T(8,128)(2,1)} %after.11), calls=%async_computation.1 | async-start | bytes 4194304 | tf_op jit(solution)/shard_map/all_to_all | solution.py:472
  33.4 26.6 %collective-permute-start = (bf16[128,2048]{1,0:T(8,128)(2,1)S(1)}, bf16[128,2048]{1,0:T(8,128)(2,1)}, u32[]{:S(2)}, u32[]{:S(2)}) collective-permute-start(bf16[128,2048]{1,0:T(8,128)(2,1)S(1)} %copy-done.20), channel_id=1, source_target_pairs={{0,2},{1,3},{2,0},{3,1},{4,6},{5,7},{6,4},{7,5},{8,10},{9,11},{10,... | collective-permute-start | bytes 1572872 | tf_op jit(solution)/shard_map/ppermute | solution.py:464
  66.0 4.0 %copy-start.6 = (bf16[288,1024]{1,0:T(8,128)(2,1)S(1)}, bf16[288,1024]{1,0:T(8,128)(2,1)}, u32[]{:S(2)}) copy-start(bf16[288,1024]{1,0:T(8,128)(2,1)} %copy-done.5) | copy-start | bytes 1769476
  66.1 34.3 %all-to-all-start.2 = ((bf16[8,32,2048]{2,1,0:T(8,128)(2,1)}), bf16[8,32,2048]{2,1,0:T(8,128)(2,1)S(1)}, u32[]{:S(2)}, u32[]{:S(2)}) async-start(bf16[8,32,2048]{2,1,0:T(8,128)(2,1)} %after.12), calls=%async_computation.2 | async-start | bytes 2097152 | tf_op jit(solution)/shard_map/all_to_all | solution.py:472
  70.0 29.3 %collective-permute-start.3 = (bf16[288,1024]{1,0:T(8,128)(2,1)S(1)}, bf16[288,1024]{1,0:T(8,128)(2,1)S(1)}, u32[]{:S(2)}, u32[]{:S(2)}) collective-permute-start(bf16[288,1024]{1,0:T(8,128)(2,1)S(1)} %copy-done.6), channel_id=1, source_target_pairs={{0,2},{1,3},{2,0},{3,1},{4,6},{5,7},{6,4},{7,5},{8,10},{9,11},{10,... | collective-permute-start | bytes 1769480 | tf_op jit(solution)/shard_map/ppermute | solution.py:464
  100.4 94.0 %copy-start.38 = (s32[8,256]{1,0:T(8,128)}, s32[8,256]{1,0:T(8,128)S(1)}, u32[]{:S(2)}) copy-start(s32[8,256]{1,0:T(8,128)S(1)} %get-tuple-element.24.refs_1_.refs_0_.refs_3_) | copy-start | bytes 24580
  102.6 38.1 %all-to-all-start.3 = ((bf16[8,72,2048]{2,1,0:T(8,128)(2,1)}), bf16[8,72,2048]{2,1,0:T(8,128)(2,1)}, u32[]{:S(2)}, u32[]{:S(2)}) async-start(bf16[8,72,2048]{2,1,0:T(8,128)(2,1)} %bitcast.20), calls=%async_computation.3 | async-start | bytes 4718592 | tf_op jit(solution)/shard_map/all_to_all | solution.py:472
  107.0 18.3 %collective-permute-start.5 = (bf16[288,1024]{1,0:T(8,128)(2,1)}, bf16[288,1024]{1,0:T(8,128)(2,1)S(1)}, u32[]{:S(2)}, u32[]{:S(2)}) collective-permute-start(bf16[288,1024]{1,0:T(8,128)(2,1)} %after.13), channel_id=1, source_target_pairs={{0,3},{1,2},{2,1},{3,0},{4,7},{5,6},{6,5},{7,4},{8,11},{9,10},{10,... | collective-permute-start | bytes 1769480 | tf_op jit(solution)/shard_map/ppermute | solution.py:464
  109.6 27.8 %collective-permute-start.4 = (bf16[288,1024]{1,0:T(8,128)(2,1)}, bf16[288,1024]{1,0:T(8,128)(2,1)S(1)}, u32[]{:S(2)}, u32[]{:S(2)}) collective-permute-start(bf16[288,1024]{1,0:T(8,128)(2,1)} %after.13), channel_id=1, source_target_pairs={{0,1},{1,0},{2,3},{3,2},{4,5},{5,4},{6,7},{7,6},{8,9},{9,8},{10,11... | collective-permute-start | bytes 1769480 | tf_op jit(solution)/shard_map/ppermute | solution.py:464
  125.3 15.4 %copy-start.16 = (bf16[288,1024]{1,0:T(8,128)(2,1)}, bf16[288,1024]{1,0:T(8,128)(2,1)S(1)}, u32[]{:S(2)}) copy-start(bf16[288,1024]{1,0:T(8,128)(2,1)S(1)} %collective-permute-done.5.refs_2_.refs_4_) | copy-start | bytes 1769476
  138.4 83.0 %copy-start.40 = (s32[8,256]{1,0:T(8,128)}, s32[8,256]{1,0:T(8,128)S(1)}, u32[]{:S(2)}) copy-start(s32[8,256]{1,0:T(8,128)S(1)} %get-tuple-element.28.refs_1_.refs_0_.refs_3_.refs_5_) | copy-start | bytes 24580
  140.7 4.0 %copy-start.7 = (bf16[1,128,2048]{2,1,0:T(8,128)(2,1)S(1)}, bf16[1,128,2048]{2,1,0:T(8,128)(2,1)}, u32[]{:S(2)}) copy-start(bf16[1,128,2048]{2,1,0:T(8,128)(2,1)} %param.29) | copy-start | bytes 1572868
  140.7 33.5 %all-to-all-start.5 = ((bf16[8,72,2048]{2,1,0:T(8,128)(2,1)}), bf16[8,72,2048]{2,1,0:T(8,128)(2,1)S(1)}, u32[]{:S(2)}, u32[]{:S(2)}) async-start(bf16[8,72,2048]{2,1,0:T(8,128)(2,1)} %bitcast.30), calls=%async_computation.5 | async-start | bytes 4718592 | tf_op jit(solution)/shard_map/all_to_all | solution.py:472
  145.5 26.7 %collective-permute-start.6 = (bf16[128,2048]{1,0:T(8,128)(2,1)}, bf16[128,2048]{1,0:T(8,128)(2,1)S(1)}, u32[]{:S(2)}, u32[]{:S(2)}) collective-permute-start(bf16[128,2048]{1,0:T(8,128)(2,1)} %after.14), channel_id=1, source_target_pairs={{0,2},{1,3},{2,0},{3,1},{4,6},{5,7},{6,4},{7,5},{8,10},{9,11},{10,... | collective-permute-start | bytes 1572872 | tf_op jit(solution)/shard_map/ppermute | solution.py:464
  175.6 34.6 %all-to-all-start.4 = ((bf16[8,72,2176]{2,1,0:T(8,128)(2,1)}), bf16[8,72,2176]{2,1,0:T(8,128)(2,1)S(1)}, u32[]{:S(2)}, u32[]{:S(2)}) async-start(bf16[8,72,2176]{2,1,0:T(8,128)(2,1)} %bitcast.78), calls=%async_computation.4 | async-start | bytes 5013504 | tf_op jit(solution)/shard_map/all_to_all | solution.py:472
  180.2 17.7 %collective-permute-start.8 = (bf16[128,2048]{1,0:T(8,128)(2,1)}, bf16[128,2048]{1,0:T(8,128)(2,1)S(1)}, u32[]{:S(2)}, u32[]{:S(2)}) collective-permute-start(bf16[128,2048]{1,0:T(8,128)(2,1)} %after.16), channel_id=1, source_target_pairs={{0,3},{1,2},{2,1},{3,0},{4,7},{5,6},{6,5},{7,4},{8,11},{9,10},{10,... | collective-permute-start | bytes 1572872 | tf_op jit(solution)/shard_map/ppermute | solution.py:464
  181.8 25.2 %collective-permute-start.7 = (bf16[128,2048]{1,0:T(8,128)(2,1)}, bf16[128,2048]{1,0:T(8,128)(2,1)S(1)}, u32[]{:S(2)}, u32[]{:S(2)}) collective-permute-start(bf16[128,2048]{1,0:T(8,128)(2,1)} %after.16), channel_id=1, source_target_pairs={{0,1},{1,0},{2,3},{3,2},{4,5},{5,4},{6,7},{7,6},{8,9},{9,8},{10,11... | collective-permute-start | bytes 1572872 | tf_op jit(solution)/shard_map/ppermute | solution.py:464
  181.8 12.6 %copy-start.9 = (bf16[128,2048]{1,0:T(8,128)(2,1)S(1)}, bf16[128,2048]{1,0:T(8,128)(2,1)}, u32[]{:S(2)}) copy-start(bf16[128,2048]{1,0:T(8,128)(2,1)} %copy-done.8) | copy-start | bytes 1572868
  197.9 10.0 %copy-start.21 = (bf16[128,2048]{1,0:T(8,128)(2,1)}, bf16[128,2048]{1,0:T(8,128)(2,1)S(1)}, u32[]{:S(2)}) copy-start(bf16[128,2048]{1,0:T(8,128)(2,1)S(1)} %collective-permute-done.8.refs_2_.refs_8_) | copy-start | bytes 1572868
  211.6 37.2 %all-to-all-start.6 = ((bf16[8,72,2176]{2,1,0:T(8,128)(2,1)}), bf16[8,72,2176]{2,1,0:T(8,128)(2,1)}, u32[]{:S(2)}, u32[]{:S(2)}) async-start(bf16[8,72,2176]{2,1,0:T(8,128)(2,1)} %bitcast.77), calls=%async_computation.6 | async-start | bytes 5013504 | tf_op jit(solution)/shard_map/all_to_all | solution.py:472
  216.0 5.5 %copy-start.10 = (bf16[128,2048]{1,0:T(8,128)(2,1)S(1)}, bf16[128,2048]{1,0:T(8,128)(2,1)}, u32[]{:S(2)}) copy-start(bf16[128,2048]{1,0:T(8,128)(2,1)} %copy-done.8) | copy-start | bytes 1572868
  216.0 5.4 %copy-start.12 = (bf16[8,32,2048]{2,1,0:T(8,128)(2,1)S(1)}, bf16[8,32,2048]{2,1,0:T(8,128)(2,1)}, u32[]{:S(2)}) copy-start(bf16[8,32,2048]{2,1,0:T(8,128)(2,1)} %copy-done.11) | copy-start | bytes 3145732
  216.0 5.4 %copy-start.22 = (bf16[128,2048]{1,0:T(8,128)(2,1)S(1)}, bf16[128,2048]{1,0:T(8,128)(2,1)}, u32[]{:S(2)}) copy-start(bf16[128,2048]{1,0:T(8,128)(2,1)} %copy-done.21) | copy-start | bytes 1572868
  216.1 5.4 %copy-start.25 = (bf16[128,2048]{1,0:T(8,128)(2,1)S(1)}, bf16[128,2048]{1,0:T(8,128)(2,1)}, u32[]{:S(2)}) copy-start(bf16[128,2048]{1,0:T(8,128)(2,1)} %copy-done.24) | copy-start | bytes 1572868
  216.1 5.4 %copy-start.39 = (s32[8,256]{1,0:T(8,128)S(1)}, s32[8,256]{1,0:T(8,128)}, u32[]{:S(2)}) copy-start(s32[8,256]{1,0:T(8,128)} %copy-done.38) | copy-start | bytes 24580
  220.9 27.9 %collective-permute-start.9 = (bf16[128,2176]{1,0:T(8,128)(2,1)}, bf16[128,2176]{1,0:T(8,128)(2,1)S(1)}, u32[]{:S(2)}, u32[]{:S(2)}) collective-permute-start(bf16[128,2176]{1,0:T(8,128)(2,1)} %get-tuple-element.34), channel_id=1, source_target_pairs={{0,2},{1,3},{2,0},{3,1},{4,6},{5,7},{6,4},{7,5},{8,10},{9,11},{10,... | collective-permute-start | bytes 1671176 | tf_op jit(solution)/shard_map/ppermute | solution.py:464
  249.6 4.9 %copy-start.2 = (bf16[8,72,2176]{2,1,0:T(8,128)(2,1)S(1)}, bf16[8,72,2176]{2,1,0:T(8,128)(2,1)}, u32[]{:S(2)}) copy-start(bf16[8,72,2176]{2,1,0:T(8,128)(2,1)} %copy-done.1) | copy-start | bytes 7520260
  249.6 4.9 %copy-start.23 = (bf16[128,2048]{1,0:T(8,128)(2,1)S(1)}, bf16[128,2048]{1,0:T(8,128)(2,1)}, u32[]{:S(2)}) copy-start(bf16[128,2048]{1,0:T(8,128)(2,1)} %copy-done.21) | copy-start | bytes 1572868
  249.6 4.9 %copy-start.26 = (bf16[128,2048]{1,0:T(8,128)(2,1)S(1)}, bf16[128,2048]{1,0:T(8,128)(2,1)}, u32[]{:S(2)}) copy-start(bf16[128,2048]{1,0:T(8,128)(2,1)} %copy-done.24) | copy-start | bytes 1572868
  249.6 4.9 %copy-start.29 = (bf16[256,576]{1,0:T(8,128)(2,1)S(1)}, bf16[256,576]{1,0:T(8,128)(2,1)}, u32[]{:S(2)}) copy-start(bf16[256,576]{1,0:T(8,128)(2,1)} %copy-done.28) | copy-start | bytes 884740
  249.7 4.9 %copy-start.31 = (bf16[256,576]{1,0:T(8,128)(2,1)S(1)}, bf16[256,576]{1,0:T(8,128)(2,1)}, u32[]{:S(2)}) copy-start(bf16[256,576]{1,0:T(8,128)(2,1)} %copy-done.30) | copy-start | bytes 884740
  258.6 4.0 %copy-start.36 = (bf16[128,2176]{1,0:T(8,128)(2,1)S(1)}, bf16[128,2176]{1,0:T(8,128)(2,1)}, u32[]{:S(2)}) copy-start(bf16[128,2176]{1,0:T(8,128)(2,1)} %get-tuple-element.35.refs_9_) | copy-start | bytes 1671172
  258.6 35.0 %copy-start.14 = (bf16[576,768]{1,0:T(8,128)(2,1)S(1)}, bf16[576,768]{1,0:T(8,128)(2,1)}, u32[]{:S(2)}) copy-start(bf16[576,768]{1,0:T(8,128)(2,1)} %get-tuple-element.30.refs_3_.refs_1_) | copy-start | bytes 2654212
  258.6 35.0 %copy-start.34 = (bf16[576,768]{1,0:T(8,128)(2,1)S(1)}, bf16[576,768]{1,0:T(8,128)(2,1)}, u32[]{:S(2)}) copy-start(bf16[576,768]{1,0:T(8,128)(2,1)} %get-tuple-element.40.refs_0_) | copy-start | bytes 2654212
  258.6 35.0 %all-to-all-start.7 = ((bf16[8,32,2304]{2,1,0:T(8,128)(2,1)}), bf16[8,32,2304]{2,1,0:T(8,128)(2,1)S(1)}, u32[]{:S(2)}, u32[]{:S(2)}) async-start(bf16[8,32,2304]{2,1,0:T(8,128)(2,1)} %gradient.1), calls=%async_computation.7 | async-start | bytes 2359296 | tf_op jit(solution)/shard_map/all_to_all | solution.py:472
  262.7 27.1 %collective-permute-start.10 = (bf16[128,2176]{1,0:T(8,128)(2,1)S(1)}, bf16[128,2176]{1,0:T(8,128)(2,1)}, u32[]{:S(2)}, u32[]{:S(2)}) collective-permute-start(bf16[128,2176]{1,0:T(8,128)(2,1)S(1)} %copy-done.36), channel_id=1, source_target_pairs={{0,1},{1,0},{2,3},{3,2},{4,5},{5,4},{6,7},{7,6},{8,9},{9,8},{10,11... | collective-permute-start | bytes 1671176 | tf_op jit(solution)/shard_map/ppermute | solution.py:464
  262.7 26.9 %collective-permute-start.11 = (bf16[128,2176]{1,0:T(8,128)(2,1)}, bf16[128,2176]{1,0:T(8,128)(2,1)}, u32[]{:S(2)}, u32[]{:S(2)}) collective-permute-start(bf16[128,2176]{1,0:T(8,128)(2,1)} %get-tuple-element.36), channel_id=1, source_target_pairs={{0,3},{1,2},{2,1},{3,0},{4,7},{5,6},{6,5},{7,4},{8,11},{9,10},{10,... | collective-permute-start | bytes 1671176 | tf_op jit(solution)/shard_map/ppermute | solution.py:464
  (24 other events, 41.6 us)

commit v4 on v3

--- a/solution.py
+++ b/solution.py
@@ -134,14 +134,20 @@
     routing = routing_ref[...]
     picks = routing.shape[0] // 2
     gates = routing[:picks].astype(BF16).astype(F32)
-    rest = outs[0].shape[0] - blocks * tokens - 3 * picks - 2 * blocks
-    rest = [jnp.zeros((rest, tokens), F32)] if rest else []
-    outs[0][blocks * tokens :, tokens:] = jnp.zeros(
-        (outs[0].shape[0] - blocks * tokens, outs[0].shape[1] - tokens), BF16
-    )
-    outs[0][blocks * tokens :, :tokens] = jnp.concatenate(
-        [gates, routing[:picks] - gates, routing[picks:], high, square - high, *rest], axis=0
-    ).astype(BF16)
+    rest = jnp.zeros((8 - blocks, tokens), F32)
+    table = jnp.concatenate(
+        [
+            jnp.concatenate([gates, routing[:picks] - gates], axis=0),
+            jnp.concatenate([routing[picks:], jnp.zeros((picks, tokens), F32)], axis=0),
+            jnp.concatenate([high, rest, square - high, rest], axis=0),
+        ],
+        axis=1,
+    )
+    wide = table.shape[1]
+    out_ref = outs[0]
+    out_ref[blocks * tokens :, :wide] = table.astype(BF16)
+    if wide < out_ref.shape[1]:
+        out_ref[blocks * tokens :, wide:] = jnp.zeros((16, out_ref.shape[1] - wide), BF16)
 
 
 def project(attended, residuals, own_weight, pair_weight, gain, routing, chunks):
@@ -149,8 +155,7 @@
     tokens, width = attended[0].shape
     cols = own_weight.shape[1]
     rows = blocks * tokens
-    more = 3 * routing.shape[0] // 2 + 2 * blocks
-    more = -(-more // 16) * 16
+    more = 16
     return pl.pallas_call(
         lambda *refs: project_kernel(*refs, blocks=blocks, chunks=chunks),
         in_specs=[vmem()] * (2 * blocks + 4),
@@ -178,15 +183,17 @@
 
 
 def route_kernel(column_ref, *refs, capacity, picks, columns, width):
-    blocks = refs[:-4]
-    slot_ref, gate_ref, weight_ref, inverse_ref = refs[-4:]
+    blocks = refs[:-3]
+    slot_ref, gate_ref, inverse_ref = refs[-3:]
     groups, near = slot_ref.shape
     count = len(blocks)
     tokens = near // count
-    tables = [block[near:, :tokens].astype(F32) for block in blocks]
-    table = jnp.concatenate(tables, axis=1)
-    probs = table[:picks] + table[picks : 2 * picks]
-    ids = table[2 * picks : 3 * picks].astype(jnp.int32)
+    tables = [block[near:, :].astype(F32) for block in blocks]
+    probs = jnp.concatenate([x[:, :tokens] for x in tables], axis=1)
+    probs = probs[:picks] + probs[picks : 2 * picks]
+    ids = jnp.concatenate([x[:picks, tokens : 2 * tokens] for x in tables], axis=1)
+    ids = ids.astype(jnp.int32)
+    squares = [x[:, 2 * tokens : 3 * tokens] for x in tables]
     member, gates = [], []
     for group in range(groups):
         hit = ids == group * columns + column_ref[0]
@@ -200,21 +207,12 @@
     slots = jnp.where(member > 0.0, ranks, capacity)
     slot_ref[...] = slots
     gate_ref[...] = jnp.concatenate(gates, axis=0)
-    places = lax.broadcasted_iota(jnp.int32, (capacity, near), 0)
-    weights = [
-        jnp.where(places == slots[group : group + 1], gates[group], 0.0) for group in range(groups)
-    ]
-    rows = groups * capacity
-    if rows % 128:
-        weights.append(jnp.zeros((-rows % 128, near), F32))
-    weight_ref[...] = jnp.concatenate(weights, axis=0).T[:, :rows].astype(BF16)
     inverses = []
     for b in range(count):
         total = jnp.zeros((1, tokens), F32)
         for i in range(count):
-            row = 3 * picks + (i ^ b)
-            total += tables[i][row : row + 1]
-            total += tables[i][count + row : count + row + 1]
+            row = i ^ b
+            total += squares[i][row : row + 1] + squares[i][8 + row : 9 + row]
         inverses.append(lax.rsqrt(total / width + norm_eps))
     inverse_ref[...] = jnp.concatenate(inverses, axis=1)
 
@@ -226,11 +224,10 @@
             *refs, capacity=capacity, picks=picks, columns=columns, width=width
         ),
         in_specs=[smem()] + [vmem()] * len(blocks),
-        out_specs=[vmem()] * 4,
+        out_specs=[vmem()] * 3,
         out_shape=[
             jax.ShapeDtypeStruct((groups, near), jnp.int32),
             jax.ShapeDtypeStruct((groups, near), F32),
-            jax.ShapeDtypeStruct((near, groups * capacity), BF16),
             jax.ShapeDtypeStruct((1, near), F32),
         ],
         compiler_params=params(),
@@ -273,24 +270,36 @@
     )(first.reshape(1), slots, inverse, *blocks, *earlier)
 
 
-def fill_kernel(slot_ref, *refs, capacity):
-    blocks, out_ref = refs[:-1], refs[-1]
+def fill_kernel(slot_ref, gate_ref, *refs, capacity):
+    blocks, out_ref, weight_ref = refs[:-2], refs[-2], refs[-1]
     rows = jnp.concatenate([block[...] for block in blocks], axis=0)
-    out_ref[...] = dot(hits_of(slot_ref[...], capacity).astype(BF16), rows).astype(BF16)
-
-
-def fill(slots, blocks, capacity, earlier):
+    hits = hits_of(slot_ref[...], capacity)
+    out_ref[...] = dot(hits.astype(BF16), rows).astype(BF16)
+    count, near = hits.shape
+    gates = [
+        hits[group * capacity : (group + 1) * capacity] * gate_ref[group : group + 1, :]
+        for group in range(gate_ref.shape[0])
+    ]
+    if count % 128:
+        gates.append(jnp.zeros((-count % 128, near), F32))
+    weight_ref[...] = jnp.concatenate(gates, axis=0).T[:, :count].astype(BF16)
+
+
+def fill(slots, gates, blocks, capacity, earlier):
     groups, near = slots.shape
     rows, cols = groups * capacity, blocks[0].shape[1]
     return pl.pallas_call(
-        lambda *refs: fill_kernel(*refs[: 1 + len(blocks)], refs[-1], capacity=capacity),
-        in_specs=[vmem()] * (1 + len(blocks)) + [anywhere()],
-        out_specs=vmem(),
-        out_shape=jax.ShapeDtypeStruct((rows, cols), BF16),
+        lambda *refs: fill_kernel(*refs[: 2 + len(blocks)], *refs[-2:], capacity=capacity),
+        in_specs=[vmem()] * (2 + len(blocks)) + [anywhere()],
+        out_specs=[vmem()] * 2,
+        out_shape=[
+            jax.ShapeDtypeStruct((rows, cols), BF16),
+            jax.ShapeDtypeStruct((near, rows), BF16),
+        ],
         compiler_params=params(),
         cost_estimate=cost(2 * rows * near * cols, 2 * rows * cols),
         name="fill",
-    )(slots, *blocks, earlier)
+    )(slots, gates, *blocks, earlier)
 
 
 def back_kernel(factor_ref, *refs, capacity, count):
@@ -415,7 +424,7 @@
             jax.ShapeDtypeStruct((count, units), BF16),
             jax.ShapeDtypeStruct((count, width + 128), BF16),
         ],
-        compiler_params=params(56),
+        compiler_params=params(40),
         cost_estimate=cost(0, 0),
         name="expert",
     )(rows, *weights, *earlier)
@@ -453,7 +462,7 @@
         in_specs=[vmem()] * 4 + [anywhere()] * len(earlier),
         out_specs=[vmem()] * blocks,
         out_shape=[jax.ShapeDtypeStruct((near // blocks, cols + 128), BF16)] * blocks,
-        compiler_params=params(56),
+        compiler_params=params(40),
         cost_estimate=cost(2 * rows * near * cols, 2 * cols * (rows + near)),
         name="combine",
     )(back, weights, upstream, slots, *earlier)
@@ -470,11 +479,6 @@
 
 def swap(x):
     return lax.all_to_all(x, "seq", split_axis=0, concat_axis=0, tiled=True)
-
-
-def spread(x):
-    count = lax.axis_size("seq")
-    return swap(jnp.broadcast_to(x[None], (count,) + x.shape)).reshape(-1, x.shape[-1])
 
 
 def after(x, *earlier):
@@ -560,7 +564,7 @@
             jax.ShapeDtypeStruct((tokens, pieces[0].shape[1] - 128), BF16),
             jax.ShapeDtypeStruct(probs.shape[::-1], F32),
         ],
-        compiler_params=params(56),
+        compiler_params=params(40),
         name="finish",
     )(*pieces, probs, ids, names, earlier)
 
@@ -594,7 +598,8 @@
     block = width // columns
 
     kv_own = jnp.concatenate([keys[0], values[0]], axis=1)
-    kv_all = spread(kv_own)
+    kv_own = jnp.broadcast_to(kv_own[None], (seq_devices,) + kv_own.shape)
+    kv_all = swap(kv_own).reshape(seq_devices * tokens, -1)
     share = output_projection.shape[0] // seq_devices
     pair_share = after(
         lax.dynamic_slice_in_dim(output_projection, place * share, share, 0), kv_own
@@ -610,8 +615,9 @@
     residuals = [residuals[0]] + [
         from_plane(after(residuals[r // 2], kv_own), r) for r in range(2, columns, 2)
     ]
-    attended = attend(queries[0], kv_all, document_index[0], ())
     pair_share = jnp.broadcast_to(pair_share[None], (seq_devices,) + pair_share.shape)
+    up_wide = jnp.broadcast_to(adapter_up[0][None], (seq_devices, rank, width))
+    attended = attend(queries[0], kv_all, document_index[0], (pair_share, up_wide))
     pair_projection = swap(after(pair_share, attended, *residuals[1:]))
     pair_projection = pair_projection.reshape(-1, block)
     attended = [attended] + [from_plane(attended, r) for r in range(2, columns, 2)]
@@ -627,8 +633,7 @@
         [(0, block)],
     )[0]
     capacity = columns // 2 * (9 * tokens * PICKS_PER_TOKEN // (8 * experts))
-    up_factors = jnp.broadcast_to(adapter_up[0][None], (seq_devices, rank, width))
-    up_factors = swap(after(up_factors, scaled)).reshape(-1, width)
+    up_factors = swap(after(up_wide, scaled)).reshape(-1, width)
     even = range(2, columns, 2)
     odd = range(1, columns, 2)
     crossed = {0: scaled, **{r: from_plane(scaled, r) for r in even}}
@@ -643,13 +648,13 @@
     halves = []
     for half in range(2):
         blocks = [crossed[r] for r in range(half, columns, 2)]
-        slots, gates, weights, inverse = route(
+        slots, gates, inverse = route(
             column, blocks, seq_devices, capacity, tokens, PICKS_PER_TOKEN, columns, width
         )
         earlier = (up_factors,) if half == 0 else ()
         rows = swap(pick(column ^ half, slots, inverse, blocks, capacity, earlier))
         cotangents = [upstream[r] for r in range(half, columns, 2)]
-        halves.append((slots, gates, weights, rows, cotangents))
+        halves.append((slots, gates, rows, cotangents))
     made = [
         expert(
             rows,
@@ -660,30 +665,33 @@
             adapter_up[0],
             (),
         )
-        for half, (_, _, _, rows, cotangents) in enumerate(halves)
+        for _, _, rows, _ in halves
     ]
 
     filled = [
-        fill(slots, cotangents, capacity, made[1][0]) for slots, _, _, _, cotangents in halves
+        fill(slots, gates, cotangents, capacity, made[1][0])
+        for slots, gates, _, cotangents in halves
     ]
     backs, pieces, earlier = [], {}, ()
-    for half, (slots, _, weights, _, _) in enumerate(halves):
-        sent = after(made[half][1], *(filled if half else [upstream[r] for r in even]))
+    for half, (slots, _, _, _) in enumerate(halves):
+        earlier_sent = [x[0] for x in filled] if half else [upstream[r] for r in even]
+        sent = after(made[half][1], *earlier_sent)
         backs.append(swap(sent))
-        sums = combine(backs[half], weights, filled[half], slots, columns // 2, earlier)
+        rows, weights = filled[half]
+        sums = combine(backs[half], weights, rows, slots, columns // 2, earlier)
         planes = range(half, columns, 2)
         pieces.update({r: from_plane(x, r) if r else x for r, x in zip(planes, sums)})
         earlier = tuple(pieces[r] for r in planes if r)
 
     back_slots = back_slots_of(
         up_factors,
-        [(slots, gates, cotangents) for slots, gates, _, _, cotangents in halves],
+        [(slots, gates, cotangents) for slots, gates, _, cotangents in halves],
         capacity,
         pieces[0],
     )
     parts = gradient_parts(
         back_slots,
-        [(back, half[2], half[4]) for back, half in zip(backs, halves)],
+        [(back, fills[1], half[3]) for back, fills, half in zip(backs, filled, halves)],
         sums[0],
     )
     up_factor_gradient, down_factor_gradient = adapter_gradients(
@@ -700,7 +708,7 @@
         routed_experts[0],
         names.reshape(1, experts),
         seq_devices,
-        pieces[0],
+        up_factor_gradient,
     )
     return (
         combined_output[None],

time: 296 us -> 289 us (0.976)
  local copies, waits for them, and re-layouts: 24.5 us -> 37.5 us
  waiting for transfers between devices: 159 us -> 148 us
  Pallas kernels: 57.1 us -> 47.1 us
    ppermute x12, waiting for transfers between devices: 149 us -> 110 us  [from_plane(): return lax.ppermute(x, 'expert', [(i, i ^ r) for i in range(size)])]
    all_to_all x8, waiting for transfers between devices: 10.6 us -> 37.5 us  [swap(): return lax.all_to_all(x, 'seq', split_axis=0, concat_axis=0, tiled=True)]
    unnamed x109 -> x117, local copies, waits for them, and re-layouts: 18.2 us -> 33.5 us
    pallas_call x2, Pallas kernels: 25 us -> 18.5 us  [expert(): pl.pallas_call(lambda *refs: expert_kernel(*refs[:6], *refs[-2:]), grid=(...]
    pallas_call x2, Pallas kernels: 9.66 us -> 5.11 us  [combine(): pl.pallas_call(lambda *refs: combine_kernel(*refs[:4], *refs[4 + len(earl...]
  transfers between devices with their start and end apart: 20 -> 20, of which waited for: 12 -> 14; matrix products, arithmetic and copies ran while one was open for 3% -> 4% of each run, Pallas kernels for 15% -> 12%
where the time goes in v4:
time: 289 us; the launch traced here: 288 us
  waiting for transfers between devices  148 us (51%)
  starting transfers between devices  49.7 us (17%)
  Pallas kernels  47.1 us (16%)
  local copies, waits for them, and re-layouts  37.5 us (13%)
  other arithmetic  4.65 us (2%)
    ppermute x12, waiting for transfers between devices, from_plane(): return lax.ppermute(x, 'expert', [(i, i ^ r) for i in range(size)])  110 us
    all_to_all x8, waiting for transfers between devices, swap(): return lax.all_to_all(x, 'seq', split_axis=0, concat_axis=0, tiled=True)  37.5 us
    all_to_all x8, starting transfers between devices, swap(): return lax.all_to_all(x, 'seq', split_axis=0, concat_axis=0, tiled=True)  33.7 us
    unnamed x117, local copies, waits for them, and re-layouts  33.5 us
    pallas_call x2, Pallas kernels, expert(): pl.pallas_call(lambda *refs: expert_kernel(*refs[:6], *refs[-2:]), grid=(...  18.5 us
    ppermute x12, starting transfers between devices, from_plane(): return lax.ppermute(x, 'expert', [(i, i ^ r) for i in range(size)])  16 us
  transfers between devices with their start and end apart: 20, of which 14 were waited for; matrix products, arithmetic and copies ran while one was open for 4% of the time, Pallas kernels for 12%

profile of v4, /device:TPU:0, one launch (start us, length us, event | category | flops | bytes accessed | tf_op | source)
XLA Modules:
  0.0 287.8 jit_solution(5372470339094068016)
XLA Ops:
  2.6 5.3 %all-to-all-start = ((bf16[8,128,512]{2,1,0:T(8,128)(2,1)}), bf16[8,128,512]{2,1,0:T(8,128)(2,1)S(1)}, u32[]{:S(2)}, u32[]{:S(2)}) async-start(bf16[8,128,512]{2,1,0:T(8,128)(2,1)} %broadcast_in_dim.24.refs_1_), calls=%async_computation | async-start | bytes 2097152 | tf_op jit(solution)/shard_map/all_to_all | solution.py:481
  7.9 1.7 constant_dynamic-slice_fusion.refs_0_
  9.6 1.6 collective-permute-start
  12.6 2.6 collective-permute-start.2
  15.3 7.2 %collective-permute-done = bf16[256,512]{1,0:T(8,128)(2,1)S(1)} collective-permute-done((bf16[256,512]{1,0:T(8,128)(2,1)}, bf16[256,512]{1,0:T(8,128)(2,1)S(1)}, u32[]{:S(2)}, u32[]{:S(2)}) %collective-permute-start) | collective-permute-done | bytes 262176 | tf_op jit(solution)/shard_map/ppermute | solution.py:473
  23.6 3.5 %attend.1.refs_1_.refs_0_ = bf16[128,2048]{1,0:T(8,128)(2,1)S(1)} custom-call(s32[1]{0:T(128)} %bitcast.1.start_ref, bf16[128,2048]{1,0:T(8,128)(2,1)S(1)} %bitcast.83, bf16[1024,512]{1,0:T(8,128)(2,1)S(1)} %bitcast.76, f32[128,640]{1,0:T(8,128)S(1)} %and_select_fusion.bias_ref, bf16[8,256,512]{2,1,0:T(8,128)(2,1)S(1)} %broadcast_in_dim.27.refs_0_, ...), custom_call_target="tpu_custom_call" | custom-call | tf_op jit(solution)/shard_map/attend/pallas_call | solution.py:73
  28.7 3.8 %all-to-all-start.1 = ((bf16[8,256,512]{2,1,0:T(8,128)(2,1)}), bf16[8,256,512]{2,1,0:T(8,128)(2,1)S(1)}, u32[]{:S(2)}, u32[]{:S(2)}) async-start(bf16[8,256,512]{2,1,0:T(8,128)(2,1)} %after.11), calls=%async_computation.1 | async-start | bytes 4194304 | tf_op jit(solution)/shard_map/all_to_all | solution.py:481
  33.1 2.6 collective-permute-start.1
  36.8 22.9 %collective-permute-done.1.refs_1_ = bf16[128,2048]{1,0:T(8,128)(2,1)} collective-permute-done((bf16[128,2048]{1,0:T(8,128)(2,1)S(1)}, bf16[128,2048]{1,0:T(8,128)(2,1)}, u32[]{:S(2)}, u32[]{:S(2)}) %collective-permute-start.1) | collective-permute-done | bytes 524320 | tf_op jit(solution)/shard_map/ppermute | solution.py:473
  59.7 1.6 copy-done.26
  61.3 2.4 project.1.refs_1_.refs_3_.refs_0_
  64.6 4.0 %all-to-all-start.2 = ((bf16[8,32,2048]{2,1,0:T(8,128)(2,1)}), bf16[8,32,2048]{2,1,0:T(8,128)(2,1)S(1)}, u32[]{:S(2)}, u32[]{:S(2)}) async-start(bf16[8,32,2048]{2,1,0:T(8,128)(2,1)} %after.12), calls=%async_computation.2 | async-start | bytes 2097152 | tf_op jit(solution)/shard_map/all_to_all | solution.py:481
  68.6 1.7 collective-permute-start.3
  70.2 26.4 %collective-permute-done.3.refs_2_.refs_4_.refs_1_ = bf16[272,1024]{1,0:T(8,128)(2,1)S(1)} collective-permute-done((bf16[272,1024]{1,0:T(8,128)(2,1)}, bf16[272,1024]{1,0:T(8,128)(2,1)S(1)}, u32[]{:S(2)}, u32[]{:S(2)}) %collective-permute-start.3) | collective-permute-done | bytes 557088 | tf_op jit(solution)/shard_map/ppermute | solution.py:473
  96.8 2.2 pick.2
  99.0 3.8 %all-to-all-start.3 = ((bf16[8,72,2048]{2,1,0:T(8,128)(2,1)}), bf16[8,72,2048]{2,1,0:T(8,128)(2,1)S(1)}, u32[]{:S(2)}, u32[]{:S(2)}) async-start(bf16[8,72,2048]{2,1,0:T(8,128)(2,1)} %bitcast.20), calls=%async_computation.3 | async-start | bytes 4718592 | tf_op jit(solution)/shard_map/all_to_all | solution.py:481
  102.8 2.5 collective-permute-start.5
  105.3 15.1 %collective-permute-done.5.refs_2_.refs_4_ = bf16[272,1024]{1,0:T(8,128)(2,1)S(1)} collective-permute-done((bf16[272,1024]{1,0:T(8,128)(2,1)}, bf16[272,1024]{1,0:T(8,128)(2,1)S(1)}, u32[]{:S(2)}, u32[]{:S(2)}) %collective-permute-start.5) | collective-permute-done | bytes 557088 | tf_op jit(solution)/shard_map/ppermute | solution.py:473
  120.4 11.5 %collective-permute-done.4.refs_1_.refs_3_ = bf16[272,1024]{1,0:T(8,128)(2,1)S(1)} collective-permute-done((bf16[272,1024]{1,0:T(8,128)(2,1)}, bf16[272,1024]{1,0:T(8,128)(2,1)S(1)}, u32[]{:S(2)}, u32[]{:S(2)}) %collective-permute-start.4) | collective-permute-done | bytes 557088 | tf_op jit(solution)/shard_map/ppermute | solution.py:473
  132.8 2.2 pick.3
  136.4 4.4 %all-to-all-start.5 = ((bf16[8,72,2048]{2,1,0:T(8,128)(2,1)}), bf16[8,72,2048]{2,1,0:T(8,128)(2,1)}, u32[]{:S(2)}, u32[]{:S(2)}) async-start(bf16[8,72,2048]{2,1,0:T(8,128)(2,1)} %bitcast.30), calls=%async_computation.5 | async-start | bytes 4718592 | tf_op jit(solution)/shard_map/all_to_all | solution.py:481
  140.8 2.0 copy.42.refs_0_
  144.3 1.9 copy-done.7
  146.2 1.7 copy-done.14
  147.9 9.1 %expert.2 = (bf16[576,768]{1,0:T(8,128)(2,1)S(1)}, bf16[576,2176]{1,0:T(8,128)(2,1)S(1)}) custom-call(bf16[576,2048]{1,0:T(8,128)(2,1)S(1)} %bitcast.67, bf16[2048,768]{1,0:T(8,128)(2,1)S(1)} %bitcast.61, bf16[2048,768]{1,0:T(8,128)(2,1)S(1)} %bitcast.63, bf16[768,32]{1,0:T(8,128)(2,1)S(1)} %bitcast.77, bf16[768,2048]{1,0:T(8,128)(2,1)} %bitcast.85, ...), custom_call_target="tpu_custom_call" | custom-call | tf_op jit(solution)/shard_map/expert/pallas_call | solution.py:413
  159.3 10.1 %collective-permute-done.6.refs_1_.refs_3_.refs_4_ = bf16[128,2048]{1,0:T(8,128)(2,1)} collective-permute-done((bf16[128,2048]{1,0:T(8,128)(2,1)}, bf16[128,2048]{1,0:T(8,128)(2,1)}, u32[]{:S(2)}, u32[]{:S(2)}) %collective-permute-start.6) | collective-permute-done | bytes 524320 | tf_op jit(solution)/shard_map/ppermute | solution.py:473
  170.2 3.9 %all-to-all-start.4 = ((bf16[8,72,2176]{2,1,0:T(8,128)(2,1)}), bf16[8,72,2176]{2,1,0:T(8,128)(2,1)S(1)}, u32[]{:S(2)}, u32[]{:S(2)}) async-start(bf16[8,72,2176]{2,1,0:T(8,128)(2,1)} %bitcast.66), calls=%async_computation.4 | async-start | bytes 5013504 | tf_op jit(solution)/shard_map/all_to_all | solution.py:481
  175.0 1.6 collective-permute-start.8
  176.6 1.9 copy-done.6
  178.5 1.9 copy-done.8
  180.4 9.5 %expert.3 = (bf16[576,768]{1,0:T(8,128)(2,1)S(1)}, bf16[576,2176]{1,0:T(8,128)(2,1)S(1)}) custom-call(bf16[576,2048]{1,0:T(8,128)(2,1)} %bitcast.31.refs_0_, bf16[2048,768]{1,0:T(8,128)(2,1)S(1)} %bitcast.62, bf16[2048,768]{1,0:T(8,128)(2,1)S(1)} %bitcast.64, bf16[768,32]{1,0:T(8,128)(2,1)S(1)} %bitcast.78, bf16[768,2048]{1,0:T(8,128)(2,1)} %bitcast.86, ...), custom_call_target="tpu_custom_call" | custom-call | tf_op jit(solution)/shard_map/expert/pallas_call | solution.py:413
  191.3 2.2 fill.2
  193.5 1.5 copy-done.11
  195.0 6.8 %collective-permute-done.7.refs_2_.refs_7_ = bf16[128,2048]{1,0:T(8,128)(2,1)S(1)} collective-permute-done((bf16[128,2048]{1,0:T(8,128)(2,1)}, bf16[128,2048]{1,0:T(8,128)(2,1)S(1)}, u32[]{:S(2)}, u32[]{:S(2)}) %collective-permute-start.7) | collective-permute-done | bytes 524320 | tf_op jit(solution)/shard_map/ppermute | solution.py:473
  204.9 4.4 %all-to-all-start.6 = ((bf16[8,72,2176]{2,1,0:T(8,128)(2,1)}), bf16[8,72,2176]{2,1,0:T(8,128)(2,1)}, u32[]{:S(2)}, u32[]{:S(2)}) async-start(bf16[8,72,2176]{2,1,0:T(8,128)(2,1)} %bitcast.65), calls=%async_computation.6 | async-start | bytes 5013504 | tf_op jit(solution)/shard_map/all_to_all | solution.py:481
  209.4 1.7 copy-done.12
  211.0 2.0 combine.2
  214.0 2.8 back_low.1.refs_0_
  217.6 22.8 %all-to-all-done.6 = bf16[8,72,2176]{2,1,0:T(8,128)(2,1)} async-done(((bf16[8,72,2176]{2,1,0:T(8,128)(2,1)}), bf16[8,72,2176]{2,1,0:T(8,128)(2,1)}, u32[]{:S(2)}, u32[]{:S(2)}) %all-to-all-start.6) | async-done | bytes 2506784 | tf_op jit(solution)/shard_map/all_to_all | solution.py:481
  241.1 1.7 copy-done.16
  243.8 3.1 %combine.3 = (bf16[128,2176]{1,0:T(8,128)(2,1)S(1)}, bf16[128,2176]{1,0:T(8,128)(2,1)S(1)}) custom-call(bf16[576,2176]{1,0:T(8,128)(2,1)} %bitcast.33.refs_0_.refs_5_, bf16[256,576]{1,0:T(8,128)(2,1)S(1)} %copy-done.36, bf16[576,2048]{1,0:T(8,128)(2,1)S(1)} %copy-done.16, s32[8,256]{1,0:T(8,128)S(1)} %get-tuple-element.30.refs_1_.refs_0_.refs_3_.refs_5_, ...), custom_call_target="tpu_custom_call" | custom-call | flops 603979776 | bytes 3407872 | tf_op jit(solution)/shard_map/combine/pallas_call | solution.py:460
  247.6 2.2 gradient.1
  251.6 4.0 %all-to-all-start.7 = ((bf16[8,32,2304]{2,1,0:T(8,128)(2,1)}), bf16[8,32,2304]{2,1,0:T(8,128)(2,1)S(1)}, u32[]{:S(2)}, u32[]{:S(2)}) async-start(bf16[8,32,2304]{2,1,0:T(8,128)(2,1)} %copy-done.23), calls=%async_computation.7 | async-start | bytes 2359296 | tf_op jit(solution)/shard_map/all_to_all | solution.py:481
  255.7 1.9 collective-permute-start.11
  257.8 1.6 fusion.1.refs_4_
  259.4 13.1 %all-to-all-done.7.parts_ref = bf16[8,32,2304]{2,1,0:T(8,128)(2,1)S(1)} async-done(((bf16[8,32,2304]{2,1,0:T(8,128)(2,1)}), bf16[8,32,2304]{2,1,0:T(8,128)(2,1)S(1)}, u32[]{:S(2)}, u32[]{:S(2)}) %all-to-all-start.7) | async-done | bytes 1179680 | tf_op jit(solution)/shard_map/all_to_all | solution.py:481
  273.7 9.4 %collective-permute-done.11.refs_3_ = bf16[128,2176]{1,0:T(8,128)(2,1)} collective-permute-done((bf16[128,2176]{1,0:T(8,128)(2,1)}, bf16[128,2176]{1,0:T(8,128)(2,1)}, u32[]{:S(2)}, u32[]{:S(2)}) %collective-permute-start.11) | collective-permute-done | bytes 557088 | tf_op jit(solution)/shard_map/ppermute | solution.py:473
  284.1 3.7 %finish.1 = (bf16[128,2048]{1,0:T(8,128)(2,1)}, f32[8,128]{1,0:T(8,128)}) custom-call(bf16[128,2176]{1,0:T(8,128)(2,1)S(1)} %copy-done.28, bf16[128,2176]{1,0:T(8,128)(2,1)} %collective-permute-done.10.refs_1_, bf16[128,2176]{1,0:T(8,128)(2,1)} %collective-permute-done.9.refs_4_.refs_2_, bf16[128,2176]{1,0:T(8,128)(2,1)} %collective-permute-done.11.refs_3_, ...), custom_call_target="tpu_custom_call" | custom-call | tf_op jit(solution)/shard_map/finish/pallas_call | solution.py:559
  (161 shorter events, 29.5 us)
Async XLA Ops:
  0.6 14.5 %copy-start = (s32[1,1024]{1,0:T(1,128)S(1)}, s32[1,1024]{1,0:T(1,128)}, u32[]{:S(2)}) copy-start(s32[1,1024]{1,0:T(1,128)} %param.18) | copy-start | bytes 12292
  2.6 8.6 %copy-start.52 = (bf16[1,128,2048]{2,1,0:T(8,128)(2,1)S(1)}, bf16[1,128,2048]{2,1,0:T(8,128)(2,1)}, u32[]{:S(2)}) copy-start(bf16[1,128,2048]{2,1,0:T(8,128)(2,1)} %param.19) | copy-start | bytes 1572868
  2.6 20.7 %all-to-all-start = ((bf16[8,128,512]{2,1,0:T(8,128)(2,1)}), bf16[8,128,512]{2,1,0:T(8,128)(2,1)S(1)}, u32[]{:S(2)}, u32[]{:S(2)}) async-start(bf16[8,128,512]{2,1,0:T(8,128)(2,1)} %broadcast_in_dim.24.refs_1_), calls=%async_computation | async-start | bytes 2097152 | tf_op jit(solution)/shard_map/all_to_all | solution.py:481
  9.6 13.7 %copy-start.37 = (bf16[1,32,2048]{2,1,0:T(8,128)(2,1)S(1)}, bf16[1,32,2048]{2,1,0:T(8,128)(2,1)}, u32[]{:S(2)}) copy-start(bf16[1,32,2048]{2,1,0:T(8,128)(2,1)} %param.28) | copy-start | bytes 393220
  9.6 13.0 %collective-permute-start = (bf16[256,512]{1,0:T(8,128)(2,1)}, bf16[256,512]{1,0:T(8,128)(2,1)S(1)}, u32[]{:S(2)}, u32[]{:S(2)}) collective-permute-start(bf16[256,512]{1,0:T(8,128)(2,1)} %after.9), channel_id=1, source_target_pairs={{0,1},{1,0},{2,3},{3,2},{4,5},{5,4},{6,7},{7,6},{8,9},{9,8},{10,11... | collective-permute-start | bytes 786440 | tf_op jit(solution)/shard_map/ppermute | solution.py:473
  12.6 11.0 %copy-start.47 = (bf16[1,128,2048]{2,1,0:T(8,128)(2,1)S(1)}, bf16[1,128,2048]{2,1,0:T(8,128)(2,1)}, u32[]{:S(2)}) copy-start(bf16[1,128,2048]{2,1,0:T(8,128)(2,1)} %param.15) | copy-start | bytes 1572868
  12.6 15.4 %collective-permute-start.2 = (bf16[128,1024]{1,0:T(8,128)(2,1)}, bf16[128,1024]{1,0:T(8,128)(2,1)S(1)}, u32[]{:S(2)}, u32[]{:S(2)}) collective-permute-start(bf16[128,1024]{1,0:T(8,128)(2,1)} %after.10), channel_id=1, source_target_pairs={{0,2},{1,3},{2,0},{3,1},{4,6},{5,7},{6,4},{7,5},{8,10},{9,11},{10,... | collective-permute-start | bytes 786440 | tf_op jit(solution)/shard_map/ppermute | solution.py:473
  23.4 3.7 %copy-start.2 = (bf16[8,32,2048]{2,1,0:T(8,128)(2,1)}, bf16[8,32,2048]{2,1,0:T(8,128)(2,1)S(1)}, u32[]{:S(2)}) copy-start(bf16[8,32,2048]{2,1,0:T(8,128)(2,1)S(1)} %broadcast_in_dim.53.refs_1_.refs_0_) | copy-start | bytes 3145732
  23.6 3.5 %copy-start.1 = (bf16[8,256,512]{2,1,0:T(8,128)(2,1)}, bf16[8,256,512]{2,1,0:T(8,128)(2,1)S(1)}, u32[]{:S(2)}) copy-start(bf16[8,256,512]{2,1,0:T(8,128)(2,1)S(1)} %broadcast_in_dim.27.refs_0_) | copy-start | bytes 6291460
  28.6 3.9 %copy-start.53 = (f32[1,128,8]{1,2,0:T(8,128)S(1)}, f32[1,128,8]{1,2,0:T(8,128)}, u32[]{:S(2)}) copy-start(f32[1,128,8]{1,2,0:T(8,128)} %param.23) | copy-start | bytes 12292
  28.6 4.0 %copy-start.54 = (s32[1,128,8]{1,2,0:T(8,128)S(1)}, s32[1,128,8]{1,2,0:T(8,128)}, u32[]{:S(2)}) copy-start(s32[1,128,8]{1,2,0:T(8,128)} %param.22) | copy-start | bytes 12292
  28.6 4.4 %copy-start.25 = (bf16[128,2048]{1,0:T(8,128)(2,1)S(1)}, bf16[128,2048]{1,0:T(8,128)(2,1)}, u32[]{:S(2)}) copy-start(bf16[128,2048]{1,0:T(8,128)(2,1)} %copy-done.24) | copy-start | bytes 1572868
  28.6 7.1 %copy-start.55 = (f32[2048]{0:T(1024)S(1)}, f32[2048]{0:T(1024)}, u32[]{:S(2)}) copy-start(f32[2048]{0:T(1024)} %param.21) | copy-start | bytes 24580
  28.6 31.1 %copy-start.39 = (bf16[128,1024]{1,0:T(8,128)(2,1)S(1)}, bf16[128,1024]{1,0:T(8,128)(2,1)}, u32[]{:S(2)}) copy-start(bf16[128,1024]{1,0:T(8,128)(2,1)} %copy-done.38) | copy-start | bytes 786436
  28.7 31.0 %all-to-all-start.1 = ((bf16[8,256,512]{2,1,0:T(8,128)(2,1)}), bf16[8,256,512]{2,1,0:T(8,128)(2,1)S(1)}, u32[]{:S(2)}, u32[]{:S(2)}) async-start(bf16[8,256,512]{2,1,0:T(8,128)(2,1)} %after.11), calls=%async_computation.1 | async-start | bytes 4194304 | tf_op jit(solution)/shard_map/all_to_all | solution.py:481
  32.6 3.3 %copy-start.51 = (f32[1,128,8]{2,1,0:T(8,128)}, f32[1,128,8]{2,1,0:T(8,128)S(1)}, u32[]{:S(2)}) copy-start(f32[1,128,8]{2,1,0:T(8,128)S(1)} %copy.32) | copy-start | bytes 12292
  32.7 3.2 %copy-start.44 = (s32[1,128,8]{2,1,0:T(8,128)}, s32[1,128,8]{2,1,0:T(8,128)S(1)}, u32[]{:S(2)}) copy-start(s32[1,128,8]{2,1,0:T(8,128)S(1)} %copy.33) | copy-start | bytes 12292
  33.1 26.6 %collective-permute-start.1 = (bf16[128,2048]{1,0:T(8,128)(2,1)S(1)}, bf16[128,2048]{1,0:T(8,128)(2,1)}, u32[]{:S(2)}, u32[]{:S(2)}) collective-permute-start(bf16[128,2048]{1,0:T(8,128)(2,1)S(1)} %copy-done.25), channel_id=1, source_target_pairs={{0,2},{1,3},{2,0},{3,1},{4,6},{5,7},{6,4},{7,5},{8,10},{9,11},{10,... | collective-permute-start | bytes 1572872 | tf_op jit(solution)/shard_map/ppermute | solution.py:473
  64.6 32.1 %copy-start.4 = (bf16[272,1024]{1,0:T(8,128)(2,1)S(1)}, bf16[272,1024]{1,0:T(8,128)(2,1)}, u32[]{:S(2)}) copy-start(bf16[272,1024]{1,0:T(8,128)(2,1)} %copy-done.3) | copy-start | bytes 1671172
  64.6 32.2 %all-to-all-start.2 = ((bf16[8,32,2048]{2,1,0:T(8,128)(2,1)}), bf16[8,32,2048]{2,1,0:T(8,128)(2,1)S(1)}, u32[]{:S(2)}, u32[]{:S(2)}) async-start(bf16[8,32,2048]{2,1,0:T(8,128)(2,1)} %after.12), calls=%async_computation.2 | async-start | bytes 2097152 | tf_op jit(solution)/shard_map/all_to_all | solution.py:481
  68.6 28.1 %collective-permute-start.3 = (bf16[272,1024]{1,0:T(8,128)(2,1)}, bf16[272,1024]{1,0:T(8,128)(2,1)S(1)}, u32[]{:S(2)}, u32[]{:S(2)}) collective-permute-start(bf16[272,1024]{1,0:T(8,128)(2,1)} %copy-done.3), channel_id=1, source_target_pairs={{0,2},{1,3},{2,0},{3,1},{4,6},{5,7},{6,4},{7,5},{8,10},{9,11},{10,... | collective-permute-start | bytes 1671176 | tf_op jit(solution)/shard_map/ppermute | solution.py:473
  99.0 36.0 %all-to-all-start.3 = ((bf16[8,72,2048]{2,1,0:T(8,128)(2,1)}), bf16[8,72,2048]{2,1,0:T(8,128)(2,1)S(1)}, u32[]{:S(2)}, u32[]{:S(2)}) async-start(bf16[8,72,2048]{2,1,0:T(8,128)(2,1)} %bitcast.20), calls=%async_computation.3 | async-start | bytes 4718592 | tf_op jit(solution)/shard_map/all_to_all | solution.py:481
  102.8 17.6 %collective-permute-start.5 = (bf16[272,1024]{1,0:T(8,128)(2,1)}, bf16[272,1024]{1,0:T(8,128)(2,1)S(1)}, u32[]{:S(2)}, u32[]{:S(2)}) collective-permute-start(bf16[272,1024]{1,0:T(8,128)(2,1)} %after.13), channel_id=1, source_target_pairs={{0,3},{1,2},{2,1},{3,0},{4,7},{5,6},{6,5},{7,4},{8,11},{9,10},{10,... | collective-permute-start | bytes 1671176 | tf_op jit(solution)/shard_map/ppermute | solution.py:473
  105.3 26.6 %collective-permute-start.4 = (bf16[272,1024]{1,0:T(8,128)(2,1)}, bf16[272,1024]{1,0:T(8,128)(2,1)S(1)}, u32[]{:S(2)}, u32[]{:S(2)}) collective-permute-start(bf16[272,1024]{1,0:T(8,128)(2,1)} %after.13), channel_id=1, source_target_pairs={{0,1},{1,0},{2,3},{3,2},{4,5},{5,4},{6,7},{7,6},{8,9},{9,8},{10,11... | collective-permute-start | bytes 1671176 | tf_op jit(solution)/shard_map/ppermute | solution.py:473
  120.4 11.7 %copy-start.20 = (bf16[272,1024]{1,0:T(8,128)(2,1)}, bf16[272,1024]{1,0:T(8,128)(2,1)S(1)}, u32[]{:S(2)}) copy-start(bf16[272,1024]{1,0:T(8,128)(2,1)S(1)} %collective-permute-done.5.refs_2_.refs_4_) | copy-start | bytes 1671172
  136.4 33.9 %all-to-all-start.5 = ((bf16[8,72,2048]{2,1,0:T(8,128)(2,1)}), bf16[8,72,2048]{2,1,0:T(8,128)(2,1)}, u32[]{:S(2)}, u32[]{:S(2)}) async-start(bf16[8,72,2048]{2,1,0:T(8,128)(2,1)} %bitcast.30), calls=%async_computation.5 | async-start | bytes 4718592 | tf_op jit(solution)/shard_map/all_to_all | solution.py:481
  140.8 3.6 %copy-start.5 = (bf16[1,2048,768]{2,1,0:T(8,128)(2,1)S(1)}, bf16[1,2048,768]{2,1,0:T(8,128)(2,1)}, u32[]{:S(2)}) copy-start(bf16[1,2048,768]{2,1,0:T(8,128)(2,1)} %param.24) | copy-start | bytes 9437188
  142.8 26.6 %collective-permute-start.6 = (bf16[128,2048]{1,0:T(8,128)(2,1)}, bf16[128,2048]{1,0:T(8,128)(2,1)}, u32[]{:S(2)}, u32[]{:S(2)}) collective-permute-start(bf16[128,2048]{1,0:T(8,128)(2,1)} %after.14), channel_id=1, source_target_pairs={{0,2},{1,3},{2,0},{3,1},{4,6},{5,7},{6,4},{7,5},{8,10},{9,11},{10,... | collective-permute-start | bytes 1572872 | tf_op jit(solution)/shard_map/ppermute | solution.py:473
  170.2 3.9 %copy-start.19 = (bf16[1,128,2048]{2,1,0:T(8,128)(2,1)S(1)}, bf16[1,128,2048]{2,1,0:T(8,128)(2,1)}, u32[]{:S(2)}) copy-start(bf16[1,128,2048]{2,1,0:T(8,128)(2,1)} %param.29) | copy-start | bytes 1572868
  170.2 34.7 %all-to-all-start.4 = ((bf16[8,72,2176]{2,1,0:T(8,128)(2,1)}), bf16[8,72,2176]{2,1,0:T(8,128)(2,1)S(1)}, u32[]{:S(2)}, u32[]{:S(2)}) async-start(bf16[8,72,2176]{2,1,0:T(8,128)(2,1)} %bitcast.66), calls=%async_computation.4 | async-start | bytes 5013504 | tf_op jit(solution)/shard_map/all_to_all | solution.py:481
  175.0 20.1 %collective-permute-start.8 = (bf16[128,2048]{1,0:T(8,128)(2,1)}, bf16[128,2048]{1,0:T(8,128)(2,1)S(1)}, u32[]{:S(2)}, u32[]{:S(2)}) collective-permute-start(bf16[128,2048]{1,0:T(8,128)(2,1)} %after.16), channel_id=1, source_target_pairs={{0,3},{1,2},{2,1},{3,0},{4,7},{5,6},{6,5},{7,4},{8,11},{9,10},{10,... | collective-permute-start | bytes 1572872 | tf_op jit(solution)/shard_map/ppermute | solution.py:473
  176.6 25.2 %collective-permute-start.7 = (bf16[128,2048]{1,0:T(8,128)(2,1)}, bf16[128,2048]{1,0:T(8,128)(2,1)S(1)}, u32[]{:S(2)}, u32[]{:S(2)}) collective-permute-start(bf16[128,2048]{1,0:T(8,128)(2,1)} %after.16), channel_id=1, source_target_pairs={{0,1},{1,0},{2,3},{3,2},{4,5},{5,4},{6,7},{7,6},{8,9},{9,8},{10,11... | collective-permute-start | bytes 1572872 | tf_op jit(solution)/shard_map/ppermute | solution.py:473
  191.3 13.5 %copy-start.42 = (bf16[576,768]{1,0:T(8,128)(2,1)}, bf16[576,768]{1,0:T(8,128)(2,1)S(1)}, u32[]{:S(2)}) copy-start(bf16[576,768]{1,0:T(8,128)(2,1)S(1)} %get-tuple-element.32.refs_4_.refs_1_) | copy-start | bytes 2654212
  195.0 7.6 %copy-start.29 = (bf16[128,2048]{1,0:T(8,128)(2,1)}, bf16[128,2048]{1,0:T(8,128)(2,1)S(1)}, u32[]{:S(2)}) copy-start(bf16[128,2048]{1,0:T(8,128)(2,1)S(1)} %collective-permute-done.8.refs_3_.refs_8_) | copy-start | bytes 1572868
  201.8 3.0 %copy-start.32 = (bf16[128,2048]{1,0:T(8,128)(2,1)}, bf16[128,2048]{1,0:T(8,128)(2,1)S(1)}, u32[]{:S(2)}) copy-start(bf16[128,2048]{1,0:T(8,128)(2,1)S(1)} %collective-permute-done.7.refs_2_.refs_7_) | copy-start | bytes 1572868
  204.9 35.4 %all-to-all-start.6 = ((bf16[8,72,2176]{2,1,0:T(8,128)(2,1)}), bf16[8,72,2176]{2,1,0:T(8,128)(2,1)}, u32[]{:S(2)}, u32[]{:S(2)}) async-start(bf16[8,72,2176]{2,1,0:T(8,128)(2,1)} %bitcast.65), calls=%async_computation.6 | async-start | bytes 5013504 | tf_op jit(solution)/shard_map/all_to_all | solution.py:481
  211.0 3.0 %copy-start.33 = (bf16[128,2048]{1,0:T(8,128)(2,1)S(1)}, bf16[128,2048]{1,0:T(8,128)(2,1)}, u32[]{:S(2)}) copy-start(bf16[128,2048]{1,0:T(8,128)(2,1)} %copy-done.32) | copy-start | bytes 1572868
  213.1 28.1 %collective-permute-start.9 = (bf16[128,2176]{1,0:T(8,128)(2,1)}, bf16[128,2176]{1,0:T(8,128)(2,1)}, u32[]{:S(2)}, u32[]{:S(2)}) collective-permute-start(bf16[128,2176]{1,0:T(8,128)(2,1)} %get-tuple-element.40), channel_id=1, source_target_pairs={{0,2},{1,3},{2,0},{3,1},{4,6},{5,7},{6,4},{7,5},{8,10},{9,11},{10,... | collective-permute-start | bytes 1671176 | tf_op jit(solution)/shard_map/ppermute | solution.py:473
  243.8 3.9 %copy-start.31 = (bf16[128,2048]{1,0:T(8,128)(2,1)S(1)}, bf16[128,2048]{1,0:T(8,128)(2,1)}, u32[]{:S(2)}) copy-start(bf16[128,2048]{1,0:T(8,128)(2,1)} %copy-done.29) | copy-start | bytes 1572868
  243.8 3.9 %copy-start.34 = (bf16[128,2048]{1,0:T(8,128)(2,1)S(1)}, bf16[128,2048]{1,0:T(8,128)(2,1)}, u32[]{:S(2)}) copy-start(bf16[128,2048]{1,0:T(8,128)(2,1)} %copy-done.32) | copy-start | bytes 1572868
  251.6 20.8 %copy-start.41 = (bf16[576,768]{1,0:T(8,128)(2,1)S(1)}, bf16[576,768]{1,0:T(8,128)(2,1)}, u32[]{:S(2)}) copy-start(bf16[576,768]{1,0:T(8,128)(2,1)} %copy-done.40) | copy-start | bytes 2654212
  251.6 20.8 %copy-start.43 = (bf16[576,768]{1,0:T(8,128)(2,1)S(1)}, bf16[576,768]{1,0:T(8,128)(2,1)}, u32[]{:S(2)}) copy-start(bf16[576,768]{1,0:T(8,128)(2,1)} %copy-done.42) | copy-start | bytes 2654212
  251.6 31.5 %copy-start.28 = (bf16[128,2176]{1,0:T(8,128)(2,1)S(1)}, bf16[128,2176]{1,0:T(8,128)(2,1)}, u32[]{:S(2)}) copy-start(bf16[128,2176]{1,0:T(8,128)(2,1)} %copy-done.27) | copy-start | bytes 1671172
  251.6 20.8 %all-to-all-start.7 = ((bf16[8,32,2304]{2,1,0:T(8,128)(2,1)}), bf16[8,32,2304]{2,1,0:T(8,128)(2,1)S(1)}, u32[]{:S(2)}, u32[]{:S(2)}) async-start(bf16[8,32,2304]{2,1,0:T(8,128)(2,1)} %copy-done.23), calls=%async_computation.7 | async-start | bytes 2359296 | tf_op jit(solution)/shard_map/all_to_all | solution.py:481
  255.7 27.5 %collective-permute-start.10 = (bf16[128,2176]{1,0:T(8,128)(2,1)}, bf16[128,2176]{1,0:T(8,128)(2,1)}, u32[]{:S(2)}, u32[]{:S(2)}) collective-permute-start(bf16[128,2176]{1,0:T(8,128)(2,1)} %copy-done.46), channel_id=1, source_target_pairs={{0,1},{1,0},{2,3},{3,2},{4,5},{5,4},{6,7},{7,6},{8,9},{9,8},{10,11... | collective-permute-start | bytes 1671176 | tf_op jit(solution)/shard_map/ppermute | solution.py:473
  255.7 27.4 %collective-permute-start.11 = (bf16[128,2176]{1,0:T(8,128)(2,1)}, bf16[128,2176]{1,0:T(8,128)(2,1)}, u32[]{:S(2)}, u32[]{:S(2)}) collective-permute-start(bf16[128,2176]{1,0:T(8,128)(2,1)} %copy-done.50), channel_id=1, source_target_pairs={{0,3},{1,2},{2,1},{3,0},{4,7},{5,6},{6,5},{7,4},{8,11},{9,10},{10,... | collective-permute-start | bytes 1671176 | tf_op jit(solution)/shard_map/ppermute | solution.py:473
  272.5 10.7 %copy-start.45 = (s32[1,128,8]{2,1,0:T(8,128)S(1)}, s32[1,128,8]{2,1,0:T(8,128)}, u32[]{:S(2)}) copy-start(s32[1,128,8]{2,1,0:T(8,128)} %copy-done.44) | copy-start | bytes 12292
  272.5 10.7 %copy-start.48 = (f32[128,8]{1,0:T(8,128)S(1)}, f32[128,8]{1,0:T(8,128)}, u32[]{:S(2)}) copy-start(f32[128,8]{1,0:T(8,128)} %fusion.1.refs_4_) | copy-start | bytes 12292
  (28 other events, 40.2 us)

commit v5 on v4

--- a/solution.py
+++ b/solution.py
@@ -106,23 +106,57 @@
     return pl.CostEstimate(flops=flops, bytes_accessed=bytes_accessed, transcendentals=0)
 
 
-def project_kernel(*refs, blocks, chunks):
+def pack_kernel(residual_ref, routing_ref, out_ref):
+    tokens = residual_ref.shape[0]
+    out_ref[:tokens, :] = residual_ref[...]
+    routing = routing_ref[...]
+    picks = routing.shape[0] // 2
+    gates = routing[:picks].astype(BF16).astype(F32)
+    table = jnp.concatenate(
+        [
+            jnp.concatenate([gates, routing[:picks] - gates], axis=0),
+            jnp.concatenate([routing[picks:], jnp.zeros((picks, tokens), F32)], axis=0),
+        ],
+        axis=1,
+    )
+    wide = table.shape[1]
+    out_ref[tokens:, :wide] = table.astype(BF16)
+    if wide < out_ref.shape[1]:
+        out_ref[tokens:, wide:] = jnp.zeros((16, out_ref.shape[1] - wide), BF16)
+
+
+def pack(residual, routing):
+    tokens, cols = residual.shape
+    return pl.pallas_call(
+        pack_kernel,
+        in_specs=[vmem()] * 2,
+        out_specs=vmem(),
+        out_shape=jax.ShapeDtypeStruct((tokens + 16, cols), BF16),
+        compiler_params=params(),
+        name="pack",
+    )(residual, routing)
+
+
+def tile_place(number, cols):
+    across = cols // 128
+    return number // across * 16, number % across * 128
+
+
+def project_kernel(*refs, blocks):
     attended, residuals = refs[:blocks], refs[blocks : 2 * blocks]
-    own_ref, pair_ref, gain_ref, routing_ref = refs[2 * blocks : 2 * blocks + 4]
-    outs = refs[2 * blocks + 4 :]
+    own_ref, pair_ref, gain_ref, out_ref = refs[2 * blocks :]
     cols = own_ref.shape[1]
-    tokens = residuals[0].shape[0]
+    tokens = attended[0].shape[0]
+    near = blocks * tokens
     rows = jnp.concatenate([ref[...] for ref in attended], axis=0)
     square = None
     for side, weight_ref in enumerate((own_ref, pair_ref)):
         at = side * cols
         stream = dot(rows, weight_ref[...])
-        stream += jnp.concatenate([ref[:, at : at + cols] for ref in residuals], axis=0).astype(F32)
-        scaled = (stream * gain_ref[:, at : at + cols]).astype(BF16)
-        for out_ref, (start, size) in zip(outs, chunks):
-            out_ref[: blocks * tokens, side * size : (side + 1) * size] = scaled[
-                :, start : start + size
-            ]
+        stream += jnp.concatenate(
+            [ref[:tokens, at : at + cols] for ref in residuals], axis=0
+        ).astype(F32)
+        out_ref[:near, at : at + cols] = (stream * gain_ref[:, at : at + cols]).astype(BF16)
         for lane in range(0, cols, 128):
             piece = stream[:, lane : lane + 128]
             square = piece * piece if square is None else square + piece * piece
@@ -131,43 +165,34 @@
         [square[:, i * tokens : (i + 1) * tokens] for i in range(blocks)], axis=0
     )
     high = square.astype(BF16).astype(F32)
-    routing = routing_ref[...]
-    picks = routing.shape[0] // 2
-    gates = routing[:picks].astype(BF16).astype(F32)
     rest = jnp.zeros((8 - blocks, tokens), F32)
-    table = jnp.concatenate(
-        [
-            jnp.concatenate([gates, routing[:picks] - gates], axis=0),
-            jnp.concatenate([routing[picks:], jnp.zeros((picks, tokens), F32)], axis=0),
-            jnp.concatenate([high, rest, square - high, rest], axis=0),
-        ],
-        axis=1,
-    )
-    wide = table.shape[1]
-    out_ref = outs[0]
-    out_ref[blocks * tokens :, :wide] = table.astype(BF16)
-    if wide < out_ref.shape[1]:
-        out_ref[blocks * tokens :, wide:] = jnp.zeros((16, out_ref.shape[1] - wide), BF16)
-
-
-def project(attended, residuals, own_weight, pair_weight, gain, routing, chunks):
+    out_ref[near:, :] = jnp.zeros((out_ref.shape[0] - near, 2 * cols), BF16)
+    for i, ref in enumerate(residuals):
+        row, lane = tile_place(2 * i, 2 * cols)
+        out_ref[near + row : near + row + 16, lane : lane + 2 * tokens] = ref[
+            tokens:, : 2 * tokens
+        ]
+    row, lane = tile_place(2 * blocks, 2 * cols)
+    out_ref[near + row : near + row + 16, lane : lane + tokens] = jnp.concatenate(
+        [high, rest, square - high, rest], axis=0
+    ).astype(BF16)
+
+
+def project(attended, residuals, own_weight, pair_weight, gain):
     blocks = len(attended)
     tokens, width = attended[0].shape
     cols = own_weight.shape[1]
     rows = blocks * tokens
-    more = 16
-    return pl.pallas_call(
-        lambda *refs: project_kernel(*refs, blocks=blocks, chunks=chunks),
-        in_specs=[vmem()] * (2 * blocks + 4),
-        out_specs=[vmem()] * len(chunks),
-        out_shape=[
-            jax.ShapeDtypeStruct((rows + (0 if number else more), 2 * size), BF16)
-            for number, (_, size) in enumerate(chunks)
-        ],
+    more = tile_place(2 * blocks, 2 * cols)[0] + 16
+    return pl.pallas_call(
+        lambda *refs: project_kernel(*refs, blocks=blocks),
+        in_specs=[vmem()] * (2 * blocks + 3),
+        out_specs=vmem(),
+        out_shape=jax.ShapeDtypeStruct((rows + more, 2 * cols), BF16),
         compiler_params=params(),
         cost_estimate=cost(4 * rows * width * cols, 4 * width * cols),
         name="project",
-    )(*attended, *residuals, own_weight, pair_weight, gain.reshape(1, 2 * cols), routing)
+    )(*attended, *residuals, own_weight, pair_weight, gain.reshape(1, 2 * cols))
 
 
 def hits_of(slots, capacity):
@@ -182,18 +207,17 @@
     )
 
 
-def route_kernel(column_ref, *refs, capacity, picks, columns, width):
-    blocks = refs[:-3]
-    slot_ref, gate_ref, inverse_ref = refs[-3:]
+def route_kernel(column_ref, *refs, places, capacity, picks, columns):
+    blocks, slot_ref, gate_ref = refs[:-2], refs[-2], refs[-1]
     groups, near = slot_ref.shape
-    count = len(blocks)
-    tokens = near // count
-    tables = [block[near:, :].astype(F32) for block in blocks]
+    tokens = near // len(places)
+    tables = [
+        blocks[number][row : row + 16, lane : lane + 2 * tokens].astype(F32)
+        for number, row, lane in places
+    ]
     probs = jnp.concatenate([x[:, :tokens] for x in tables], axis=1)
     probs = probs[:picks] + probs[picks : 2 * picks]
-    ids = jnp.concatenate([x[:picks, tokens : 2 * tokens] for x in tables], axis=1)
-    ids = ids.astype(jnp.int32)
-    squares = [x[:, 2 * tokens : 3 * tokens] for x in tables]
+    ids = jnp.concatenate([x[:picks, tokens:] for x in tables], axis=1).astype(jnp.int32)
     member, gates = [], []
     for group in range(groups):
         hit = ids == group * columns + column_ref[0]
@@ -204,70 +228,90 @@
         jnp.int32, (near, near), 1
     )
     ranks = dot(member.astype(BF16), earlier.astype(BF16)).astype(jnp.int32)
-    slots = jnp.where(member > 0.0, ranks, capacity)
-    slot_ref[...] = slots
+    slot_ref[...] = jnp.where(member > 0.0, ranks, capacity)
     gate_ref[...] = jnp.concatenate(gates, axis=0)
+
+
+def route(column, blocks, places, groups, capacity, tokens, picks, columns):
+    near = len(places) * tokens
+    return pl.pallas_call(
+        lambda *refs: route_kernel(
+            *refs, places=places, capacity=capacity, picks=picks, columns=columns
+        ),
+        in_specs=[smem()] + [vmem()] * len(blocks),
+        out_specs=[vmem()] * 2,
+        out_shape=[
+            jax.ShapeDtypeStruct((groups, near), jnp.int32),
+            jax.ShapeDtypeStruct((groups, near), F32),
+        ],
+        compiler_params=params(),
+        name="route",
+    )(column.reshape(1), *blocks)
+
+
+def place_sides(out_ref, picked, at, first):
+    half = picked.shape[1] // 2
+    for side in range(2):
+        lane = pl.multiple_of(at + ((first ^ side) % 2) * half, 128)
+        out_ref[:, pl.ds(lane, half)] = picked[:, side * half : (side + 1) * half]
+
+
+def pick_kernel(first_ref, slot_ref, *refs, count, capacity, first, rest):
+    blocks, out_ref = refs[:count], refs[-1]
+    near = slot_ref.shape[1]
+    hits = hits_of(slot_ref[...], capacity)
+    places = hits.astype(BF16)
+    cols = blocks[0].shape[1]
+    skip = 0 if first else cols
+    if first:
+        picked = dot(places, blocks[0][:near, :]).astype(BF16)
+        place_sides(out_ref, picked, 0, first_ref[0])
+    if not rest:
+        return
+    tokens = near // count
+    row, lane = tile_place(2 * count, cols)
+    squares = [
+        x[near + row : near + row + 16, lane : lane + tokens].astype(F32) for x in blocks
+    ]
     inverses = []
     for b in range(count):
         total = jnp.zeros((1, tokens), F32)
         for i in range(count):
-            row = i ^ b
-            total += squares[i][row : row + 1] + squares[i][8 + row : 9 + row]
-        inverses.append(lax.rsqrt(total / width + norm_eps))
-    inverse_ref[...] = jnp.concatenate(inverses, axis=1)
-
-
-def route(column, blocks, groups, capacity, tokens, picks, columns, width):
-    near = len(blocks) * tokens
-    return pl.pallas_call(
-        lambda *refs: route_kernel(
-            *refs, capacity=capacity, picks=picks, columns=columns, width=width
-        ),
-        in_specs=[smem()] + [vmem()] * len(blocks),
-        out_specs=[vmem()] * 3,
-        out_shape=[
-            jax.ShapeDtypeStruct((groups, near), jnp.int32),
-            jax.ShapeDtypeStruct((groups, near), F32),
-            jax.ShapeDtypeStruct((1, near), F32),
-        ],
-        compiler_params=params(),
-        name="route",
-    )(column.reshape(1), *blocks)
-
-
-def pick_kernel(first_ref, slot_ref, inverse_ref, *refs, count, capacity):
-    blocks = refs[:count]
-    out_ref = refs[-1]
-    near = slot_ref.shape[1]
-    tokens = near // count
-    half = blocks[0].shape[1] // 2
-    hits = hits_of(slot_ref[...], capacity)
-    factors = jnp.sum(hits * inverse_ref[...], axis=1, keepdims=True)
-    hits = hits.astype(BF16)
-    for i, block in enumerate(blocks):
+            total += squares[i][i ^ b : (i ^ b) + 1] + squares[i][8 + (i ^ b) : 9 + (i ^ b)]
+        inverses.append(lax.rsqrt(total / (count * cols) + norm_eps))
+    factors = jnp.sum(hits * jnp.concatenate(inverses, axis=1), axis=1, keepdims=True)
+    for i in range(1, count):
         rows = jnp.concatenate(
-            [block[(i ^ b) * tokens : ((i ^ b) + 1) * tokens, :] for b in range(count)], axis=0
+            [blocks[i][(i ^ b) * tokens : ((i ^ b) + 1) * tokens, :] for b in range(count)], axis=0
         )
-        picked = (dot(hits, rows) * factors).astype(BF16)
-        for side in range(2):
-            at = pl.multiple_of((first_ref[0] ^ (2 * i + side)) * half, 128)
-            out_ref[:, pl.ds(at, half)] = picked[:, side * half : (side + 1) * half]
-
-
-def pick(first, slots, inverse, blocks, capacity, earlier):
+        place_sides(out_ref, dot(places, rows).astype(BF16), i * cols - skip, first_ref[0])
+    high = factors.astype(BF16).astype(F32)
+    lanes = lax.broadcasted_iota(jnp.int32, (factors.shape[0], 128), 1)
+    table = jnp.where(lanes == 0, high, jnp.where(lanes == 1, factors - high, 0.0))
+    out_ref[:, count * cols - skip :] = table.astype(BF16)
+
+
+def pick(plane, slots, blocks, capacity, first, rest, earlier):
     groups, near = slots.shape
     count = len(blocks)
-    cols = blocks[0].shape[1] * count
-    rows = groups * capacity
-    return pl.pallas_call(
-        lambda *refs: pick_kernel(*refs[: 3 + count], refs[-1], count=count, capacity=capacity),
-        in_specs=[smem()] + [vmem()] * (2 + count) + [anywhere()] * len(earlier),
+    rows, cols = groups * capacity, blocks[0].shape[1]
+    wide = (cols if first else 0) + ((count - 1) * cols + 128 if rest else 0)
+    return pl.pallas_call(
+        lambda *refs: pick_kernel(
+            *refs[: 2 + count],
+            refs[-1],
+            count=count,
+            capacity=capacity,
+            first=first,
+            rest=rest,
+        ),
+        in_specs=[smem()] + [vmem()] * (1 + count) + [anywhere()] * len(earlier),
         out_specs=vmem(),
-        out_shape=jax.ShapeDtypeStruct((rows, cols), BF16),
-        compiler_params=params(),
-        cost_estimate=cost(2 * rows * near * cols, 2 * rows * cols),
+        out_shape=jax.ShapeDtypeStruct((rows, wide), BF16),
+        compiler_params=params(),
+        cost_estimate=cost(2 * rows * near * wide, 2 * rows * wide),
         name="pick",
-    )(first.reshape(1), slots, inverse, *blocks, *earlier)
+    )(plane.reshape(1), slots, *blocks, *earlier)
 
 
 def fill_kernel(slot_ref, gate_ref, *refs, capacity):
@@ -290,7 +334,7 @@
     rows, cols = groups * capacity, blocks[0].shape[1]
     return pl.pallas_call(
         lambda *refs: fill_kernel(*refs[: 2 + len(blocks)], *refs[-2:], capacity=capacity),
-        in_specs=[vmem()] * (2 + len(blocks)) + [anywhere()],
+        in_specs=[vmem()] * (2 + len(blocks)) + [anywhere()] * len(earlier),
         out_specs=[vmem()] * 2,
         out_shape=[
             jax.ShapeDtypeStruct((rows, cols), BF16),
@@ -299,45 +343,50 @@
         compiler_params=params(),
         cost_estimate=cost(2 * rows * near * cols, 2 * rows * cols),
         name="fill",
-    )(slots, gates, *blocks, earlier)
-
-
-def back_kernel(factor_ref, *refs, capacity, count):
-    out_ref = refs[-1]
+    )(slots, gates, *blocks, *earlier)
+
+
+def back_kernel(place_ref, *refs, capacity, count):
+    out_ref, made_ref = refs[-2:]
     groups, rank, wide = out_ref.shape
+    factors = jnp.concatenate([ref[...] for ref in refs[:groups]], axis=0)
+    refs = refs[groups:]
     halves = 2
     part = wide // halves
     out_ref[...] = jnp.zeros(out_ref.shape, BF16)
     for half in range(halves):
         slot_ref, gate_ref, *blocks = refs[half * (2 + count) : (half + 1) * (2 + count)]
         rows = jnp.concatenate([block[...] for block in blocks], axis=0)
-        made = dot_t(factor_ref[...], rows)
+        made_ref[...] = dot_t(factors, rows)
         hits = hits_of(slot_ref[...], capacity)
         for group in range(groups):
-            mine = made[group * rank : (group + 1) * rank] * gate_ref[group : group + 1, :]
+            x = place_ref[0] ^ group
+            at = pl.multiple_of((x // 2 + x % 2 * (groups // 2)) * rank, rank)
+            mine = made_ref[pl.ds(at, rank), :] * gate_ref[group : group + 1, :]
             slots = hits[group * capacity : (group + 1) * capacity].astype(BF16)
             out_ref[group, :, half * part : half * part + capacity] = dot_t(
                 mine.astype(BF16), slots
             ).astype(BF16)
 
 
-def back_slots_of(factors, halves, capacity, earlier):
+def back_slots_of(place, factors, halves, capacity, earlier):
     operands = [x for slots, gates, blocks in halves for x in (slots, gates, *blocks)]
     count = len(halves[0][2])
     groups, near = halves[0][0].shape
-    rank = factors.shape[0] // groups
+    rank, width = factors[0].shape
     part = capacity + -capacity % 128
     return pl.pallas_call(
         lambda *refs: back_kernel(
-            *refs[: 1 + len(operands)], refs[-1], capacity=capacity, count=count
+            *refs[: 1 + groups + len(operands)], *refs[-2:], capacity=capacity, count=count
         ),
-        in_specs=[vmem()] * (1 + len(operands)) + [anywhere()],
+        in_specs=[smem()] + [vmem()] * (groups + len(operands)) + [anywhere()],
         out_specs=vmem(),
         out_shape=jax.ShapeDtypeStruct((groups, rank, 2 * part), BF16),
         compiler_params=params(),
-        cost_estimate=cost(4 * near * factors.size, 4 * factors.size),
+        scratch_shapes=[pltpu.VMEM((groups * rank, near), F32)],
+        cost_estimate=cost(4 * near * groups * rank * width, 4 * groups * rank * width),
         name="back_low",
-    )(factors, *operands, earlier)
+    )(place.reshape(1), *factors, *operands, earlier)
 
 
 def gradient_kernel(back_ref, *refs, count, rank):
@@ -386,24 +435,38 @@
 
 
 def expert_kernel(
-    rows_ref, gate_ref, up_ref, factor_ref, down_ref, up_factor_ref, out_active, out_ref
+    pair_ref,
+    *refs,
+    cols,
 ):
-    rows = rows_ref[...]
-    gate = dot(rows, gate_ref[...])
-    up = dot(rows, up_ref[...])
+    *parts, gate_ref, up_ref, factor_ref, down_ref, up_factor_ref, out_active, out_ref = refs
+    more_ref = parts[-1]
+    skip = cols if len(parts) > 1 else 0
+    gate = up = 0.0
+    for i in range(gate_ref.shape[0] // cols):
+        if i == 0:
+            rows = parts[0][:, :cols]
+        else:
+            rows = more_ref[:, i * cols - skip : (i + 1) * cols - skip]
+        at = pl.ds(pl.multiple_of((pair_ref[0] ^ i) * cols, cols), cols)
+        gate += dot(rows, gate_ref[at, :])
+        up += dot(rows, up_ref[at, :])
+    norm = more_ref[:, more_ref.shape[1] - 128 :].astype(F32)
+    norm = norm[:, :1] + norm[:, 1:2]
+    gate, up = gate * norm, up * norm
     active = (gate / (1.0 + jnp.exp(-gate)) * up).astype(BF16)
     out_active[...] = active
     low = dot(active, factor_ref[...]).astype(BF16)
     made = dot(active, down_ref[...]) + adapter_scale * dot(low, up_factor_ref[...])
     cols, rank = made.shape[1], low.shape[1]
     out_ref[:, :cols] = made.astype(BF16)
-    out_ref[:, cols:] = jnp.zeros((rows.shape[0], out_ref.shape[1] - cols), BF16)
+    out_ref[:, cols:] = jnp.zeros((made.shape[0], out_ref.shape[1] - cols), BF16)
     out_ref[:, cols : cols + rank] = low
 
 
-def expert(rows, gate_weight, up_weight, factor, down_weight, up_factor, earlier):
-    count, width = rows.shape
-    units = gate_weight.shape[1]
+def expert(pair, parts, cols, gate_weight, up_weight, factor, down_weight, up_factor):
+    count = parts[0].shape[0]
+    width, units = gate_weight.shape
     step = count // 2
 
     def whole(x):
@@ -411,11 +474,11 @@
 
     weights = (gate_weight, up_weight, factor, down_weight, up_factor)
     return pl.pallas_call(
-        lambda *refs: expert_kernel(*refs[:6], *refs[-2:]),
+        lambda *refs: expert_kernel(*refs, cols=cols),
         grid=(count // step,),
-        in_specs=[pl.BlockSpec((step, width), lambda i: (i, 0))]
-        + [whole(x) for x in weights]
-        + [anywhere()] * len(earlier),
+        in_specs=[smem()]
+        + [pl.BlockSpec((step, x.shape[1]), lambda i: (i, 0)) for x in parts]
+        + [whole(x) for x in weights],
         out_specs=[
             pl.BlockSpec((step, units), lambda i: (i, 0)),
             pl.BlockSpec((step, width + 128), lambda i: (i, 0)),
@@ -427,7 +490,7 @@
         compiler_params=params(40),
         cost_estimate=cost(0, 0),
         name="expert",
-    )(rows, *weights, *earlier)
+    )(pair.reshape(1), *parts, *weights)
 
 
 def combine_kernel(back_ref, weight_ref, upstream_ref, slot_ref, *outs):
@@ -471,6 +534,34 @@
 def from_plane(x, r):
     size = lax.axis_size("expert")
     return lax.ppermute(x, "expert", [(i, i ^ r) for i in range(size)])
+
+
+def from_place(x, r):
+    size = lax.axis_size("seq")
+    return lax.ppermute(x, "seq", [(i, i ^ r) for i in range(size)])
+
+
+def copy_kernel(x_ref, *refs):
+    refs[-1][...] = x_ref[...]
+
+
+def later(x, *earlier):
+    return pl.pallas_call(
+        copy_kernel,
+        in_specs=[vmem()] + [anywhere()] * len(earlier),
+        out_specs=vmem(),
+        out_shape=jax.ShapeDtypeStruct(x.shape, x.dtype),
+        compiler_params=params(),
+        name="later",
+    )(x, *earlier)
+
+
+def all_planes(x):
+    found = [x, from_plane(x, 1)]
+    for r in range(2, lax.axis_size("expert"), 2):
+        found.append(from_plane(x, r))
+        found.append(from_plane(found[-1], 1))
+    return found
 
 
 def columns_of(x, r, size):
@@ -609,15 +700,19 @@
     routing = jnp.concatenate([gate_probs, routed_experts[0].T.astype(F32)], axis=0)
     gate_probs = gate_probs.T
     residuals = [
-        jnp.concatenate([columns_of(residual[0], r, block), columns_of(residual[0], r + 1, block)], 1)
+        pack(
+            jnp.concatenate(
+                [columns_of(residual[0], r, block), columns_of(residual[0], r + 1, block)], 1
+            ),
+            routing,
+        )
         for r in range(0, columns, 2)
     ]
     residuals = [residuals[0]] + [
         from_plane(after(residuals[r // 2], kv_own), r) for r in range(2, columns, 2)
     ]
     pair_share = jnp.broadcast_to(pair_share[None], (seq_devices,) + pair_share.shape)
-    up_wide = jnp.broadcast_to(adapter_up[0][None], (seq_devices, rank, width))
-    attended = attend(queries[0], kv_all, document_index[0], (pair_share, up_wide))
+    attended = attend(queries[0], kv_all, document_index[0], (pair_share,))
     pair_projection = swap(after(pair_share, attended, *residuals[1:]))
     pair_projection = pair_projection.reshape(-1, block)
     attended = [attended] + [from_plane(attended, r) for r in range(2, columns, 2)]
@@ -629,69 +724,71 @@
         output_projection,
         pair_projection,
         jnp.concatenate([columns_of(gain, 0, block), columns_of(gain, 1, block)], 1),
-        routing,
-        [(0, block)],
-    )[0]
+    )
     capacity = columns // 2 * (9 * tokens * PICKS_PER_TOKEN // (8 * experts))
-    up_factors = swap(after(up_wide, scaled)).reshape(-1, width)
-    even = range(2, columns, 2)
-    odd = range(1, columns, 2)
-    crossed = {0: scaled, **{r: from_plane(scaled, r) for r in even}}
-    later = after(scaled, *(crossed[r] for r in even))
-    crossed.update({r: from_plane(later, r) for r in odd})
-    upstream = {0: cotangent[0]}
-    later = after(cotangent[0], *(crossed[r] for r in odd))
-    upstream.update({r: from_plane(later, r) for r in even})
-    later = after(cotangent[0], *(upstream[r] for r in even))
-    upstream.update({r: from_plane(later, r) for r in odd})
-
-    halves = []
+    crossed = all_planes(scaled)
+    upstream = all_planes(later(cotangent[0], crossed[-1]))
+    near = columns // 2 * tokens
+    slots = []
     for half in range(2):
-        blocks = [crossed[r] for r in range(half, columns, 2)]
-        slots, gates, inverse = route(
-            column, blocks, seq_devices, capacity, tokens, PICKS_PER_TOKEN, columns, width
+        if half == 0:
+            blocks = residuals
+            places = [(i, tokens, 0) for i in range(columns // 2)]
+        else:
+            blocks = [crossed[1]]
+            places = [tile_place(2 * i, 2 * block) for i in range(columns // 2)]
+            places = [(0, near + row, lane) for row, lane in places]
+        slots.append(
+            route(
+                column, blocks, places, seq_devices, capacity, tokens, PICKS_PER_TOKEN, columns
+            )
         )
-        earlier = (up_factors,) if half == 0 else ()
-        rows = swap(pick(column ^ half, slots, inverse, blocks, capacity, earlier))
-        cotangents = [upstream[r] for r in range(half, columns, 2)]
-        halves.append((slots, gates, rows, cotangents))
+    def to_experts(half, first, rest, earlier):
+        blocks = crossed[half::2] if rest else [crossed[half]]
+        places = slots[half][0]
+        return pick(column ^ half, places, blocks, capacity, first, rest, earlier)
+
+    parts = [swap(to_experts(0, True, False, ()))]
+    up_factors = later(adapter_up[0], parts[0])
+    up_factors = [up_factors] + [from_place(up_factors, r) for r in range(2, seq_devices, 2)]
+    picked = to_experts(0, False, True, (*up_factors[1:], crossed[1]))
+    parts.append(swap(picked))
+    other = [swap(to_experts(1, True, True, (picked,)))]
+    up_factors += [from_place(x, 1) for x in up_factors]
     made = [
         expert(
-            rows,
+            column // 2,
+            x,
+            2 * block,
             gate_weight[0],
             up_weight[0],
             adapter_down[0],
             down_weight[0],
             adapter_up[0],
-            (),
         )
-        for _, _, rows, _ in halves
+        for x in (parts, other)
     ]
+    halves = [(slots[half][0], slots[half][1], upstream[half::2]) for half in range(2)]
 
     filled = [
-        fill(slots, gates, cotangents, capacity, made[1][0])
-        for slots, gates, _, cotangents in halves
+        fill(places, gates, cotangents, capacity, (made[1][0],))
+        for places, gates, cotangents in halves
     ]
     backs, pieces, earlier = [], {}, ()
-    for half, (slots, _, _, _) in enumerate(halves):
-        earlier_sent = [x[0] for x in filled] if half else [upstream[r] for r in even]
+    for half, (places, gates, cotangents) in enumerate(halves):
+        earlier_sent = [x[0] for x in filled] if half else halves[0][2][1:]
         sent = after(made[half][1], *earlier_sent)
         backs.append(swap(sent))
         rows, weights = filled[half]
-        sums = combine(backs[half], weights, rows, slots, columns // 2, earlier)
+        sums = combine(backs[half], weights, rows, places, columns // 2, earlier)
         planes = range(half, columns, 2)
         pieces.update({r: from_plane(x, r) if r else x for r, x in zip(planes, sums)})
         earlier = tuple(pieces[r] for r in planes if r)
 
-    back_slots = back_slots_of(
-        up_factors,
-        [(slots, gates, cotangents) for slots, gates, _, cotangents in halves],
-        capacity,
-        pieces[0],
-    )
+    back_slots = back_slots_of(place, up_factors, halves, capacity, pieces[0])
     parts = gradient_parts(
         back_slots,
-        [(back, fills[1], half[3]) for back, fills, half in zip(backs, filled, halves)],
+        [(back, fills[1], half[2]) for back, fills, half in zip(backs, filled, halves)],
         sums[0],
     )
     up_factor_gradient, down_factor_gradient = adapter_gradients(

time: 289 us -> 282 us (0.976)
  waiting for transfers between devices: 148 us -> 125 us
  local copies, waits for them, and re-layouts: 37.5 us -> 50.8 us
  starting transfers between devices: 49.7 us -> 54.3 us
    ppermute x12, waiting for transfers between devices: 110 us -> 90.1 us  [from_plane(): return lax.ppermute(x, 'expert', [(i, i ^ r) for i in range(size)])]
    unnamed x117 -> x169, local copies, waits for them, and re-layouts: 33.5 us -> 45.8 us
    ppermute x0 -> x7, starting transfers between devices: none -> 4.57 us  [from_place(): return lax.ppermute(x, 'seq', [(i, i ^ r) for i in range(size)])]
    all_to_all x8, waiting for transfers between devices: 37.5 us -> 34.2 us  [swap(): return lax.all_to_all(x, 'seq', split_axis=0, concat_axis=0, tiled=True)]
    pallas_call x8 -> x13, Pallas kernels: 28.5 us -> 27.3 us  [the longest x2 18.8 us: expert(): pl.pallas_call(lambda *refs: expert_kernel(*refs, cols=cols), grid=(count...]
  transfers between devices with their start and end apart: 20 -> 27, of which waited for: 14 -> 20; matrix products, arithmetic and copies ran while one was open for 4% -> 3% of each run, Pallas kernels for 12% -> 12%
where the time goes in v5:
time: 282 us; the launch traced here: 280 us
  waiting for transfers between devices  125 us (44%)
  starting transfers between devices  54.3 us (19%)
  local copies, waits for them, and re-layouts  50.8 us (18%)
  Pallas kernels  45.1 us (16%)
  other arithmetic  3.26 us (1%)
    ppermute x12, waiting for transfers between devices, from_plane(): return lax.ppermute(x, 'expert', [(i, i ^ r) for i in range(size)])  90.1 us
    unnamed x169, local copies, waits for them, and re-layouts  45.8 us
    all_to_all x8, waiting for transfers between devices, swap(): return lax.all_to_all(x, 'seq', split_axis=0, concat_axis=0, tiled=True)  34.2 us
    all_to_all x8, starting transfers between devices, swap(): return lax.all_to_all(x, 'seq', split_axis=0, concat_axis=0, tiled=True)  33.9 us
    pallas_call x2, Pallas kernels, expert(): pl.pallas_call(lambda *refs: expert_kernel(*refs, cols=cols), grid=(count...  18.8 us
    ppermute x12, starting transfers between devices, from_plane(): return lax.ppermute(x, 'expert', [(i, i ^ r) for i in range(size)])  15.8 us
  transfers between devices with their start and end apart: 27, of which 20 were waited for; matrix products, arithmetic and copies ran while one was open for 3% of the time, Pallas kernels for 12%

profile of v5, /device:TPU:0, one launch (start us, length us, event | category | flops | bytes accessed | tf_op | source)
XLA Modules:
  0.0 280.0 jit_solution(3700417205057308057)
XLA Ops:
  2.6 5.3 %all-to-all-start = ((bf16[8,128,512]{2,1,0:T(8,128)(2,1)}), bf16[8,128,512]{2,1,0:T(8,128)(2,1)S(1)}, u32[]{:S(2)}, u32[]{:S(2)}) async-start(bf16[8,128,512]{2,1,0:T(8,128)(2,1)} %broadcast_in_dim.20.refs_1_), calls=%async_computation | async-start | bytes 2097152 | tf_op jit(solution)/shard_map/all_to_all | solution.py:572
  7.9 1.7 constant_dynamic-slice_fusion.refs_0_
  9.6 1.6 collective-permute-start.1
  14.0 2.6 collective-permute-start
  17.4 3.7 %collective-permute-done.1 = bf16[256,512]{1,0:T(8,128)(2,1)S(1)} collective-permute-done((bf16[256,512]{1,0:T(8,128)(2,1)}, bf16[256,512]{1,0:T(8,128)(2,1)S(1)}, u32[]{:S(2)}, u32[]{:S(2)}) %collective-permute-start.1) | collective-permute-done | bytes 262176 | tf_op jit(solution)/shard_map/ppermute | solution.py:536
  21.2 2.1 all-to-all-done
  25.6 3.5 %attend.1.refs_1_.refs_0_ = bf16[128,2048]{1,0:T(8,128)(2,1)S(1)} custom-call(s32[1]{0:T(128)} %bitcast.12.start_ref, bf16[128,2048]{1,0:T(8,128)(2,1)S(1)} %bitcast.83, bf16[1024,512]{1,0:T(8,128)(2,1)S(1)} %bitcast.76, f32[128,640]{1,0:T(8,128)S(1)} %copy-done.39, bf16[8,256,512]{2,1,0:T(8,128)(2,1)S(1)} %broadcast_in_dim.23.refs_0_), custom_call_target="tpu_custom_call" | custom-call | tf_op jit(solution)/shard_map/attend/pallas_call | solution.py:73
  31.3 4.0 %all-to-all-start.1 = ((bf16[8,256,512]{2,1,0:T(8,128)(2,1)}), bf16[8,256,512]{2,1,0:T(8,128)(2,1)S(1)}, u32[]{:S(2)}, u32[]{:S(2)}) async-start(bf16[8,256,512]{2,1,0:T(8,128)(2,1)} %after.7), calls=%async_computation.1 | async-start | bytes 4194304 | tf_op jit(solution)/shard_map/all_to_all | solution.py:572
  35.3 1.7 collective-permute-start.2
  39.3 22.4 %collective-permute-done.2.refs_1_ = bf16[128,2048]{1,0:T(8,128)(2,1)S(1)} collective-permute-done((bf16[128,2048]{1,0:T(8,128)(2,1)S(1)}, bf16[128,2048]{1,0:T(8,128)(2,1)S(1)}, u32[]{:S(2)}, u32[]{:S(2)}) %collective-permute-start.2) | collective-permute-done | bytes 524320 | tf_op jit(solution)/shard_map/ppermute | solution.py:536
  63.4 1.6 copy-done.25
  69.0 3.9 %all-to-all-start.2 = ((bf16[8,72,1024]{2,1,0:T(8,128)(2,1)}), bf16[8,72,1024]{2,1,0:T(8,128)(2,1)S(1)}, u32[]{:S(2)}, u32[]{:S(2)}) async-start(bf16[8,72,1024]{2,1,0:T(8,128)(2,1)} %bitcast.75), calls=%async_computation.2 | async-start | bytes 2359296 | tf_op jit(solution)/shard_map/all_to_all | solution.py:572
  72.9 3.0 %collective-permute-start.3 = (bf16[272,1024]{1,0:T(8,128)(2,1)S(1)}, bf16[272,1024]{1,0:T(8,128)(2,1)S(1)}, u32[]{:S(2)}, u32[]{:S(2)}) collective-permute-start(bf16[272,1024]{1,0:T(8,128)(2,1)S(1)} %project.1.refs_2_), channel_id=1, source_target_pairs={{0,2},{1,3},{2,0},{3,1},{4,6},{5,7},{6,4},{7,5},{8,10},{9,11},{10,... | collective-permute-start | bytes 1671176 | tf_op jit(solution)/shard_map/ppermute | solution.py:536
  75.9 13.8 %all-to-all-done.2 = bf16[8,72,1024]{2,1,0:T(8,128)(2,1)S(1)} async-done(((bf16[8,72,1024]{2,1,0:T(8,128)(2,1)}), bf16[8,72,1024]{2,1,0:T(8,128)(2,1)S(1)}, u32[]{:S(2)}, u32[]{:S(2)}) %all-to-all-start.2) | async-done | bytes 1179680 | tf_op jit(solution)/shard_map/all_to_all | solution.py:572
  91.8 1.5 collective-permute-start.4
  93.3 6.3 %collective-permute-done.7.refs_7_.refs_1_.refs_2_ = bf16[272,1024]{1,0:T(8,128)(2,1)S(1)} collective-permute-done((bf16[272,1024]{1,0:T(8,128)(2,1)S(1)}, bf16[272,1024]{1,0:T(8,128)(2,1)S(1)}, u32[]{:S(2)}, u32[]{:S(2)}) %collective-permute-start.7) | collective-permute-done | bytes 557088 | tf_op jit(solution)/shard_map/ppermute | solution.py:536
  100.9 1.6 pick.4.refs_4_
  102.5 3.8 %all-to-all-start.3 = ((bf16[8,72,1152]{2,1,0:T(8,128)(2,1)}), bf16[8,72,1152]{2,1,0:T(8,128)(2,1)S(1)}, u32[]{:S(2)}, u32[]{:S(2)}) async-start(bf16[8,72,1152]{2,1,0:T(8,128)(2,1)} %bitcast.22), calls=%async_computation.3 | async-start | bytes 2654208 | tf_op jit(solution)/shard_map/all_to_all | solution.py:572
  106.9 14.5 %collective-permute-done.8.refs_0_.refs_3_ = bf16[272,1024]{1,0:T(8,128)(2,1)S(1)} collective-permute-done((bf16[272,1024]{1,0:T(8,128)(2,1)S(1)}, bf16[272,1024]{1,0:T(8,128)(2,1)S(1)}, u32[]{:S(2)}, u32[]{:S(2)}) %collective-permute-start.8) | collective-permute-done | bytes 557088 | tf_op jit(solution)/shard_map/ppermute | solution.py:536
  122.2 1.5 copy-done.8
  125.9 4.6 %all-to-all-start.5 = ((bf16[8,72,2176]{2,1,0:T(8,128)(2,1)}), bf16[8,72,2176]{2,1,0:T(8,128)(2,1)}, u32[]{:S(2)}, u32[]{:S(2)}) async-start(bf16[8,72,2176]{2,1,0:T(8,128)(2,1)} %bitcast.70), calls=%async_computation.5 | async-start | bytes 5013504 | tf_op jit(solution)/shard_map/all_to_all | solution.py:572
  135.6 1.9 copy-done.4
  140.0 9.2 %expert.2 = (bf16[576,768]{1,0:T(8,128)(2,1)S(1)}, bf16[576,2176]{1,0:T(8,128)(2,1)S(1)}) custom-call(s32[1]{0:T(128)} %bitcast.refs_0_, bf16[576,1024]{1,0:T(8,128)(2,1)S(1)} %bitcast.69, bf16[576,1152]{1,0:T(8,128)(2,1)S(1)} %bitcast.74, bf16[2048,768]{1,0:T(8,128)(2,1)S(1)} %bitcast.64, bf16[2048,768]{1,0:T(8,128)(2,1)S(1)} %bitcast.66, ...), custom_call_target="tpu_custom_call" | custom-call | tf_op jit(solution)/shard_map/expert/pallas_call | solution.py:476
  149.3 1.5 copy-done.10
  151.8 8.1 %collective-permute-done.9.refs_1_.refs_3_.refs_12_.refs_4_ = bf16[128,2048]{1,0:T(8,128)(2,1)} collective-permute-done((bf16[128,2048]{1,0:T(8,128)(2,1)}, bf16[128,2048]{1,0:T(8,128)(2,1)}, u32[]{:S(2)}, u32[]{:S(2)}) %collective-permute-start.9) | collective-permute-done | bytes 524320 | tf_op jit(solution)/shard_map/ppermute | solution.py:536
  159.9 1.7 all-to-all-done.5
  161.6 3.8 %all-to-all-start.4 = ((bf16[8,72,2176]{2,1,0:T(8,128)(2,1)}), bf16[8,72,2176]{2,1,0:T(8,128)(2,1)S(1)}, u32[]{:S(2)}, u32[]{:S(2)}) async-start(bf16[8,72,2176]{2,1,0:T(8,128)(2,1)} %bitcast.72), calls=%async_computation.4 | async-start | bytes 5013504 | tf_op jit(solution)/shard_map/all_to_all | solution.py:572
  165.8 1.7 collective-permute-start.11
  167.5 1.9 copy-done.3
  169.4 1.9 copy-done.5
  171.3 9.6 %expert.3 = (bf16[576,768]{1,0:T(8,128)(2,1)S(1)}, bf16[576,2176]{1,0:T(8,128)(2,1)S(1)}) custom-call(s32[1]{0:T(128)} %bitcast.refs_0_, bf16[576,2176]{1,0:T(8,128)(2,1)} %bitcast.33.refs_1_, bf16[2048,768]{1,0:T(8,128)(2,1)S(1)} %bitcast.65, bf16[2048,768]{1,0:T(8,128)(2,1)S(1)} %bitcast.67, bf16[768,32]{1,0:T(8,128)(2,1)S(1)} %bitcast.78, ...), custom_call_target="tpu_custom_call" | custom-call | tf_op jit(solution)/shard_map/expert/pallas_call | solution.py:476
  180.9 1.5 copy-done.9
  182.4 2.3 fill.2
  186.1 4.8 %collective-permute-done.11.refs_3_.refs_16_.refs_8_ = bf16[128,2048]{1,0:T(8,128)(2,1)S(1)} collective-permute-done((bf16[128,2048]{1,0:T(8,128)(2,1)}, bf16[128,2048]{1,0:T(8,128)(2,1)S(1)}, u32[]{:S(2)}, u32[]{:S(2)}) %collective-permute-start.11) | collective-permute-done | bytes 524320 | tf_op jit(solution)/shard_map/ppermute | solution.py:536
  191.8 1.5 copy-done.13
  194.0 2.3 all-to-all-done.4
  196.2 4.4 %all-to-all-start.6 = ((bf16[8,72,2176]{2,1,0:T(8,128)(2,1)}), bf16[8,72,2176]{2,1,0:T(8,128)(2,1)}, u32[]{:S(2)}, u32[]{:S(2)}) async-start(bf16[8,72,2176]{2,1,0:T(8,128)(2,1)} %bitcast.71), calls=%async_computation.6 | async-start | bytes 5013504 | tf_op jit(solution)/shard_map/all_to_all | solution.py:572
  200.7 1.7 copy-done.12
  206.8 3.1 %back_low.1.refs_0_ = bf16[8,32,256]{2,1,0:T(8,128)(2,1)S(1)} custom-call(s32[1]{0:T(128)} %bitcast.36.refs_0_, bf16[32,2048]{1,0:T(8,128)(2,1)S(1)} %copy-done.58, bf16[32,2048]{1,0:T(8,128)(2,1)S(1)} %copy-done.56, bf16[32,2048]{1,0:T(8,128)(2,1)S(1)} %copy-done.54, bf16[32,2048]{1,0:T(8,128)(2,1)S(1)} %copy-done.52, ...), custom_call_target="tpu_custom_call" | custom-call | flops 536870912 | bytes 2097152 | tf_op jit(solution)/shard_map/back_low/pallas_call | solution.py:378
  210.6 20.6 %collective-permute-done.12.refs_4_.refs_2_ = bf16[128,2176]{1,0:T(8,128)(2,1)S(1)} collective-permute-done((bf16[128,2176]{1,0:T(8,128)(2,1)S(1)}, bf16[128,2176]{1,0:T(8,128)(2,1)S(1)}, u32[]{:S(2)}, u32[]{:S(2)}) %collective-permute-start.12) | collective-permute-done | bytes 557088 | tf_op jit(solution)/shard_map/ppermute | solution.py:536
  232.1 1.7 copy-done.14
  235.8 3.1 %combine.3 = (bf16[128,2176]{1,0:T(8,128)(2,1)S(1)}, bf16[128,2176]{1,0:T(8,128)(2,1)S(1)}) custom-call(bf16[576,2176]{1,0:T(8,128)(2,1)} %bitcast.35.refs_0_.refs_5_, bf16[256,576]{1,0:T(8,128)(2,1)S(1)} %copy-done.38, bf16[576,2048]{1,0:T(8,128)(2,1)S(1)} %copy-done.14, s32[8,256]{1,0:T(8,128)S(1)} %copy-done.64, bf16[128,2176]{1,0:T(8,128)(2,1)S(1)} %copy-done.29), custom_call_target="tpu_custom_call" | custom-call | flops 603979776 | bytes 3407872 | tf_op jit(solution)/shard_map/combine/pallas_call | solution.py:523
  239.7 2.3 gradient.1
  243.9 4.0 %all-to-all-start.7 = ((bf16[8,32,2304]{2,1,0:T(8,128)(2,1)}), bf16[8,32,2304]{2,1,0:T(8,128)(2,1)S(1)}, u32[]{:S(2)}, u32[]{:S(2)}) async-start(bf16[8,32,2304]{2,1,0:T(8,128)(2,1)} %copy-done.17), calls=%async_computation.7 | async-start | bytes 2359296 | tf_op jit(solution)/shard_map/all_to_all | solution.py:572
  248.0 2.2 collective-permute-start.14
  250.5 14.2 %all-to-all-done.7.parts_ref = bf16[8,32,2304]{2,1,0:T(8,128)(2,1)S(1)} async-done(((bf16[8,32,2304]{2,1,0:T(8,128)(2,1)}), bf16[8,32,2304]{2,1,0:T(8,128)(2,1)S(1)}, u32[]{:S(2)}, u32[]{:S(2)}) %all-to-all-start.7) | async-done | bytes 1179680 | tf_op jit(solution)/shard_map/all_to_all | solution.py:572
  268.3 7.5 %collective-permute-done.14.refs_3_ = bf16[128,2176]{1,0:T(8,128)(2,1)} collective-permute-done((bf16[128,2176]{1,0:T(8,128)(2,1)}, bf16[128,2176]{1,0:T(8,128)(2,1)}, u32[]{:S(2)}, u32[]{:S(2)}) %collective-permute-start.14) | collective-permute-done | bytes 557088 | tf_op jit(solution)/shard_map/ppermute | solution.py:536
  276.7 3.3 %finish.1 = (bf16[128,2048]{1,0:T(8,128)(2,1)}, f32[8,128]{1,0:T(8,128)}) custom-call(bf16[128,2176]{1,0:T(8,128)(2,1)S(1)} %get-tuple-element.31.refs_17_.refs_0_, bf16[128,2176]{1,0:T(8,128)(2,1)S(1)} %collective-permute-done.13.refs_1_, bf16[128,2176]{1,0:T(8,128)(2,1)S(1)} %copy-done.30, bf16[128,2176]{1,0:T(8,128)(2,1)} %collective-permute-done.14.refs_3_, ...), custom_call_target="tpu_custom_call" | custom-call | tf_op jit(solution)/shard_map/finish/pallas_call | solution.py:650
  (227 shorter events, 52.3 us)
Async XLA Ops:
  0.6 15.9 %copy-start = (s32[1,1024]{1,0:T(1,128)S(1)}, s32[1,1024]{1,0:T(1,128)}, u32[]{:S(2)}) copy-start(s32[1,1024]{1,0:T(1,128)} %param.18) | copy-start | bytes 12292
  2.6 8.6 %copy-start.76 = (f32[1,128,8]{1,2,0:T(8,128)S(1)}, f32[1,128,8]{1,2,0:T(8,128)}, u32[]{:S(2)}) copy-start(f32[1,128,8]{1,2,0:T(8,128)} %param.23) | copy-start | bytes 12292
  2.6 8.7 %copy-start.81 = (s32[1,128,8]{1,2,0:T(8,128)S(1)}, s32[1,128,8]{1,2,0:T(8,128)}, u32[]{:S(2)}) copy-start(s32[1,128,8]{1,2,0:T(8,128)} %param.22) | copy-start | bytes 12292
  2.6 9.8 %copy-start.74 = (bf16[1,128,2048]{2,1,0:T(8,128)(2,1)S(1)}, bf16[1,128,2048]{2,1,0:T(8,128)(2,1)}, u32[]{:S(2)}) copy-start(bf16[1,128,2048]{2,1,0:T(8,128)(2,1)} %param.19) | copy-start | bytes 1572868
  2.6 20.7 %all-to-all-start = ((bf16[8,128,512]{2,1,0:T(8,128)(2,1)}), bf16[8,128,512]{2,1,0:T(8,128)(2,1)S(1)}, u32[]{:S(2)}, u32[]{:S(2)}) async-start(bf16[8,128,512]{2,1,0:T(8,128)(2,1)} %broadcast_in_dim.20.refs_1_), calls=%async_computation | async-start | bytes 2097152 | tf_op jit(solution)/shard_map/all_to_all | solution.py:572
  9.6 11.6 %collective-permute-start.1 = (bf16[256,512]{1,0:T(8,128)(2,1)}, bf16[256,512]{1,0:T(8,128)(2,1)S(1)}, u32[]{:S(2)}, u32[]{:S(2)}) collective-permute-start(bf16[256,512]{1,0:T(8,128)(2,1)} %after.6), channel_id=1, source_target_pairs={{0,1},{1,0},{2,3},{3,2},{4,5},{5,4},{6,7},{7,6},{8,9},{9,8},{10,11... | collective-permute-start | bytes 786440 | tf_op jit(solution)/shard_map/ppermute | solution.py:536
  14.0 16.6 %collective-permute-start = (bf16[144,1024]{1,0:T(8,128)(2,1)}, bf16[144,1024]{1,0:T(8,128)(2,1)S(1)}, u32[]{:S(2)}, u32[]{:S(2)}) collective-permute-start(bf16[144,1024]{1,0:T(8,128)(2,1)} %after.5), channel_id=1, source_target_pairs={{0,2},{1,3},{2,0},{3,1},{4,6},{5,7},{6,4},{7,5},{8,10},{9,11},{10,... | collective-permute-start | bytes 884744 | tf_op jit(solution)/shard_map/ppermute | solution.py:536
  31.3 6.7 %copy-start.82 = (f32[2048]{0:T(1024)S(1)}, f32[2048]{0:T(1024)}, u32[]{:S(2)}) copy-start(f32[2048]{0:T(1024)} %param.21) | copy-start | bytes 24580
  31.3 6.8 %copy-start.22 = (bf16[144,1024]{1,0:T(8,128)(2,1)S(1)}, bf16[144,1024]{1,0:T(8,128)(2,1)}, u32[]{:S(2)}) copy-start(bf16[144,1024]{1,0:T(8,128)(2,1)} %copy-done.21) | copy-start | bytes 884740
  31.3 31.2 %all-to-all-start.1 = ((bf16[8,256,512]{2,1,0:T(8,128)(2,1)}), bf16[8,256,512]{2,1,0:T(8,128)(2,1)S(1)}, u32[]{:S(2)}, u32[]{:S(2)}) async-start(bf16[8,256,512]{2,1,0:T(8,128)(2,1)} %after.7), calls=%async_computation.1 | async-start | bytes 4194304 | tf_op jit(solution)/shard_map/all_to_all | solution.py:572
  35.3 26.4 %collective-permute-start.2 = (bf16[128,2048]{1,0:T(8,128)(2,1)S(1)}, bf16[128,2048]{1,0:T(8,128)(2,1)S(1)}, u32[]{:S(2)}, u32[]{:S(2)}) collective-permute-start(bf16[128,2048]{1,0:T(8,128)(2,1)S(1)} %copy-done.20), channel_id=1, source_target_pairs={{0,2},{1,3},{2,0},{3,1},{4,6},{5,7},{6,4},{7,5},{8,10},{9,11},{10,... | collective-permute-start | bytes 1572872 | tf_op jit(solution)/shard_map/ppermute | solution.py:536
  67.5 22.2 %copy-start.40 = (bf16[1,32,2048]{2,1,0:T(8,128)(2,1)S(1)}, bf16[1,32,2048]{2,1,0:T(8,128)(2,1)}, u32[]{:S(2)}) copy-start(bf16[1,32,2048]{2,1,0:T(8,128)(2,1)} %param.28) | copy-start | bytes 393220
  69.0 20.7 %all-to-all-start.2 = ((bf16[8,72,1024]{2,1,0:T(8,128)(2,1)}), bf16[8,72,1024]{2,1,0:T(8,128)(2,1)S(1)}, u32[]{:S(2)}, u32[]{:S(2)}) async-start(bf16[8,72,1024]{2,1,0:T(8,128)(2,1)} %bitcast.75), calls=%async_computation.2 | async-start | bytes 2359296 | tf_op jit(solution)/shard_map/all_to_all | solution.py:572
  72.9 26.7 %collective-permute-start.7 = (bf16[272,1024]{1,0:T(8,128)(2,1)S(1)}, bf16[272,1024]{1,0:T(8,128)(2,1)S(1)}, u32[]{:S(2)}, u32[]{:S(2)}) collective-permute-start(bf16[272,1024]{1,0:T(8,128)(2,1)S(1)} %project.1.refs_2_), channel_id=1, source_target_pairs={{0,1},{1,0},{2,3},{3,2},{4,5},{5,4},{6,7},{7,6},{8,9},{9,8},{10,11... | collective-permute-start | bytes 1671176 | tf_op jit(solution)/shard_map/ppermute | solution.py:536
  72.9 28.0 %collective-permute-start.3 = (bf16[272,1024]{1,0:T(8,128)(2,1)S(1)}, bf16[272,1024]{1,0:T(8,128)(2,1)S(1)}, u32[]{:S(2)}, u32[]{:S(2)}) collective-permute-start(bf16[272,1024]{1,0:T(8,128)(2,1)S(1)} %project.1.refs_2_), channel_id=1, source_target_pairs={{0,2},{1,3},{2,0},{3,1},{4,6},{5,7},{6,4},{7,5},{8,10},{9,11},{10,... | collective-permute-start | bytes 1671176 | tf_op jit(solution)/shard_map/ppermute | solution.py:536
  89.7 12.8 %copy-start.6 = (bf16[8,72,1024]{2,1,0:T(8,128)(2,1)}, bf16[8,72,1024]{2,1,0:T(8,128)(2,1)S(1)}, u32[]{:S(2)}) copy-start(bf16[8,72,1024]{2,1,0:T(8,128)(2,1)S(1)} %all-to-all-done.2) | copy-start | bytes 3538948
  89.7 12.8 %copy-start.57 = (bf16[32,2048]{1,0:T(8,128)(2,1)}, bf16[32,2048]{1,0:T(8,128)(2,1)S(1)}, u32[]{:S(2)}) copy-start(bf16[32,2048]{1,0:T(8,128)(2,1)S(1)} %later.2.refs_1_) | copy-start | bytes 393220
  89.7 11.2 %collective-permute-start.6 = (bf16[32,2048]{1,0:T(8,128)(2,1)S(1)}, bf16[32,2048]{1,0:T(8,128)(2,1)S(1)}, u32[]{:S(2)}, u32[]{:S(2)}) collective-permute-start(bf16[32,2048]{1,0:T(8,128)(2,1)S(1)} %later.2.refs_1_), channel_id=1, source_target_pairs={{0,24},{4,28},{8,16},{12,20},{16,8},{20,12},{24,0},{28,4},{1,25},{... | collective-permute-start | bytes 393224 | tf_op jit(solution)/shard_map/ppermute | solution.py:541
  90.4 10.5 %collective-permute-start.5 = (bf16[32,2048]{1,0:T(8,128)(2,1)S(1)}, bf16[32,2048]{1,0:T(8,128)(2,1)S(1)}, u32[]{:S(2)}, u32[]{:S(2)}) collective-permute-start(bf16[32,2048]{1,0:T(8,128)(2,1)S(1)} %later.2.refs_1_), channel_id=1, source_target_pairs={{0,16},{4,20},{8,24},{12,28},{16,0},{20,4},{24,8},{28,12},{1,17},{... | collective-permute-start | bytes 393224 | tf_op jit(solution)/shard_map/ppermute | solution.py:541
  91.8 9.2 %collective-permute-start.4 = (bf16[32,2048]{1,0:T(8,128)(2,1)S(1)}, bf16[32,2048]{1,0:T(8,128)(2,1)S(1)}, u32[]{:S(2)}, u32[]{:S(2)}) collective-permute-start(bf16[32,2048]{1,0:T(8,128)(2,1)S(1)} %later.2.refs_1_), channel_id=1, source_target_pairs={{0,8},{4,12},{8,0},{12,4},{16,24},{20,28},{24,16},{28,20},{1,9},{5... | collective-permute-start | bytes 393224 | tf_op jit(solution)/shard_map/ppermute | solution.py:541
  102.5 22.2 %all-to-all-start.3 = ((bf16[8,72,1152]{2,1,0:T(8,128)(2,1)}), bf16[8,72,1152]{2,1,0:T(8,128)(2,1)S(1)}, u32[]{:S(2)}, u32[]{:S(2)}) async-start(bf16[8,72,1152]{2,1,0:T(8,128)(2,1)} %bitcast.22), calls=%async_computation.3 | async-start | bytes 2654208 | tf_op jit(solution)/shard_map/all_to_all | solution.py:572
  106.4 15.0 %collective-permute-start.8 = (bf16[272,1024]{1,0:T(8,128)(2,1)S(1)}, bf16[272,1024]{1,0:T(8,128)(2,1)S(1)}, u32[]{:S(2)}, u32[]{:S(2)}) collective-permute-start(bf16[272,1024]{1,0:T(8,128)(2,1)S(1)} %collective-permute-done.3.refs_3_), channel_id=1, source_target_pairs={{0,1},{1,0},{2,3},{3,2},{4,5},{5,4},{6,7},{7,6},{8,9},{9,8},{10,11... | collective-permute-start | bytes 1671176 | tf_op jit(solution)/shard_map/ppermute | solution.py:536
  106.9 15.3 %copy-start.62 = (s32[8,256]{1,0:T(8,128)}, s32[8,256]{1,0:T(8,128)S(1)}, u32[]{:S(2)}) copy-start(s32[8,256]{1,0:T(8,128)S(1)} %get-tuple-element.27.refs_1_.refs_0_.refs_3_.refs_13_) | copy-start | bytes 24580
  106.9 15.3 %copy-start.68 = (f32[8,256]{1,0:T(8,128)}, f32[8,256]{1,0:T(8,128)S(1)}, u32[]{:S(2)}) copy-start(f32[8,256]{1,0:T(8,128)S(1)} %get-tuple-element.33.refs_1_.refs_14_) | copy-start | bytes 24580
  125.9 9.6 %copy-start.2 = (bf16[1,2048,768]{2,1,0:T(8,128)(2,1)S(1)}, bf16[1,2048,768]{2,1,0:T(8,128)(2,1)}, u32[]{:S(2)}) copy-start(bf16[1,2048,768]{2,1,0:T(8,128)(2,1)} %param.24) | copy-start | bytes 9437188
  125.9 35.7 %all-to-all-start.5 = ((bf16[8,72,2176]{2,1,0:T(8,128)(2,1)}), bf16[8,72,2176]{2,1,0:T(8,128)(2,1)}, u32[]{:S(2)}, u32[]{:S(2)}) async-start(bf16[8,72,2176]{2,1,0:T(8,128)(2,1)} %bitcast.70), calls=%async_computation.5 | async-start | bytes 5013504 | tf_op jit(solution)/shard_map/all_to_all | solution.py:572
  133.5 26.4 %collective-permute-start.9 = (bf16[128,2048]{1,0:T(8,128)(2,1)}, bf16[128,2048]{1,0:T(8,128)(2,1)}, u32[]{:S(2)}, u32[]{:S(2)}) collective-permute-start(bf16[128,2048]{1,0:T(8,128)(2,1)} %later.3.refs_2_.refs_11_.refs_3_), channel_id=1, source_target_pairs={{0,2},{1,3},{2,0},{3,1},{4,6},{5,7},{6,4},{7,5},{8,10},{9,11},{10,... | collective-permute-start | bytes 1572872 | tf_op jit(solution)/shard_map/ppermute | solution.py:536
  161.6 34.6 %all-to-all-start.4 = ((bf16[8,72,2176]{2,1,0:T(8,128)(2,1)}), bf16[8,72,2176]{2,1,0:T(8,128)(2,1)S(1)}, u32[]{:S(2)}, u32[]{:S(2)}) async-start(bf16[8,72,2176]{2,1,0:T(8,128)(2,1)} %bitcast.72), calls=%async_computation.4 | async-start | bytes 5013504 | tf_op jit(solution)/shard_map/all_to_all | solution.py:572
  165.4 20.7 %collective-permute-start.10 = (bf16[128,2048]{1,0:T(8,128)(2,1)}, bf16[128,2048]{1,0:T(8,128)(2,1)S(1)}, u32[]{:S(2)}, u32[]{:S(2)}) collective-permute-start(bf16[128,2048]{1,0:T(8,128)(2,1)} %later.3.refs_2_.refs_11_.refs_3_), channel_id=1, source_target_pairs={{0,1},{1,0},{2,3},{3,2},{4,5},{5,4},{6,7},{7,6},{8,9},{9,8},{10,11... | collective-permute-start | bytes 1572872 | tf_op jit(solution)/shard_map/ppermute | solution.py:536
  165.8 25.1 %collective-permute-start.11 = (bf16[128,2048]{1,0:T(8,128)(2,1)}, bf16[128,2048]{1,0:T(8,128)(2,1)S(1)}, u32[]{:S(2)}, u32[]{:S(2)}) collective-permute-start(bf16[128,2048]{1,0:T(8,128)(2,1)} %collective-permute-done.9.refs_1_.refs_3_.refs_12_.refs_4_), channel_id=1, source_target_pairs={{0,1},{1,0},{2,3},{3,2},{4,5},{5,4},{6,7},{7,6},{8,9},{9,8},{10,11... | collective-permute-start | bytes 1572872 | tf_op jit(solution)/shard_map/ppermute | solution.py:536
  171.3 11.1 %copy-start.66 = (f32[8,256]{1,0:T(8,128)S(1)}, f32[8,256]{1,0:T(8,128)}, u32[]{:S(2)}) copy-start(f32[8,256]{1,0:T(8,128)} %copy-done.65) | copy-start | bytes 24580
  171.3 19.6 %copy-start.63 = (s32[8,256]{1,0:T(8,128)S(1)}, s32[8,256]{1,0:T(8,128)}, u32[]{:S(2)}) copy-start(s32[8,256]{1,0:T(8,128)} %copy-done.62) | copy-start | bytes 24580
  171.3 19.6 %copy-start.69 = (f32[8,256]{1,0:T(8,128)S(1)}, f32[8,256]{1,0:T(8,128)}, u32[]{:S(2)}) copy-start(f32[8,256]{1,0:T(8,128)} %copy-done.68) | copy-start | bytes 24580
  182.4 10.9 %copy-start.44 = (bf16[576,768]{1,0:T(8,128)(2,1)}, bf16[576,768]{1,0:T(8,128)(2,1)S(1)}, u32[]{:S(2)}) copy-start(bf16[576,768]{1,0:T(8,128)(2,1)S(1)} %get-tuple-element.28.refs_4_.refs_1_) | copy-start | bytes 2654212
  186.1 5.6 %copy-start.31 = (bf16[128,2048]{1,0:T(8,128)(2,1)}, bf16[128,2048]{1,0:T(8,128)(2,1)S(1)}, u32[]{:S(2)}) copy-start(bf16[128,2048]{1,0:T(8,128)(2,1)S(1)} %collective-permute-done.10.refs_2_.refs_15_.refs_7_) | copy-start | bytes 1572868
  196.2 35.9 %all-to-all-start.6 = ((bf16[8,72,2176]{2,1,0:T(8,128)(2,1)}), bf16[8,72,2176]{2,1,0:T(8,128)(2,1)}, u32[]{:S(2)}, u32[]{:S(2)}) async-start(bf16[8,72,2176]{2,1,0:T(8,128)(2,1)} %bitcast.71), calls=%async_computation.6 | async-start | bytes 5013504 | tf_op jit(solution)/shard_map/all_to_all | solution.py:572
  203.6 27.6 %collective-permute-start.12 = (bf16[128,2176]{1,0:T(8,128)(2,1)S(1)}, bf16[128,2176]{1,0:T(8,128)(2,1)S(1)}, u32[]{:S(2)}, u32[]{:S(2)}) collective-permute-start(bf16[128,2176]{1,0:T(8,128)(2,1)S(1)} %get-tuple-element.36), channel_id=1, source_target_pairs={{0,2},{1,3},{2,0},{3,1},{4,6},{5,7},{6,4},{7,5},{8,10},{9,11},{10,... | collective-permute-start | bytes 1671176 | tf_op jit(solution)/shard_map/ppermute | solution.py:536
  204.8 1.3 collective-permute-start.15
  204.8 1.5 collective-permute-start.18
  205.3 1.3 collective-permute-start.17
  205.4 1.5 collective-permute-start.16
  243.8 6.5 %copy-start.73 = (f32[1,128,8]{2,1,0:T(8,128)S(1)}, f32[1,128,8]{2,1,0:T(8,128)}, u32[]{:S(2)}) copy-start(f32[1,128,8]{2,1,0:T(8,128)} %copy-done.72) | copy-start | bytes 12292
  243.9 6.5 %copy-start.78 = (f32[128]{0:T(128)S(1)}, f32[128]{0:T(128)}, u32[]{:S(2)}) copy-start(f32[128]{0:T(128)} %copy-done.77) | copy-start | bytes 1540
  243.9 6.5 %copy-start.80 = (f32[128]{0:T(128)S(1)}, f32[128]{0:T(128)}, u32[]{:S(2)}) copy-start(f32[128]{0:T(128)} %copy-done.79) | copy-start | bytes 1540
  243.9 31.9 %copy-start.30 = (bf16[128,2176]{1,0:T(8,128)(2,1)S(1)}, bf16[128,2176]{1,0:T(8,128)(2,1)}, u32[]{:S(2)}) copy-start(bf16[128,2176]{1,0:T(8,128)(2,1)} %copy-done.28) | copy-start | bytes 1671172
  243.9 20.8 %all-to-all-start.7 = ((bf16[8,32,2304]{2,1,0:T(8,128)(2,1)}), bf16[8,32,2304]{2,1,0:T(8,128)(2,1)S(1)}, u32[]{:S(2)}, u32[]{:S(2)}) async-start(bf16[8,32,2304]{2,1,0:T(8,128)(2,1)} %copy-done.17), calls=%async_computation.7 | async-start | bytes 2359296 | tf_op jit(solution)/shard_map/all_to_all | solution.py:572
  247.9 27.8 %collective-permute-start.13 = (bf16[128,2176]{1,0:T(8,128)(2,1)}, bf16[128,2176]{1,0:T(8,128)(2,1)S(1)}, u32[]{:S(2)}, u32[]{:S(2)}) collective-permute-start(bf16[128,2176]{1,0:T(8,128)(2,1)} %copy-done.46), channel_id=1, source_target_pairs={{0,1},{1,0},{2,3},{3,2},{4,5},{5,4},{6,7},{7,6},{8,9},{9,8},{10,11... | collective-permute-start | bytes 1671176 | tf_op jit(solution)/shard_map/ppermute | solution.py:536
  248.0 27.8 %collective-permute-start.14 = (bf16[128,2176]{1,0:T(8,128)(2,1)}, bf16[128,2176]{1,0:T(8,128)(2,1)}, u32[]{:S(2)}, u32[]{:S(2)}) collective-permute-start(bf16[128,2176]{1,0:T(8,128)(2,1)} %copy-done.71), channel_id=1, source_target_pairs={{0,3},{1,2},{2,1},{3,0},{4,7},{5,6},{6,5},{7,4},{8,11},{9,10},{10,... | collective-permute-start | bytes 1671176 | tf_op jit(solution)/shard_map/ppermute | solution.py:536
  (62 other events, 112.0 us)

commit v6 on v5

--- a/solution.py
+++ b/solution.py
@@ -428,7 +428,7 @@
         in_specs=in_specs + [anywhere()],
         out_specs=pl.BlockSpec((groups, rank, width + wide), lambda i: (0, 0, 0)),
         out_shape=jax.ShapeDtypeStruct((groups, rank, width + wide), BF16),
-        compiler_params=params(),
+        compiler_params=params(56),
         cost_estimate=cost(4 * near * groups * rank * width, 4 * near * width),
         name="gradient",
     )(*operands, earlier)
@@ -487,7 +487,7 @@
             jax.ShapeDtypeStruct((count, units), BF16),
             jax.ShapeDtypeStruct((count, width + 128), BF16),
         ],
-        compiler_params=params(40),
+        compiler_params=params(50),
         cost_estimate=cost(0, 0),
         name="expert",
     )(pair.reshape(1), *parts, *weights)
@@ -615,7 +615,7 @@
             jax.ShapeDtypeStruct((rank, width), F32),
             jax.ShapeDtypeStruct((rank, actives[0].shape[1]), F32),
         ],
-        compiler_params=params(),
+        compiler_params=params(56),
         name="gradients",
     )(parts, *actives)
 

time: 282 us -> 277 us (0.982)
  local copies, waits for them, and re-layouts: 50.8 us -> 29.9 us
  waiting for transfers between devices: 125 us -> 133 us
  Pallas kernels: 45.1 us -> 52.2 us
    unnamed x169 -> x131, local copies, waits for them, and re-layouts: 45.8 us -> 24.9 us
    ppermute x12, waiting for transfers between devices: 90.1 us -> 98.8 us  [from_plane(): return lax.ppermute(x, 'expert', [(i, i ^ r) for i in range(size)])]
    pallas_call x2, Pallas kernels: 18.8 us -> 23.7 us  [expert(): pl.pallas_call(lambda *refs: expert_kernel(*refs, cols=cols), grid=(count...]
  transfers between devices with their start and end apart: 27 -> 27, of which waited for: 20 -> 20; matrix products, arithmetic and copies ran while one was open for 3% -> 2% of each run, Pallas kernels for 12% -> 14%
where the time goes in v6:
time: 277 us; the launch traced here: 276 us
  waiting for transfers between devices  133 us (48%)
  starting transfers between devices  56.3 us (20%)
  Pallas kernels  52.2 us (19%)
  local copies, waits for them, and re-layouts  29.9 us (11%)
  other arithmetic  3.14 us (1%)
    ppermute x12, waiting for transfers between devices, from_plane(): return lax.ppermute(x, 'expert', [(i, i ^ r) for i in range(size)])  98.8 us
    all_to_all x8, starting transfers between devices, swap(): return lax.all_to_all(x, 'seq', split_axis=0, concat_axis=0, tiled=True)  34.3 us
    all_to_all x8, waiting for transfers between devices, swap(): return lax.all_to_all(x, 'seq', split_axis=0, concat_axis=0, tiled=True)  33.1 us
    unnamed x131, local copies, waits for them, and re-layouts  24.9 us
    pallas_call x2, Pallas kernels, expert(): pl.pallas_call(lambda *refs: expert_kernel(*refs, cols=cols), grid=(count...  23.7 us
    ppermute x12, starting transfers between devices, from_plane(): return lax.ppermute(x, 'expert', [(i, i ^ r) for i in range(size)])  17.5 us
  transfers between devices with their start and end apart: 27, of which 20 were waited for; matrix products, arithmetic and copies ran while one was open for 2% of the time, Pallas kernels for 14%

profile of v6, /device:TPU:0, one launch (start us, length us, event | category | flops | bytes accessed | tf_op | source)
XLA Modules:
  0.0 275.7 jit_solution(7227958475573242837)
XLA Ops:
  2.6 5.3 %all-to-all-start = ((bf16[8,128,512]{2,1,0:T(8,128)(2,1)}), bf16[8,128,512]{2,1,0:T(8,128)(2,1)S(1)}, u32[]{:S(2)}, u32[]{:S(2)}) async-start(bf16[8,128,512]{2,1,0:T(8,128)(2,1)} %broadcast_in_dim.20.refs_1_), calls=%async_computation | async-start | bytes 2097152 | tf_op jit(solution)/shard_map/all_to_all | solution.py:572
  7.9 1.7 constant_dynamic-slice_fusion.refs_0_
  9.6 1.6 collective-permute-start.1
  13.4 2.6 collective-permute-start
  16.8 5.0 %collective-permute-done.1 = bf16[256,512]{1,0:T(8,128)(2,1)S(1)} collective-permute-done((bf16[256,512]{1,0:T(8,128)(2,1)}, bf16[256,512]{1,0:T(8,128)(2,1)S(1)}, u32[]{:S(2)}, u32[]{:S(2)}) %collective-permute-start.1) | collective-permute-done | bytes 262176 | tf_op jit(solution)/shard_map/ppermute | solution.py:536
  21.8 1.5 all-to-all-done
  25.6 3.5 %attend.1.refs_1_.refs_0_ = bf16[128,2048]{1,0:T(8,128)(2,1)S(1)} custom-call(s32[1]{0:T(128)} %bitcast.12.start_ref, bf16[128,2048]{1,0:T(8,128)(2,1)S(1)} %bitcast.77, bf16[1024,512]{1,0:T(8,128)(2,1)S(1)} %bitcast.70, f32[128,640]{1,0:T(8,128)S(1)} %copy-done.31, bf16[8,256,512]{2,1,0:T(8,128)(2,1)S(1)} %broadcast_in_dim.23.refs_0_), custom_call_target="tpu_custom_call" | custom-call | tf_op jit(solution)/shard_map/attend/pallas_call | solution.py:73
  30.7 4.0 %all-to-all-start.1 = ((bf16[8,256,512]{2,1,0:T(8,128)(2,1)}), bf16[8,256,512]{2,1,0:T(8,128)(2,1)S(1)}, u32[]{:S(2)}, u32[]{:S(2)}) async-start(bf16[8,256,512]{2,1,0:T(8,128)(2,1)} %after.7), calls=%async_computation.1 | async-start | bytes 4194304 | tf_op jit(solution)/shard_map/all_to_all | solution.py:572
  34.7 2.3 collective-permute-start.2
  37.3 23.8 %collective-permute-done.2.refs_1_ = bf16[128,2048]{1,0:T(8,128)(2,1)S(1)} collective-permute-done((bf16[128,2048]{1,0:T(8,128)(2,1)S(1)}, bf16[128,2048]{1,0:T(8,128)(2,1)S(1)}, u32[]{:S(2)}, u32[]{:S(2)}) %collective-permute-start.2) | collective-permute-done | bytes 524320 | tf_op jit(solution)/shard_map/ppermute | solution.py:536
  62.0 1.6 copy-done.16
  64.6 1.4 project.1.refs_2_
  66.0 1.5 pick.3
  68.3 4.0 %all-to-all-start.2 = ((bf16[8,72,1024]{2,1,0:T(8,128)(2,1)}), bf16[8,72,1024]{2,1,0:T(8,128)(2,1)S(1)}, u32[]{:S(2)}, u32[]{:S(2)}) async-start(bf16[8,72,1024]{2,1,0:T(8,128)(2,1)} %bitcast.19), calls=%async_computation.2 | async-start | bytes 2359296 | tf_op jit(solution)/shard_map/all_to_all | solution.py:572
  72.6 3.4 %collective-permute-start.3 = (bf16[272,1024]{1,0:T(8,128)(2,1)S(1)}, bf16[272,1024]{1,0:T(8,128)(2,1)S(1)}, u32[]{:S(2)}, u32[]{:S(2)}) collective-permute-start(bf16[272,1024]{1,0:T(8,128)(2,1)S(1)} %copy-done.10), channel_id=1, source_target_pairs={{0,2},{1,3},{2,0},{3,1},{4,6},{5,7},{6,4},{7,5},{8,10},{9,11},{10,... | collective-permute-start | bytes 1671176 | tf_op jit(solution)/shard_map/ppermute | solution.py:536
  76.0 13.1 %all-to-all-done.2 = bf16[8,72,1024]{2,1,0:T(8,128)(2,1)S(1)} async-done(((bf16[8,72,1024]{2,1,0:T(8,128)(2,1)}), bf16[8,72,1024]{2,1,0:T(8,128)(2,1)S(1)}, u32[]{:S(2)}, u32[]{:S(2)}) %all-to-all-start.2) | async-done | bytes 1179680 | tf_op jit(solution)/shard_map/all_to_all | solution.py:572
  89.8 1.4 collective-permute-start.5
  91.2 1.5 collective-permute-start.4
  92.7 6.3 %collective-permute-done.7.refs_7_.refs_1_.refs_2_ = bf16[272,1024]{1,0:T(8,128)(2,1)S(1)} collective-permute-done((bf16[272,1024]{1,0:T(8,128)(2,1)S(1)}, bf16[272,1024]{1,0:T(8,128)(2,1)S(1)}, u32[]{:S(2)}, u32[]{:S(2)}) %collective-permute-start.7) | collective-permute-done | bytes 557088 | tf_op jit(solution)/shard_map/ppermute | solution.py:536
  99.1 1.9 collective-permute-done.3.refs_3_
  101.0 1.5 pick.4.refs_4_
  102.5 3.9 %all-to-all-start.3 = ((bf16[8,72,1152]{2,1,0:T(8,128)(2,1)}), bf16[8,72,1152]{2,1,0:T(8,128)(2,1)S(1)}, u32[]{:S(2)}, u32[]{:S(2)}) async-start(bf16[8,72,1152]{2,1,0:T(8,128)(2,1)} %bitcast.22), calls=%async_computation.3 | async-start | bytes 2654208 | tf_op jit(solution)/shard_map/all_to_all | solution.py:572
  106.9 14.8 %collective-permute-done.8.refs_0_.refs_3_ = bf16[272,1024]{1,0:T(8,128)(2,1)S(1)} collective-permute-done((bf16[272,1024]{1,0:T(8,128)(2,1)}, bf16[272,1024]{1,0:T(8,128)(2,1)S(1)}, u32[]{:S(2)}, u32[]{:S(2)}) %collective-permute-start.8) | collective-permute-done | bytes 557088 | tf_op jit(solution)/shard_map/ppermute | solution.py:536
  122.4 1.5 copy-done.3
  124.8 4.5 %all-to-all-start.5 = ((bf16[8,72,2176]{2,1,0:T(8,128)(2,1)}), bf16[8,72,2176]{2,1,0:T(8,128)(2,1)}, u32[]{:S(2)}, u32[]{:S(2)}) async-start(bf16[8,72,2176]{2,1,0:T(8,128)(2,1)} %bitcast.66), calls=%async_computation.5 | async-start | bytes 5013504 | tf_op jit(solution)/shard_map/all_to_all | solution.py:572
  132.9 12.3 %expert.2 = (bf16[576,768]{1,0:T(8,128)(2,1)S(1)}, bf16[576,2176]{1,0:T(8,128)(2,1)}) custom-call(s32[1]{0:T(128)} %bitcast.refs_0_, bf16[576,1024]{1,0:T(8,128)(2,1)S(1)} %bitcast.65, bf16[576,1152]{1,0:T(8,128)(2,1)S(1)} %bitcast.69, bf16[2048,768]{1,0:T(8,128)(2,1)} %bitcast.80, bf16[2048,768]{1,0:T(8,128)(2,1)} %bitcast.82, ...), custom_call_target="tpu_custom_call" | custom-call | tf_op jit(solution)/shard_map/expert/pallas_call | solution.py:476
  146.1 11.7 %collective-permute-done.9.refs_1_.refs_3_.refs_12_.refs_4_ = bf16[128,2048]{1,0:T(8,128)(2,1)} collective-permute-done((bf16[128,2048]{1,0:T(8,128)(2,1)S(1)}, bf16[128,2048]{1,0:T(8,128)(2,1)}, u32[]{:S(2)}, u32[]{:S(2)}) %collective-permute-start.9) | collective-permute-done | bytes 524320 | tf_op jit(solution)/shard_map/ppermute | solution.py:536
  157.8 2.6 all-to-all-done.5
  160.4 3.8 %all-to-all-start.4 = ((bf16[8,72,2176]{2,1,0:T(8,128)(2,1)}), bf16[8,72,2176]{2,1,0:T(8,128)(2,1)S(1)}, u32[]{:S(2)}, u32[]{:S(2)}) async-start(bf16[8,72,2176]{2,1,0:T(8,128)(2,1)} %bitcast.86), calls=%async_computation.4 | async-start | bytes 5013504 | tf_op jit(solution)/shard_map/all_to_all | solution.py:572
  164.6 1.7 collective-permute-start.11
  166.3 11.4 %expert.3 = (bf16[576,768]{1,0:T(8,128)(2,1)S(1)}, bf16[576,2176]{1,0:T(8,128)(2,1)S(1)}) custom-call(s32[1]{0:T(128)} %bitcast.refs_0_, bf16[576,2176]{1,0:T(8,128)(2,1)} %bitcast.33.refs_1_, bf16[2048,768]{1,0:T(8,128)(2,1)} %bitcast.81, bf16[2048,768]{1,0:T(8,128)(2,1)} %bitcast.83, bf16[768,32]{1,0:T(8,128)(2,1)S(1)} %bitcast.72, ...), custom_call_target="tpu_custom_call" | custom-call | tf_op jit(solution)/shard_map/expert/pallas_call | solution.py:476
  177.7 1.4 copy-done.4
  179.1 2.2 fill.2
  181.3 1.4 copy-done.5
  182.7 6.7 %collective-permute-done.11.refs_3_.refs_16_.refs_8_ = bf16[128,2048]{1,0:T(8,128)(2,1)S(1)} collective-permute-done((bf16[128,2048]{1,0:T(8,128)(2,1)}, bf16[128,2048]{1,0:T(8,128)(2,1)S(1)}, u32[]{:S(2)}, u32[]{:S(2)}) %collective-permute-start.11) | collective-permute-done | bytes 524320 | tf_op jit(solution)/shard_map/ppermute | solution.py:536
  192.4 2.5 all-to-all-done.4
  195.0 4.4 %all-to-all-start.6 = ((bf16[8,72,2176]{2,1,0:T(8,128)(2,1)}), bf16[8,72,2176]{2,1,0:T(8,128)(2,1)}, u32[]{:S(2)}, u32[]{:S(2)}) async-start(bf16[8,72,2176]{2,1,0:T(8,128)(2,1)} %bitcast.67), calls=%async_computation.6 | async-start | bytes 5013504 | tf_op jit(solution)/shard_map/all_to_all | solution.py:572
  199.4 1.7 copy-done.6
  205.7 2.9 %back_low.1.refs_0_ = bf16[8,32,256]{2,1,0:T(8,128)(2,1)S(1)} custom-call(s32[1]{0:T(128)} %bitcast.36.refs_0_, bf16[32,2048]{1,0:T(8,128)(2,1)S(1)} %copy-done.49, bf16[32,2048]{1,0:T(8,128)(2,1)S(1)} %copy-done.47, bf16[32,2048]{1,0:T(8,128)(2,1)S(1)} %copy-done.45, bf16[32,2048]{1,0:T(8,128)(2,1)S(1)} %copy-done.43, ...), custom_call_target="tpu_custom_call" | custom-call | flops 536870912 | bytes 2097152 | tf_op jit(solution)/shard_map/back_low/pallas_call | solution.py:378
  209.3 20.7 %collective-permute-done.12.refs_4_.refs_2_ = bf16[128,2176]{1,0:T(8,128)(2,1)S(1)} collective-permute-done((bf16[128,2176]{1,0:T(8,128)(2,1)S(1)}, bf16[128,2176]{1,0:T(8,128)(2,1)S(1)}, u32[]{:S(2)}, u32[]{:S(2)}) %collective-permute-start.12) | collective-permute-done | bytes 557088 | tf_op jit(solution)/shard_map/ppermute | solution.py:536
  231.8 3.0 %combine.3 = (bf16[128,2176]{1,0:T(8,128)(2,1)S(1)}, bf16[128,2176]{1,0:T(8,128)(2,1)S(1)}) custom-call(bf16[576,2176]{1,0:T(8,128)(2,1)} %bitcast.35.refs_0_.refs_5_, bf16[256,576]{1,0:T(8,128)(2,1)S(1)} %copy-done.30, bf16[576,2048]{1,0:T(8,128)(2,1)S(1)} %copy-done.8, s32[8,256]{1,0:T(8,128)S(1)} %get-tuple-element.27.refs_1_.refs_0_.refs_3_.refs_13_, ...), custom_call_target="tpu_custom_call" | custom-call | flops 603979776 | bytes 3407872 | tf_op jit(solution)/shard_map/combine/pallas_call | solution.py:523
  236.5 4.0 %gradient.1 = bf16[8,32,2304]{2,1,0:T(8,128)(2,1)} custom-call(bf16[8,32,256]{2,1,0:T(8,128)(2,1)} %copy-done.39, bf16[576,2176]{1,0:T(8,128)(2,1)} %bitcast.63, bf16[256,576]{1,0:T(8,128)(2,1)} %copy-done.28, bf16[128,2048]{1,0:T(8,128)(2,1)} %copy-done.11, bf16[128,2048]{1,0:T(8,128)(2,1)} %collective-permute-done.9.refs_1_.refs_3_.refs_12_.refs_4_, ...), custom_call_target="tpu_custom_call" | custom-call | flops 536870912 | bytes 2097152 | tf_op jit(solution)/shard_map/gradient/pallas_call | solution.py:425
  240.5 4.4 %all-to-all-start.7 = ((bf16[8,32,2304]{2,1,0:T(8,128)(2,1)}), bf16[8,32,2304]{2,1,0:T(8,128)(2,1)}, u32[]{:S(2)}, u32[]{:S(2)}) async-start(bf16[8,32,2304]{2,1,0:T(8,128)(2,1)} %gradient.1), calls=%async_computation.7 | async-start | bytes 2359296 | tf_op jit(solution)/shard_map/all_to_all | solution.py:572
  245.0 2.3 collective-permute-start.14
  248.5 13.3 %all-to-all-done.7.parts_ref = bf16[8,32,2304]{2,1,0:T(8,128)(2,1)} async-done(((bf16[8,32,2304]{2,1,0:T(8,128)(2,1)}), bf16[8,32,2304]{2,1,0:T(8,128)(2,1)}, u32[]{:S(2)}, u32[]{:S(2)}) %all-to-all-start.7) | async-done | bytes 1179680 | tf_op jit(solution)/shard_map/all_to_all | solution.py:572
  261.7 3.0 %gradients.1 = (f32[32,2048]{1,0:T(8,128)}, f32[32,768]{1,0:T(8,128)}) custom-call(bf16[8,32,2304]{2,1,0:T(8,128)(2,1)} %all-to-all-done.7.parts_ref, bf16[576,768]{1,0:T(8,128)(2,1)} %copy-done.34, bf16[576,768]{1,0:T(8,128)(2,1)} %copy-done.35), custom_call_target="tpu_custom_call" | custom-call | tf_op jit(solution)/shard_map/gradients/pallas_call | solution.py:610
  264.7 7.7 %collective-permute-done.14.refs_3_ = bf16[128,2176]{1,0:T(8,128)(2,1)S(1)} collective-permute-done((bf16[128,2176]{1,0:T(8,128)(2,1)S(1)}, bf16[128,2176]{1,0:T(8,128)(2,1)S(1)}, u32[]{:S(2)}, u32[]{:S(2)}) %collective-permute-start.14) | collective-permute-done | bytes 557088 | tf_op jit(solution)/shard_map/ppermute | solution.py:536
  273.4 2.3 finish.1
  (189 shorter events, 33.6 us)
Async XLA Ops:
  0.6 15.3 %copy-start = (s32[1,1024]{1,0:T(1,128)S(1)}, s32[1,1024]{1,0:T(1,128)}, u32[]{:S(2)}) copy-start(s32[1,1024]{1,0:T(1,128)} %param.18) | copy-start | bytes 12292
  2.6 8.6 %copy-start.61 = (f32[1,128,8]{1,2,0:T(8,128)S(1)}, f32[1,128,8]{1,2,0:T(8,128)}, u32[]{:S(2)}) copy-start(f32[1,128,8]{1,2,0:T(8,128)} %param.23) | copy-start | bytes 12292
  2.6 8.7 %copy-start.62 = (s32[1,128,8]{1,2,0:T(8,128)S(1)}, s32[1,128,8]{1,2,0:T(8,128)}, u32[]{:S(2)}) copy-start(s32[1,128,8]{1,2,0:T(8,128)} %param.22) | copy-start | bytes 12292
  2.6 9.2 %copy-start.56 = (bf16[1,128,2048]{2,1,0:T(8,128)(2,1)S(1)}, bf16[1,128,2048]{2,1,0:T(8,128)(2,1)}, u32[]{:S(2)}) copy-start(bf16[1,128,2048]{2,1,0:T(8,128)(2,1)} %param.19) | copy-start | bytes 1572868
  2.6 20.7 %all-to-all-start = ((bf16[8,128,512]{2,1,0:T(8,128)(2,1)}), bf16[8,128,512]{2,1,0:T(8,128)(2,1)S(1)}, u32[]{:S(2)}, u32[]{:S(2)}) async-start(bf16[8,128,512]{2,1,0:T(8,128)(2,1)} %broadcast_in_dim.20.refs_1_), calls=%async_computation | async-start | bytes 2097152 | tf_op jit(solution)/shard_map/all_to_all | solution.py:572
  9.6 12.2 %collective-permute-start.1 = (bf16[256,512]{1,0:T(8,128)(2,1)}, bf16[256,512]{1,0:T(8,128)(2,1)S(1)}, u32[]{:S(2)}, u32[]{:S(2)}) collective-permute-start(bf16[256,512]{1,0:T(8,128)(2,1)} %after.6), channel_id=1, source_target_pairs={{0,1},{1,0},{2,3},{3,2},{4,5},{5,4},{6,7},{7,6},{8,9},{9,8},{10,11... | collective-permute-start | bytes 786440 | tf_op jit(solution)/shard_map/ppermute | solution.py:536
  13.4 16.6 %collective-permute-start = (bf16[144,1024]{1,0:T(8,128)(2,1)}, bf16[144,1024]{1,0:T(8,128)(2,1)S(1)}, u32[]{:S(2)}, u32[]{:S(2)}) collective-permute-start(bf16[144,1024]{1,0:T(8,128)(2,1)} %after.5), channel_id=1, source_target_pairs={{0,2},{1,3},{2,0},{3,1},{4,6},{5,7},{6,4},{7,5},{8,10},{9,11},{10,... | collective-permute-start | bytes 884744 | tf_op jit(solution)/shard_map/ppermute | solution.py:536
  30.7 6.3 %copy-start.57 = (bf16[128,512]{1,0:T(8,128)(2,1)S(1)}, bf16[128,512]{1,0:T(8,128)(2,1)}, u32[]{:S(2)}) copy-start(bf16[128,512]{1,0:T(8,128)(2,1)} %get-tuple-element.45) | copy-start | bytes 393220
  30.7 6.3 %copy-start.58 = (bf16[128,512]{1,0:T(8,128)(2,1)S(1)}, bf16[128,512]{1,0:T(8,128)(2,1)}, u32[]{:S(2)}) copy-start(bf16[128,512]{1,0:T(8,128)(2,1)} %get-tuple-element.46) | copy-start | bytes 393220
  30.7 6.4 %copy-start.63 = (f32[2048]{0:T(1024)S(1)}, f32[2048]{0:T(1024)}, u32[]{:S(2)}) copy-start(f32[2048]{0:T(1024)} %param.21) | copy-start | bytes 24580
  30.7 6.5 %copy-start.15 = (bf16[144,1024]{1,0:T(8,128)(2,1)S(1)}, bf16[144,1024]{1,0:T(8,128)(2,1)}, u32[]{:S(2)}) copy-start(bf16[144,1024]{1,0:T(8,128)(2,1)} %copy-done.14) | copy-start | bytes 884740
  30.7 31.3 %all-to-all-start.1 = ((bf16[8,256,512]{2,1,0:T(8,128)(2,1)}), bf16[8,256,512]{2,1,0:T(8,128)(2,1)S(1)}, u32[]{:S(2)}, u32[]{:S(2)}) async-start(bf16[8,256,512]{2,1,0:T(8,128)(2,1)} %after.7), calls=%async_computation.1 | async-start | bytes 4194304 | tf_op jit(solution)/shard_map/all_to_all | solution.py:572
  34.7 26.5 %collective-permute-start.2 = (bf16[128,2048]{1,0:T(8,128)(2,1)S(1)}, bf16[128,2048]{1,0:T(8,128)(2,1)S(1)}, u32[]{:S(2)}, u32[]{:S(2)}) collective-permute-start(bf16[128,2048]{1,0:T(8,128)(2,1)S(1)} %copy-done.13), channel_id=1, source_target_pairs={{0,2},{1,3},{2,0},{3,1},{4,6},{5,7},{6,4},{7,5},{8,10},{9,11},{10,... | collective-permute-start | bytes 1572872 | tf_op jit(solution)/shard_map/ppermute | solution.py:536
  66.0 23.1 %copy-start.32 = (bf16[1,32,2048]{2,1,0:T(8,128)(2,1)S(1)}, bf16[1,32,2048]{2,1,0:T(8,128)(2,1)}, u32[]{:S(2)}) copy-start(bf16[1,32,2048]{2,1,0:T(8,128)(2,1)} %param.28) | copy-start | bytes 393220
  68.3 20.8 %all-to-all-start.2 = ((bf16[8,72,1024]{2,1,0:T(8,128)(2,1)}), bf16[8,72,1024]{2,1,0:T(8,128)(2,1)S(1)}, u32[]{:S(2)}, u32[]{:S(2)}) async-start(bf16[8,72,1024]{2,1,0:T(8,128)(2,1)} %bitcast.19), calls=%async_computation.2 | async-start | bytes 2359296 | tf_op jit(solution)/shard_map/all_to_all | solution.py:572
  72.3 26.7 %collective-permute-start.7 = (bf16[272,1024]{1,0:T(8,128)(2,1)S(1)}, bf16[272,1024]{1,0:T(8,128)(2,1)S(1)}, u32[]{:S(2)}, u32[]{:S(2)}) collective-permute-start(bf16[272,1024]{1,0:T(8,128)(2,1)S(1)} %copy-done.10), channel_id=1, source_target_pairs={{0,1},{1,0},{2,3},{3,2},{4,5},{5,4},{6,7},{7,6},{8,9},{9,8},{10,11... | collective-permute-start | bytes 1671176 | tf_op jit(solution)/shard_map/ppermute | solution.py:536
  72.6 28.3 %collective-permute-start.3 = (bf16[272,1024]{1,0:T(8,128)(2,1)S(1)}, bf16[272,1024]{1,0:T(8,128)(2,1)S(1)}, u32[]{:S(2)}, u32[]{:S(2)}) collective-permute-start(bf16[272,1024]{1,0:T(8,128)(2,1)S(1)} %copy-done.10), channel_id=1, source_target_pairs={{0,2},{1,3},{2,0},{3,1},{4,6},{5,7},{6,4},{7,5},{8,10},{9,11},{10,... | collective-permute-start | bytes 1671176 | tf_op jit(solution)/shard_map/ppermute | solution.py:536
  89.1 13.4 %copy-start.48 = (bf16[32,2048]{1,0:T(8,128)(2,1)}, bf16[32,2048]{1,0:T(8,128)(2,1)S(1)}, u32[]{:S(2)}) copy-start(bf16[32,2048]{1,0:T(8,128)(2,1)S(1)} %later.2.refs_1_) | copy-start | bytes 393220
  89.1 11.8 %collective-permute-start.6 = (bf16[32,2048]{1,0:T(8,128)(2,1)S(1)}, bf16[32,2048]{1,0:T(8,128)(2,1)S(1)}, u32[]{:S(2)}, u32[]{:S(2)}) collective-permute-start(bf16[32,2048]{1,0:T(8,128)(2,1)S(1)} %later.2.refs_1_), channel_id=1, source_target_pairs={{0,24},{4,28},{8,16},{12,20},{16,8},{20,12},{24,0},{28,4},{1,25},{... | collective-permute-start | bytes 393224 | tf_op jit(solution)/shard_map/ppermute | solution.py:541
  89.8 11.1 %collective-permute-start.5 = (bf16[32,2048]{1,0:T(8,128)(2,1)S(1)}, bf16[32,2048]{1,0:T(8,128)(2,1)S(1)}, u32[]{:S(2)}, u32[]{:S(2)}) collective-permute-start(bf16[32,2048]{1,0:T(8,128)(2,1)S(1)} %later.2.refs_1_), channel_id=1, source_target_pairs={{0,16},{4,20},{8,24},{12,28},{16,0},{20,4},{24,8},{28,12},{1,17},{... | collective-permute-start | bytes 393224 | tf_op jit(solution)/shard_map/ppermute | solution.py:541
  91.2 9.7 %collective-permute-start.4 = (bf16[32,2048]{1,0:T(8,128)(2,1)S(1)}, bf16[32,2048]{1,0:T(8,128)(2,1)S(1)}, u32[]{:S(2)}, u32[]{:S(2)}) collective-permute-start(bf16[32,2048]{1,0:T(8,128)(2,1)S(1)} %later.2.refs_1_), channel_id=1, source_target_pairs={{0,8},{4,12},{8,0},{12,4},{16,24},{20,28},{24,16},{28,20},{1,9},{5... | collective-permute-start | bytes 393224 | tf_op jit(solution)/shard_map/ppermute | solution.py:541
  102.5 22.3 %all-to-all-start.3 = ((bf16[8,72,1152]{2,1,0:T(8,128)(2,1)}), bf16[8,72,1152]{2,1,0:T(8,128)(2,1)S(1)}, u32[]{:S(2)}, u32[]{:S(2)}) async-start(bf16[8,72,1152]{2,1,0:T(8,128)(2,1)} %bitcast.22), calls=%async_computation.3 | async-start | bytes 2654208 | tf_op jit(solution)/shard_map/all_to_all | solution.py:572
  106.4 15.2 %collective-permute-start.8 = (bf16[272,1024]{1,0:T(8,128)(2,1)}, bf16[272,1024]{1,0:T(8,128)(2,1)S(1)}, u32[]{:S(2)}, u32[]{:S(2)}) collective-permute-start(bf16[272,1024]{1,0:T(8,128)(2,1)} %copy-done.38), channel_id=1, source_target_pairs={{0,1},{1,0},{2,3},{3,2},{4,5},{5,4},{6,7},{7,6},{8,9},{9,8},{10,11... | collective-permute-start | bytes 1671176 | tf_op jit(solution)/shard_map/ppermute | solution.py:536
  124.8 7.9 %copy-start.60 = (bf16[1,768,32]{1,2,0:T(8,128)(2,1)S(1)}, bf16[1,768,32]{1,2,0:T(8,128)(2,1)}, u32[]{:S(2)}) copy-start(bf16[1,768,32]{1,2,0:T(8,128)(2,1)} %param.27) | copy-start | bytes 147460
  124.8 35.6 %all-to-all-start.5 = ((bf16[8,72,2176]{2,1,0:T(8,128)(2,1)}), bf16[8,72,2176]{2,1,0:T(8,128)(2,1)}, u32[]{:S(2)}, u32[]{:S(2)}) async-start(bf16[8,72,2176]{2,1,0:T(8,128)(2,1)} %bitcast.66), calls=%async_computation.5 | async-start | bytes 5013504 | tf_op jit(solution)/shard_map/all_to_all | solution.py:572
  131.5 74.2 %copy-start.11 = (bf16[128,2048]{1,0:T(8,128)(2,1)}, bf16[128,2048]{1,0:T(8,128)(2,1)S(1)}, u32[]{:S(2)}) copy-start(bf16[128,2048]{1,0:T(8,128)(2,1)S(1)} %later.3.refs_2_.refs_11_.refs_3_) | copy-start | bytes 1572868
  131.5 26.3 %collective-permute-start.9 = (bf16[128,2048]{1,0:T(8,128)(2,1)S(1)}, bf16[128,2048]{1,0:T(8,128)(2,1)}, u32[]{:S(2)}, u32[]{:S(2)}) collective-permute-start(bf16[128,2048]{1,0:T(8,128)(2,1)S(1)} %later.3.refs_2_.refs_11_.refs_3_), channel_id=1, source_target_pairs={{0,2},{1,3},{2,0},{3,1},{4,6},{5,7},{6,4},{7,5},{8,10},{9,11},{10,... | collective-permute-start | bytes 1572872 | tf_op jit(solution)/shard_map/ppermute | solution.py:536
  160.4 34.6 %all-to-all-start.4 = ((bf16[8,72,2176]{2,1,0:T(8,128)(2,1)}), bf16[8,72,2176]{2,1,0:T(8,128)(2,1)S(1)}, u32[]{:S(2)}, u32[]{:S(2)}) async-start(bf16[8,72,2176]{2,1,0:T(8,128)(2,1)} %bitcast.86), calls=%async_computation.4 | async-start | bytes 5013504 | tf_op jit(solution)/shard_map/all_to_all | solution.py:572
  164.2 18.6 %collective-permute-start.10 = (bf16[128,2048]{1,0:T(8,128)(2,1)S(1)}, bf16[128,2048]{1,0:T(8,128)(2,1)S(1)}, u32[]{:S(2)}, u32[]{:S(2)}) collective-permute-start(bf16[128,2048]{1,0:T(8,128)(2,1)S(1)} %later.3.refs_2_.refs_11_.refs_3_), channel_id=1, source_target_pairs={{0,1},{1,0},{2,3},{3,2},{4,5},{5,4},{6,7},{7,6},{8,9},{9,8},{10,11... | collective-permute-start | bytes 1572872 | tf_op jit(solution)/shard_map/ppermute | solution.py:536
  164.6 24.9 %collective-permute-start.11 = (bf16[128,2048]{1,0:T(8,128)(2,1)}, bf16[128,2048]{1,0:T(8,128)(2,1)S(1)}, u32[]{:S(2)}, u32[]{:S(2)}) collective-permute-start(bf16[128,2048]{1,0:T(8,128)(2,1)} %collective-permute-done.9.refs_1_.refs_3_.refs_12_.refs_4_), channel_id=1, source_target_pairs={{0,1},{1,0},{2,3},{3,2},{4,5},{5,4},{6,7},{7,6},{8,9},{9,8},{10,11... | collective-permute-start | bytes 1572872 | tf_op jit(solution)/shard_map/ppermute | solution.py:536
  179.1 13.3 %copy-start.35 = (bf16[576,768]{1,0:T(8,128)(2,1)}, bf16[576,768]{1,0:T(8,128)(2,1)S(1)}, u32[]{:S(2)}) copy-start(bf16[576,768]{1,0:T(8,128)(2,1)S(1)} %get-tuple-element.28.refs_4_.refs_1_) | copy-start | bytes 2654212
  182.7 16.6 %copy-start.28 = (bf16[256,576]{1,0:T(8,128)(2,1)}, bf16[256,576]{1,0:T(8,128)(2,1)S(1)}, u32[]{:S(2)}) copy-start(bf16[256,576]{1,0:T(8,128)(2,1)S(1)} %get-tuple-element.29.refs_1_.refs_2_) | copy-start | bytes 884740
  182.7 7.6 %copy-start.24 = (bf16[128,2048]{1,0:T(8,128)(2,1)}, bf16[128,2048]{1,0:T(8,128)(2,1)S(1)}, u32[]{:S(2)}) copy-start(bf16[128,2048]{1,0:T(8,128)(2,1)S(1)} %collective-permute-done.10.refs_2_.refs_15_.refs_7_) | copy-start | bytes 1572868
  195.0 35.8 %all-to-all-start.6 = ((bf16[8,72,2176]{2,1,0:T(8,128)(2,1)}), bf16[8,72,2176]{2,1,0:T(8,128)(2,1)}, u32[]{:S(2)}, u32[]{:S(2)}) async-start(bf16[8,72,2176]{2,1,0:T(8,128)(2,1)} %bitcast.67), calls=%async_computation.6 | async-start | bytes 5013504 | tf_op jit(solution)/shard_map/all_to_all | solution.py:572
  201.1 4.6 %copy-start.25 = (bf16[128,2048]{1,0:T(8,128)(2,1)S(1)}, bf16[128,2048]{1,0:T(8,128)(2,1)}, u32[]{:S(2)}) copy-start(bf16[128,2048]{1,0:T(8,128)(2,1)} %copy-done.24) | copy-start | bytes 1572868
  202.3 6.3 %copy-start.19 = (bf16[128,2176]{1,0:T(8,128)(2,1)}, bf16[128,2176]{1,0:T(8,128)(2,1)S(1)}, u32[]{:S(2)}) copy-start(bf16[128,2176]{1,0:T(8,128)(2,1)S(1)} %get-tuple-element.31.refs_17_.refs_0_) | copy-start | bytes 1671172
  202.3 28.4 %copy-start.8 = (bf16[576,2048]{1,0:T(8,128)(2,1)S(1)}, bf16[576,2048]{1,0:T(8,128)(2,1)}, u32[]{:S(2)}) copy-start(bf16[576,2048]{1,0:T(8,128)(2,1)} %copy-done.7) | copy-start | bytes 7077892
  202.4 28.4 %copy-start.30 = (bf16[256,576]{1,0:T(8,128)(2,1)S(1)}, bf16[256,576]{1,0:T(8,128)(2,1)}, u32[]{:S(2)}) copy-start(bf16[256,576]{1,0:T(8,128)(2,1)} %copy-done.29) | copy-start | bytes 884740
  202.4 27.6 %collective-permute-start.12 = (bf16[128,2176]{1,0:T(8,128)(2,1)S(1)}, bf16[128,2176]{1,0:T(8,128)(2,1)S(1)}, u32[]{:S(2)}, u32[]{:S(2)}) collective-permute-start(bf16[128,2176]{1,0:T(8,128)(2,1)S(1)} %get-tuple-element.36), channel_id=1, source_target_pairs={{0,2},{1,3},{2,0},{3,1},{4,6},{5,7},{6,4},{7,5},{8,10},{9,11},{10,... | collective-permute-start | bytes 1671176 | tf_op jit(solution)/shard_map/ppermute | solution.py:536
  203.6 1.3 collective-permute-start.15
  203.7 1.5 collective-permute-start.18
  204.1 1.3 collective-permute-start.17
  204.2 1.5 collective-permute-start.16
  240.5 32.0 %copy-start.20 = (bf16[128,2176]{1,0:T(8,128)(2,1)S(1)}, bf16[128,2176]{1,0:T(8,128)(2,1)}, u32[]{:S(2)}) copy-start(bf16[128,2176]{1,0:T(8,128)(2,1)} %copy-done.19) | copy-start | bytes 1671172
  240.5 32.0 %copy-start.23 = (bf16[128,2176]{1,0:T(8,128)(2,1)S(1)}, bf16[128,2176]{1,0:T(8,128)(2,1)}, u32[]{:S(2)}) copy-start(bf16[128,2176]{1,0:T(8,128)(2,1)} %copy-done.21) | copy-start | bytes 1671172
  240.5 21.2 %all-to-all-start.7 = ((bf16[8,32,2304]{2,1,0:T(8,128)(2,1)}), bf16[8,32,2304]{2,1,0:T(8,128)(2,1)}, u32[]{:S(2)}, u32[]{:S(2)}) async-start(bf16[8,32,2304]{2,1,0:T(8,128)(2,1)} %gradient.1), calls=%async_computation.7 | async-start | bytes 2359296 | tf_op jit(solution)/shard_map/all_to_all | solution.py:572
  244.9 27.5 %collective-permute-start.13 = (bf16[128,2176]{1,0:T(8,128)(2,1)S(1)}, bf16[128,2176]{1,0:T(8,128)(2,1)S(1)}, u32[]{:S(2)}, u32[]{:S(2)}) collective-permute-start(bf16[128,2176]{1,0:T(8,128)(2,1)S(1)} %copy-done.37), channel_id=1, source_target_pairs={{0,1},{1,0},{2,3},{3,2},{4,5},{5,4},{6,7},{7,6},{8,9},{9,8},{10,11... | collective-permute-start | bytes 1671176 | tf_op jit(solution)/shard_map/ppermute | solution.py:536
  245.0 27.4 %collective-permute-start.14 = (bf16[128,2176]{1,0:T(8,128)(2,1)S(1)}, bf16[128,2176]{1,0:T(8,128)(2,1)S(1)}, u32[]{:S(2)}, u32[]{:S(2)}) collective-permute-start(bf16[128,2176]{1,0:T(8,128)(2,1)S(1)} %copy-done.54), channel_id=1, source_target_pairs={{0,3},{1,2},{2,1},{3,0},{4,7},{5,6},{6,5},{7,4},{8,11},{9,10},{10,... | collective-permute-start | bytes 1671176 | tf_op jit(solution)/shard_map/ppermute | solution.py:536
  (43 other events, 79.8 us)
